TPU v7x, 32 devices: a whole 2x2x4 slice. The times are simulated.
32 devices in a mesh: wide: 16 (over z, x, core), narrow: 2 (over y).
Axes of the slice: x: 2, y: 2, z: 4, core: 2. Of those that a mesh axis runs over, the one named last changes fastest.
Arguments:
- ice_x: float32 [256, 10, 256], P('wide', None, 'narrow'), may hold values from -6 to 6
- ice_y: float32 [256, 10, 256], P('wide', None, 'narrow'), may hold values from -6 to 6
- ice_temp: float32 [256, 10, 256], P('wide', None, 'narrow'), may hold values from -2 to 2
- ocean_x: float32 [256, 80, 256], P('wide', None, 'narrow'), may hold values from -6 to 6
- ocean_y: float32 [256, 80, 256], P('wide', None, 'narrow'), may hold values from -6 to 6
- ocean_temp: float32 [256, 80, 256], P('wide', None, 'narrow'), may hold values from -2 to 2
- thick: float32 [256, 256], P('wide', 'narrow'), may hold values from 1 to 10
- grounded_mask: int32 [256, 256], P('wide', 'narrow'), may hold values 0 or 1
- wet_mask: int32 [256, 256], P('wide', 'narrow'), may hold values 0 or 1
- ice_links: int32 [256, 2], P('wide', 'narrow'), may hold values from -1 to 255, as said below
- ocean_links: int32 [256, 2], P('wide', 'narrow'), may hold values from -1 to 255, as said below
Outputs:
- ice_state: float32 [3, 256, 10, 256], P(None, 'wide', None, 'narrow')
- ocean_state: float32 [3, 256, 80, 256], P(None, 'wide', None, 'narrow')
- thick_out: float32 [256, 256], P('wide', 'narrow')
- melt_out: float32 [256, 256], P('wide', 'narrow')
Inputs may be any that keep to these rules, and one draw needn't show every extreme that they name: `ice_links`: within one column group an ice block names an ocean block exactly when that ocean block names it back. Per column group, for any ocean tile and ice tile, at most 2 blocks of the ocean tile names a block of the ice tile, and that bound is reached in every draw, as is an ocean tile with all 16 blocks linked. `ocean_links`: the mirror of ice_links, as described there.
All inputs are finite; a program needn't handle non-finite values. No bound on the sum of `grounded_mask` or of `wet_mask` on one device may be relied on, other than what follows from the above.
Results may differ from a plain program's by a relative error of at most 0.000071.
Values sent between devices are 32-bit elements; how exact they have to be, the bound alone decides.
No kernel may reach another device: no remote copies, remote signals or barrier semaphores. Data moves between devices by JAX's collectives and lax.ppermute only.
A program may use at most 64 MiB of HBM per device.

v0:
```python
import jax
import jax.numpy as jnp
from jax import lax
from jax.sharding import PartitionSpec as P

PICARD = 2


DIFFUSE = 0.2
GAMMA_MELT = 0.5
TIME_STEP = 0.05
SLOPE_SCALE = 0.1
STRAIN_FLOOR = 0.01
HEATING_RATE = 0.01


def padded_2(shard, sides, width):
    for axis, dim in sides:
        count, length = (lax.axis_size(axis), shard.shape[dim])
        up = [(i, (i + 1) % count) for i in range(count - 1)]
        down = [(j, i) for i, j in up]
        last = lax.slice_in_dim(shard, length - width, length, axis=dim)
        first = lax.slice_in_dim(shard, 0, width, axis=dim)
        before = lax.ppermute(last, axis, up)
        after = lax.ppermute(first, axis, down)
        shard = jnp.concatenate([before, shard, after], axis=dim)
    return shard


def apply_diffuse(field_pad, wet_pad):
    count_rows = field_pad.shape[0] - 2
    count_cols = field_pad.shape[2] - 2
    centre = field_pad[1:-1, :, 1:-1]
    wet_centre = wet_pad[1:-1, 1:-1]
    total = jnp.zeros_like(centre)
    for row_off, col_off in ((0, 1), (2, 1), (1, 0), (1, 2)):
        weight = (
            wet_centre * wet_pad[row_off : row_off + count_rows, col_off : col_off + count_cols]
        )
        total = total + weight[:, None, :] * (
            field_pad[row_off : row_off + count_rows, :, col_off : col_off + count_cols] - centre
        )
    return centre + DIFFUSE * total


def strains(padded):
    along_rows = 0.5 * (padded[2:, :, 1:-1] - padded[:-2, :, 1:-1])
    along_cols = 0.5 * (padded[1:-1, :, 2:] - padded[1:-1, :, :-2])
    middle = padded[1:-1, :, 1:-1]
    vertical = jnp.concatenate(
        [middle[:, 1:, :] - middle[:, :-1, :], jnp.zeros_like(middle[:, :1, :])], axis=1
    )
    return (along_rows, along_cols, vertical, middle)


def layer_shift(field):
    zeros = jnp.zeros_like(field[:, :1, :])
    above = jnp.concatenate([field[:, 1:, :], zeros], axis=1)
    below = jnp.concatenate([zeros, field[:, :-1, :]], axis=1)
    return above + below


def picard(pad_x, pad_y, rate_factor, inside, stress_x, stress_y, friction):
    count_rows = pad_x.shape[0] - 4
    count_cols = pad_x.shape[2] - 4
    layers = pad_x.shape[1]
    ux, uy, uz, mid_x = strains(pad_x)
    vx, vy, vz, mid_y = strains(pad_y)
    eps2 = ux * ux + vy * vy + ux * vy + 0.25 * (uy + vx) ** 2 + 0.25 * (uz * uz + vz * vz)
    eta = rate_factor * (eps2 + STRAIN_FLOOR) ** (-1.0 / 3.0) * inside[:, None, :]
    centre = eta[1:-1, :, 1:-1]
    level = jnp.arange(layers)
    vertical_count = ((level > 0).astype(jnp.float32) + (level < layers - 1).astype(jnp.float32))[
        None, :, None
    ]
    diagonal = centre * vertical_count + friction[:, None, :]
    sum_x = stress_x[:, None, :] + centre * layer_shift(mid_x[1:-1, :, 1:-1])
    sum_y = stress_y[:, None, :] + centre * layer_shift(mid_y[1:-1, :, 1:-1])
    for row_off, col_off in ((0, 1), (2, 1), (1, 0), (1, 2)):
        face = 0.5 * (
            centre + eta[row_off : row_off + count_rows, :, col_off : col_off + count_cols]
        )
        diagonal = diagonal + face
        sum_x = (
            sum_x + face * mid_x[row_off : row_off + count_rows, :, col_off : col_off + count_cols]
        )
        sum_y = (
            sum_y + face * mid_y[row_off : row_off + count_rows, :, col_off : col_off + count_cols]
        )
    return (sum_x / diagonal, sum_y / diagonal, centre * eps2[1:-1, :, 1:-1])


def slot_table(partner, ranking, linked, wide_count, capacity):
    earlier = (
        (partner[:, None] == partner[None, :])
        & linked[None, :]
        & (ranking[None, :] < ranking[:, None])
    )
    slot_rank = jnp.sum(earlier.astype(jnp.int32), axis=1)
    target = partner * capacity + slot_rank
    hits = (
        jnp.arange(wide_count * capacity, dtype=jnp.int32)[:, None] == target[None, :]
    ) & linked[None, :]
    return hits.astype(jnp.float32)


def local(
    ice_x,
    ice_y,
    ice_temp,
    ocean_x,
    ocean_y,
    ocean_temp,
    thick,
    grounded_mask,
    wet_mask,
    ice_links,
    ocean_links,
):
    wide_count = lax.axis_size("wide")
    row_place = lax.axis_index("wide")
    column = lax.axis_index("narrow")
    across = lax.axis_size("narrow")
    tile_rows, layers, tile_cols = ice_x.shape
    blocks = ice_links.shape[0]
    block_rows = tile_rows // blocks
    capacity = max(1, 2 * blocks // wide_count)
    grounded = grounded_mask.astype(jnp.float32)
    wet = wet_mask.astype(jnp.float32)
    ice_pad = (
        padded_2(ice_x, (("wide", 0), ("narrow", 2)), 2),
        padded_2(ice_y, (("wide", 0), ("narrow", 2)), 2),
        padded_2(ice_temp, (("wide", 0), ("narrow", 2)), 2),
    )
    ocean_pad = (
        padded_2(ocean_x, (("wide", 0), ("narrow", 2)), 1),
        padded_2(ocean_y, (("wide", 0), ("narrow", 2)), 1),
        padded_2(ocean_temp, (("wide", 0), ("narrow", 2)), 1),
    )
    wet_pad = padded_2(wet, (("wide", 0), ("narrow", 1)), 1)
    ocean_heat = apply_diffuse(ocean_pad[2], wet_pad)
    current_x = apply_diffuse(ocean_pad[0], wet_pad)
    current_y = apply_diffuse(ocean_pad[1], wet_pad)
    ice_list = ice_links[:, 0]
    ocean_list = ocean_links[:, 0]
    ice_linked = ice_list >= 0
    ocean_linked = ocean_list >= 0
    ice_safe = jnp.maximum(ice_list, 0)
    ocean_safe = jnp.maximum(ocean_list, 0)
    ocean_weight = ocean_linked.astype(jnp.float32)
    send_table = slot_table(
        ice_safe // blocks, jnp.arange(blocks, dtype=jnp.int32), ice_linked, wide_count, capacity
    )
    recv_table = slot_table(
        ocean_safe // blocks, ocean_safe % blocks, ocean_linked, wide_count, capacity
    )
    draft_field = 0.9 * thick * (1.0 - grounded)
    outgoing = jnp.dot(send_table, draft_field, precision=lax.Precision.HIGHEST)
    incoming = lax.all_to_all(outgoing, "wide", split_axis=0, concat_axis=0, tiled=True)
    arrived = jnp.dot(recv_table.T, incoming, precision=lax.Precision.HIGHEST)
    coupled = jnp.repeat(ocean_weight, block_rows)[:, None]
    freezing = 0.0832 - 0.761 * arrived
    melt_rate = GAMMA_MELT * (ocean_heat[:, 0, :] - freezing) * wet * coupled
    ocean_heat = ocean_heat.at[:, 0, :].add(-0.2 * melt_rate)
    outgoing_melt = jnp.dot(recv_table, melt_rate, precision=lax.Precision.HIGHEST)
    incoming_melt = lax.all_to_all(outgoing_melt, "wide", split_axis=0, concat_axis=0, tiled=True)
    melt_back = jnp.dot(send_table.T, incoming_melt, precision=lax.Precision.HIGHEST)
    new_thick = thick - TIME_STEP * melt_back * (1.0 - grounded)
    surface = new_thick * (0.1 + 0.9 * grounded)
    surface_pad = padded_2(surface, (("wide", 0), ("narrow", 1)), 1)
    stress_x = -SLOPE_SCALE * new_thick * 0.5 * (surface_pad[2:, 1:-1] - surface_pad[:-2, 1:-1])
    stress_y = -SLOPE_SCALE * new_thick * 0.5 * (surface_pad[1:-1, 2:] - surface_pad[1:-1, :-2])
    friction = 0.1 + 9.9 * grounded
    row_ext = jnp.arange(tile_rows + 2)
    col_ext = jnp.arange(tile_cols + 2)
    row_good = jnp.logical_not(
        (row_ext == 0) & (row_place == 0)
        | (row_ext == tile_rows + 1) & (row_place == wide_count - 1)
    )
    col_good = jnp.logical_not(
        (col_ext == 0) & (column == 0) | (col_ext == tile_cols + 1) & (column == across - 1)
    )
    inside = (row_good[:, None] & col_good[None, :]).astype(jnp.float32)
    rate_factor = jnp.exp(0.25 * ice_pad[2][1:-1, :, 1:-1])
    pad_x, pad_y = (ice_pad[0], ice_pad[1])
    velocity_x = ice_x
    velocity_y = ice_y
    heating = jnp.zeros_like(ice_x)
    for sweep_index in range(PICARD):
        if sweep_index > 0:
            pad_x, pad_y = (
                padded_2(velocity_x, (("wide", 0), ("narrow", 2)), 2),
                padded_2(velocity_y, (("wide", 0), ("narrow", 2)), 2),
            )
        velocity_x, velocity_y, heating = picard(
            pad_x, pad_y, rate_factor, inside, stress_x, stress_y, friction
        )
    ice_state = jnp.stack([velocity_x, velocity_y, ice_temp + HEATING_RATE * heating])
    ocean_state = jnp.stack([current_x, current_y, ocean_heat])
    return (ice_state, ocean_state, new_thick, melt_rate)


def solution(mesh):
    placed = (
        P("wide", None, "narrow"),
        P("wide", None, "narrow"),
        P("wide", None, "narrow"),
        P("wide", None, "narrow"),
        P("wide", None, "narrow"),
        P("wide", None, "narrow"),
        P("wide", "narrow"),
        P("wide", "narrow"),
        P("wide", "narrow"),
        P("wide", "narrow"),
        P("wide", "narrow"),
    )
    return jax.shard_map(
        local,
        mesh=mesh,
        in_specs=placed,
        out_specs=(
            P(None, "wide", None, "narrow"),
            P(None, "wide", None, "narrow"),
            P("wide", "narrow"),
            P("wide", "narrow"),
        ),
        check_vma=False,
    )
```

profile of v0, /device:TPU:0, one launch (start us, length us, event | category | flops | bytes accessed | tf_op | source)
XLA Modules:
  0.0 200.2 jit_solution(138464135581188185)
XLA Ops:
  2.8 3.0 %collective-permute-start.10 = (f32[2,10,128]{2,0,1:T(2,128)S(1)}, f32[2,10,128]{2,0,1:T(2,128)S(1)}, u32[]{:S(2)}, u32[]{:S(2)}) collective-permute-start(f32[2,10,128]{2,0,1:T(2,128)S(1)} %get-tuple-element.76), channel_id=1, source_target_pairs={{0,2},{2,4},{4,6},{6,8},{8,10},{10,12},{12,14},{14,16},{16,18},{18... | collective-permute-start | bytes 30728 | tf_op jit(solution)/shard_map/ppermute | solution.py:24
  10.1 5.7 %collective-permute-start = (f32[1,128]{1,0:T(1,128)S(1)}, f32[1,128]{1,0:T(1,128)S(1)}, u32[]{:S(2)}, u32[]{:S(2)}) collective-permute-start(f32[1,128]{1,0:T(1,128)S(1)} %get-tuple-element.92), channel_id=1, source_target_pairs={{0,2},{2,4},{4,6},{6,8},{8,10},{10,12},{12,14},{14,16},{16,18},{18... | collective-permute-start | bytes 1544 | tf_op jit(solution)/shard_map/ppermute | solution.py:24
  20.1 8.1 %all-to-all-start = ((f32[16,2,128]{2,1,0:T(2,128)}), f32[16,2,128]{2,1,0:T(2,128)}, u32[]{:S(2)}, u32[]{:S(2)}) async-start(f32[16,2,128]{2,1,0:T(2,128)} %bitcast.13), calls=%async_computation | async-start | bytes 32768 | tf_op jit(solution)/shard_map/all_to_all | solution.py:159
  41.8 3.4 %collective-permute-start.4 = (f32[18,1]{1,0:T(8,128)S(1)}, f32[18,1]{1,0:T(8,128)S(1)}, u32[]{:S(2)}, u32[]{:S(2)}) collective-permute-start(f32[18,1]{1,0:T(8,128)S(1)} %get-tuple-element.82), channel_id=1, source_target_pairs={{0,1},{2,3},{4,5},{6,7},{8,9},{10,11},{12,13},{14,15},{16,17},{18,... | collective-permute-start | bytes 224 | tf_op jit(solution)/shard_map/ppermute | solution.py:24
  48.5 2.3 %collective-permute-done.6 = f32[18,1]{1,0:T(8,128)S(1)} collective-permute-done((f32[18,1]{1,0:T(8,128)S(1)}, f32[18,1]{1,0:T(8,128)S(1)}, u32[]{:S(2)}, u32[]{:S(2)}) %collective-permute-start.6) | collective-permute-done | bytes 104 | tf_op jit(solution)/shard_map/ppermute | solution.py:25
  52.8 3.0 %collective-permute-start.14 = (f32[2,10,128]{2,0,1:T(2,128)S(1)}, f32[2,10,128]{2,0,1:T(2,128)S(1)}, u32[]{:S(2)}, u32[]{:S(2)}) collective-permute-start(f32[2,10,128]{2,0,1:T(2,128)S(1)} %get-tuple-element.70), channel_id=1, source_target_pairs={{0,2},{2,4},{4,6},{6,8},{8,10},{10,12},{12,14},{14,16},{16,18},{18... | collective-permute-start | bytes 30728 | tf_op jit(solution)/shard_map/ppermute | solution.py:24
  57.3 4.0 %collective-permute-start.1 = (f32[1,80,128]{2,0,1:T(1,128)S(1)}, f32[1,80,128]{2,0,1:T(1,128)S(1)}, u32[]{:S(2)}, u32[]{:S(2)}) collective-permute-start(f32[1,80,128]{2,0,1:T(1,128)S(1)} %bitcast.62), channel_id=1, source_target_pairs={{0,2},{2,4},{4,6},{6,8},{8,10},{10,12},{12,14},{14,16},{16,18},{18... | collective-permute-start | bytes 122888 | tf_op jit(solution)/shard_map/ppermute | solution.py:24
  64.1 4.6 %collective-permute-start.21 = (f32[20,10,2]{2,0,1:T(8,128)S(1)}, f32[20,10,2]{2,0,1:T(8,128)S(1)}, u32[]{:S(2)}, u32[]{:S(2)}) collective-permute-start(f32[20,10,2]{2,0,1:T(8,128)S(1)} %get-tuple-element.48), channel_id=1, source_target_pairs={{0,1},{2,3},{4,5},{6,7},{8,9},{10,11},{12,13},{14,15},{16,17},{18,... | collective-permute-start | bytes 4808 | tf_op jit(solution)/shard_map/ppermute | solution.py:24
  71.3 4.4 %collective-permute-start.16 = (f32[20,10,2]{2,0,1:T(8,128)S(1)}, f32[20,10,2]{2,0,1:T(8,128)S(1)}, u32[]{:S(2)}, u32[]{:S(2)}) collective-permute-start(f32[20,10,2]{2,0,1:T(8,128)S(1)} %get-tuple-element.47), channel_id=1, source_target_pairs={{0,1},{2,3},{4,5},{6,7},{8,9},{10,11},{12,13},{14,15},{16,17},{18,... | collective-permute-start | bytes 4808 | tf_op jit(solution)/shard_map/ppermute | solution.py:24
  79.3 4.4 %collective-permute-start.12 = (f32[20,10,2]{2,0,1:T(8,128)S(1)}, f32[20,10,2]{2,0,1:T(8,128)S(1)}, u32[]{:S(2)}, u32[]{:S(2)}) collective-permute-start(f32[20,10,2]{2,0,1:T(8,128)S(1)} %get-tuple-element.50), channel_id=1, source_target_pairs={{0,1},{2,3},{4,5},{6,7},{8,9},{10,11},{12,13},{14,15},{16,17},{18,... | collective-permute-start | bytes 4808 | tf_op jit(solution)/shard_map/ppermute | solution.py:24
  88.7 7.5 %collective-permute-start.32 = (f32[1,80,128]{2,0,1:T(1,128)}, f32[1,80,128]{2,0,1:T(1,128)}, u32[]{:S(2)}, u32[]{:S(2)}) collective-permute-start(f32[1,80,128]{2,0,1:T(1,128)} %bitcast.20), channel_id=1, source_target_pairs={{0,2},{2,4},{4,6},{6,8},{8,10},{10,12},{12,14},{14,16},{16,18},{18... | collective-permute-start | bytes 122888 | tf_op jit(solution)/shard_map/ppermute | solution.py:24
  97.5 2.1 %copy.99 = f32[18,80,1]{1,2,0:T(1,128)} copy(f32[18,80,1]{2,0,1:T(8,128)} %get-tuple-element.35) | data formatting | bytes 11520 | tf_op jit(solution)/shard_map/slice | solution.py:23
  101.8 5.7 %collective-permute-start.5 = (f32[18,80,1]{1,2,0:T(1,128)}, f32[18,80,1]{1,2,0:T(1,128)}, u32[]{:S(2)}, u32[]{:S(2)}) collective-permute-start(f32[18,80,1]{1,2,0:T(1,128)} %copy.96), channel_id=1, source_target_pairs={{0,1},{2,3},{4,5},{6,7},{8,9},{10,11},{12,13},{14,15},{16,17},{18,... | collective-permute-start | bytes 17288 | tf_op jit(solution)/shard_map/ppermute | solution.py:24
  111.6 5.7 %collective-permute-start.38 = (f32[18,80,1]{1,2,0:T(1,128)}, f32[18,80,1]{1,2,0:T(1,128)}, u32[]{:S(2)}, u32[]{:S(2)}) collective-permute-start(f32[18,80,1]{1,2,0:T(1,128)} %copy.124), channel_id=1, source_target_pairs={{0,1},{2,3},{4,5},{6,7},{8,9},{10,11},{12,13},{14,15},{16,17},{18,... | collective-permute-start | bytes 17288 | tf_op jit(solution)/shard_map/ppermute | solution.py:24
  121.7 5.7 %collective-permute-start.34 = (f32[18,80,1]{1,2,0:T(1,128)}, f32[18,80,1]{1,2,0:T(1,128)}, u32[]{:S(2)}, u32[]{:S(2)}) collective-permute-start(f32[18,80,1]{1,2,0:T(1,128)} %copy.110), channel_id=1, source_target_pairs={{0,1},{2,3},{4,5},{6,7},{8,9},{10,11},{12,13},{14,15},{16,17},{18,... | collective-permute-start | bytes 17288 | tf_op jit(solution)/shard_map/ppermute | solution.py:24
  129.7 2.6 %fusion.176 = f32[1,16,80,128]{3,1,2,0:T(8,128)} fusion(f32[16,80,128]{2,0,1:T(8,128)S(1)} %copy.102, f32[18,80,1]{2,0,1:T(8,128)S(1)} %copy.100, f32[1,80,128]{2,0,1:T(1,128)} %copy-done.24, f32[1,80,128]{2,0,1:T(1,128)} %copy-done.26, f32[16,128]{1,0:T(8,128)} %get-tuple-element.85, f32[18,80,1]{2,0,1:T(8,128)S(1)} %copy.97, ...), kind=kLoop, calls=%fused_computation.309 | loop fusion | flops 3440640 | bytes 1436928 | tf_op jit(solution)/shard_map/stack | solution.py:199
  137.0 5.7 %all-to-all-start.1 = ((f32[16,2,128]{2,1,0:T(2,128)}), f32[16,2,128]{2,1,0:T(2,128)}, u32[]{:S(2)}, u32[]{:S(2)}) async-start(f32[16,2,128]{2,1,0:T(2,128)} %bitcast.15), calls=%async_computation.1 | async-start | bytes 32768 | tf_op jit(solution)/shard_map/all_to_all | solution.py:166
  149.1 3.1 %fusion.12 = f32[1,16,80,128]{3,1,2,0:T(8,128)} fusion(f32[16,80,128]{2,0,1:T(8,128)S(1)} %copy-done.1, f32[18,80,1]{2,0,1:T(8,128)S(1)} %copy.128, f32[1,80,128]{2,0,1:T(1,128)} %copy-done.46, f32[1,80,128]{2,0,1:T(1,128)} %copy-done.47, f32[18,80,1]{2,0,1:T(8,128)} %copy.125, f32[16,128]{1,0:T(8,128)} %get-tuple-element.85, ...), kind=kLoop, calls=%fused_computation.19 | loop fusion | flops 3440640 | bytes 1436928 | tf_op jit(solution)/shard_map/stack | solution.py:199
  155.1 2.2 %collective-permute-start.9 = (f32[1,128]{1,0:T(1,128)S(1)}, f32[1,128]{1,0:T(1,128)S(1)}, u32[]{:S(2)}, u32[]{:S(2)}) collective-permute-start(f32[1,128]{1,0:T(1,128)S(1)} %get-tuple-element.90), channel_id=1, source_target_pairs={{0,2},{2,4},{4,6},{6,8},{8,10},{10,12},{12,14},{14,16},{16,18},{18... | collective-permute-start | bytes 1544 | tf_op jit(solution)/shard_map/ppermute | solution.py:24
  164.6 4.2 %collective-permute-done.26 = f32[18,1]{1,0:T(8,128)S(1)} collective-permute-done((f32[18,1]{1,0:T(8,128)S(1)}, f32[18,1]{1,0:T(8,128)S(1)}, u32[]{:S(2)}, u32[]{:S(2)}) %collective-permute-start.26) | collective-permute-done | bytes 104 | tf_op jit(solution)/shard_map/ppermute | solution.py:25
  170.6 3.6 %collective-permute-start.28 = (f32[2,10,128]{2,0,1:T(2,128)S(1)}, f32[2,10,128]{2,0,1:T(2,128)S(1)}, u32[]{:S(2)}, u32[]{:S(2)}) collective-permute-start(f32[2,10,128]{2,0,1:T(2,128)S(1)} %get-tuple-element.68), channel_id=1, source_target_pairs={{0,2},{2,4},{4,6},{6,8},{8,10},{10,12},{12,14},{14,16},{16,18},{18... | collective-permute-start | bytes 30728 | tf_op jit(solution)/shard_map/ppermute | solution.py:24
  176.0 5.4 %collective-permute-start.22 = (f32[2,10,128]{2,0,1:T(2,128)S(1)}, f32[2,10,128]{2,0,1:T(2,128)S(1)}, u32[]{:S(2)}, u32[]{:S(2)}) collective-permute-start(f32[2,10,128]{2,0,1:T(2,128)S(1)} %get-tuple-element.64), channel_id=1, source_target_pairs={{0,2},{2,4},{4,6},{6,8},{8,10},{10,12},{12,14},{14,16},{16,18},{18... | collective-permute-start | bytes 30728 | tf_op jit(solution)/shard_map/ppermute | solution.py:24
  182.8 4.6 %collective-permute-start.31 = (f32[20,10,2]{2,0,1:T(8,128)S(1)}, f32[20,10,2]{2,0,1:T(8,128)S(1)}, u32[]{:S(2)}, u32[]{:S(2)}) collective-permute-start(f32[20,10,2]{2,0,1:T(8,128)S(1)} %get-tuple-element.44), channel_id=1, source_target_pairs={{0,1},{2,3},{4,5},{6,7},{8,9},{10,11},{12,13},{14,15},{16,17},{18,... | collective-permute-start | bytes 4808 | tf_op jit(solution)/shard_map/ppermute | solution.py:24
  188.9 4.7 %collective-permute-start.24 = (f32[20,10,2]{2,0,1:T(8,128)S(1)}, f32[20,10,2]{2,0,1:T(8,128)S(1)}, u32[]{:S(2)}, u32[]{:S(2)}) collective-permute-start(f32[20,10,2]{2,0,1:T(8,128)S(1)} %get-tuple-element.42), channel_id=1, source_target_pairs={{0,1},{2,3},{4,5},{6,7},{8,9},{10,11},{12,13},{14,15},{16,17},{18,... | collective-permute-start | bytes 4808 | tf_op jit(solution)/shard_map/ppermute | solution.py:24
  (280 shorter events, 92.4 us)
Async XLA Ops:
  1.5 51.3 %collective-permute-start.11 = (f32[2,10,128]{2,0,1:T(2,128)S(1)}, f32[2,10,128]{2,0,1:T(2,128)S(1)}, u32[]{:S(2)}, u32[]{:S(2)}) collective-permute-start(f32[2,10,128]{2,0,1:T(2,128)S(1)} %get-tuple-element.77), channel_id=1, source_target_pairs={{2,0},{4,2},{6,4},{8,6},{10,8},{12,10},{14,12},{16,14},{18,16},{20... | collective-permute-start | bytes 30728 | tf_op jit(solution)/shard_map/ppermute | solution.py:25
  2.8 53.0 %collective-permute-start.10 = (f32[2,10,128]{2,0,1:T(2,128)S(1)}, f32[2,10,128]{2,0,1:T(2,128)S(1)}, u32[]{:S(2)}, u32[]{:S(2)}) collective-permute-start(f32[2,10,128]{2,0,1:T(2,128)S(1)} %get-tuple-element.76), channel_id=1, source_target_pairs={{0,2},{2,4},{4,6},{6,8},{8,10},{10,12},{12,14},{14,16},{16,18},{18... | collective-permute-start | bytes 30728 | tf_op jit(solution)/shard_map/ppermute | solution.py:24
  6.7 50.6 %collective-permute-start.19 = (f32[2,10,128]{2,0,1:T(2,128)S(1)}, f32[2,10,128]{2,0,1:T(2,128)S(1)}, u32[]{:S(2)}, u32[]{:S(2)}) collective-permute-start(f32[2,10,128]{2,0,1:T(2,128)S(1)} %get-tuple-element.75), channel_id=1, source_target_pairs={{2,0},{4,2},{6,4},{8,6},{10,8},{12,10},{14,12},{16,14},{18,16},{20... | collective-permute-start | bytes 30728 | tf_op jit(solution)/shard_map/ppermute | solution.py:25
  8.8 32.9 %collective-permute-start.2 = (f32[1,128]{1,0:T(1,128)S(1)}, f32[1,128]{1,0:T(1,128)S(1)}, u32[]{:S(2)}, u32[]{:S(2)}) collective-permute-start(f32[1,128]{1,0:T(1,128)S(1)} %get-tuple-element.93), channel_id=1, source_target_pairs={{2,0},{4,2},{6,4},{8,6},{10,8},{12,10},{14,12},{16,14},{18,16},{20... | collective-permute-start | bytes 1544 | tf_op jit(solution)/shard_map/ppermute | solution.py:25
  10.1 31.6 %collective-permute-start = (f32[1,128]{1,0:T(1,128)S(1)}, f32[1,128]{1,0:T(1,128)S(1)}, u32[]{:S(2)}, u32[]{:S(2)}) collective-permute-start(f32[1,128]{1,0:T(1,128)S(1)} %get-tuple-element.92), channel_id=1, source_target_pairs={{0,2},{2,4},{4,6},{6,8},{8,10},{10,12},{12,14},{14,16},{16,18},{18... | collective-permute-start | bytes 1544 | tf_op jit(solution)/shard_map/ppermute | solution.py:24
  20.1 113.9 %all-to-all-start = ((f32[16,2,128]{2,1,0:T(2,128)}), f32[16,2,128]{2,1,0:T(2,128)}, u32[]{:S(2)}, u32[]{:S(2)}) async-start(f32[16,2,128]{2,1,0:T(2,128)} %bitcast.13), calls=%async_computation | async-start | bytes 32768 | tf_op jit(solution)/shard_map/all_to_all | solution.py:159
  46.6 14.7 %collective-permute-start.18 = (f32[2,10,128]{2,0,1:T(2,128)S(1)}, f32[2,10,128]{2,0,1:T(2,128)S(1)}, u32[]{:S(2)}, u32[]{:S(2)}) collective-permute-start(f32[2,10,128]{2,0,1:T(2,128)S(1)} %get-tuple-element.74), channel_id=1, source_target_pairs={{0,2},{2,4},{4,6},{6,8},{8,10},{10,12},{12,14},{14,16},{16,18},{18... | collective-permute-start | bytes 30728 | tf_op jit(solution)/shard_map/ppermute | solution.py:24
  50.8 12.0 %collective-permute-start.15 = (f32[2,10,128]{2,0,1:T(2,128)S(1)}, f32[2,10,128]{2,0,1:T(2,128)S(1)}, u32[]{:S(2)}, u32[]{:S(2)}) collective-permute-start(f32[2,10,128]{2,0,1:T(2,128)S(1)} %get-tuple-element.71), channel_id=1, source_target_pairs={{2,0},{4,2},{6,4},{8,6},{10,8},{12,10},{14,12},{16,14},{18,16},{20... | collective-permute-start | bytes 30728 | tf_op jit(solution)/shard_map/ppermute | solution.py:25
  55.9 32.8 %collective-permute-start.3 = (f32[1,80,128]{2,0,1:T(1,128)S(1)}, f32[1,80,128]{2,0,1:T(1,128)S(1)}, u32[]{:S(2)}, u32[]{:S(2)}) collective-permute-start(f32[1,80,128]{2,0,1:T(1,128)S(1)} %bitcast.63), channel_id=1, source_target_pairs={{2,0},{4,2},{6,4},{8,6},{10,8},{12,10},{14,12},{16,14},{18,16},{20... | collective-permute-start | bytes 122888 | tf_op jit(solution)/shard_map/ppermute | solution.py:25
  57.3 38.8 %collective-permute-start.1 = (f32[1,80,128]{2,0,1:T(1,128)S(1)}, f32[1,80,128]{2,0,1:T(1,128)S(1)}, u32[]{:S(2)}, u32[]{:S(2)}) collective-permute-start(f32[1,80,128]{2,0,1:T(1,128)S(1)} %bitcast.62), channel_id=1, source_target_pairs={{0,2},{2,4},{4,6},{6,8},{8,10},{10,12},{12,14},{14,16},{16,18},{18... | collective-permute-start | bytes 122888 | tf_op jit(solution)/shard_map/ppermute | solution.py:24
  61.4 40.4 %collective-permute-start.37 = (f32[1,80,128]{2,0,1:T(1,128)}, f32[1,80,128]{2,0,1:T(1,128)S(1)}, u32[]{:S(2)}, u32[]{:S(2)}) collective-permute-start(f32[1,80,128]{2,0,1:T(1,128)} %bitcast.24), channel_id=1, source_target_pairs={{2,0},{4,2},{6,4},{8,6},{10,8},{12,10},{14,12},{16,14},{18,16},{20... | collective-permute-start | bytes 122888 | tf_op jit(solution)/shard_map/ppermute | solution.py:25
  84.7 22.8 %collective-permute-start.36 = (f32[1,80,128]{2,0,1:T(1,128)}, f32[1,80,128]{2,0,1:T(1,128)S(1)}, u32[]{:S(2)}, u32[]{:S(2)}) collective-permute-start(f32[1,80,128]{2,0,1:T(1,128)} %bitcast.23), channel_id=1, source_target_pairs={{0,2},{2,4},{4,6},{6,8},{8,10},{10,12},{12,14},{14,16},{16,18},{18... | collective-permute-start | bytes 122888 | tf_op jit(solution)/shard_map/ppermute | solution.py:24
  86.5 25.1 %collective-permute-start.33 = (f32[1,80,128]{2,0,1:T(1,128)}, f32[1,80,128]{2,0,1:T(1,128)}, u32[]{:S(2)}, u32[]{:S(2)}) collective-permute-start(f32[1,80,128]{2,0,1:T(1,128)} %bitcast.21), channel_id=1, source_target_pairs={{2,0},{4,2},{6,4},{8,6},{10,8},{12,10},{14,12},{16,14},{18,16},{20... | collective-permute-start | bytes 122888 | tf_op jit(solution)/shard_map/ppermute | solution.py:25
  88.7 28.7 %collective-permute-start.32 = (f32[1,80,128]{2,0,1:T(1,128)}, f32[1,80,128]{2,0,1:T(1,128)}, u32[]{:S(2)}, u32[]{:S(2)}) collective-permute-start(f32[1,80,128]{2,0,1:T(1,128)} %bitcast.20), channel_id=1, source_target_pairs={{0,2},{2,4},{4,6},{6,8},{8,10},{10,12},{12,14},{14,16},{16,18},{18... | collective-permute-start | bytes 122888 | tf_op jit(solution)/shard_map/ppermute | solution.py:24
  99.6 22.1 %collective-permute-start.7 = (f32[18,80,1]{1,2,0:T(1,128)}, f32[18,80,1]{1,2,0:T(1,128)}, u32[]{:S(2)}, u32[]{:S(2)}) collective-permute-start(f32[18,80,1]{1,2,0:T(1,128)} %copy.99), channel_id=1, source_target_pairs={{1,0},{3,2},{5,4},{7,6},{9,8},{11,10},{13,12},{15,14},{17,16},{19,... | collective-permute-start | bytes 17288 | tf_op jit(solution)/shard_map/ppermute | solution.py:25
  101.8 26.7 %collective-permute-start.5 = (f32[18,80,1]{1,2,0:T(1,128)}, f32[18,80,1]{1,2,0:T(1,128)}, u32[]{:S(2)}, u32[]{:S(2)}) collective-permute-start(f32[18,80,1]{1,2,0:T(1,128)} %copy.96), channel_id=1, source_target_pairs={{0,1},{2,3},{4,5},{6,7},{8,9},{10,11},{12,13},{14,15},{16,17},{18,... | collective-permute-start | bytes 17288 | tf_op jit(solution)/shard_map/ppermute | solution.py:24
  109.5 33.2 %collective-permute-start.39 = (f32[18,80,1]{1,2,0:T(1,128)}, f32[18,80,1]{1,2,0:T(1,128)}, u32[]{:S(2)}, u32[]{:S(2)}) collective-permute-start(f32[18,80,1]{1,2,0:T(1,128)} %copy.127), channel_id=1, source_target_pairs={{1,0},{3,2},{5,4},{7,6},{9,8},{11,10},{13,12},{15,14},{17,16},{19,... | collective-permute-start | bytes 17288 | tf_op jit(solution)/shard_map/ppermute | solution.py:25
  111.6 32.2 %collective-permute-start.38 = (f32[18,80,1]{1,2,0:T(1,128)}, f32[18,80,1]{1,2,0:T(1,128)}, u32[]{:S(2)}, u32[]{:S(2)}) collective-permute-start(f32[18,80,1]{1,2,0:T(1,128)} %copy.124), channel_id=1, source_target_pairs={{0,1},{2,3},{4,5},{6,7},{8,9},{10,11},{12,13},{14,15},{16,17},{18,... | collective-permute-start | bytes 17288 | tf_op jit(solution)/shard_map/ppermute | solution.py:24
  119.5 26.4 %collective-permute-start.35 = (f32[18,80,1]{1,2,0:T(1,128)}, f32[18,80,1]{1,2,0:T(1,128)}, u32[]{:S(2)}, u32[]{:S(2)}) collective-permute-start(f32[18,80,1]{1,2,0:T(1,128)} %copy.113), channel_id=1, source_target_pairs={{1,0},{3,2},{5,4},{7,6},{9,8},{11,10},{13,12},{15,14},{17,16},{19,... | collective-permute-start | bytes 17288 | tf_op jit(solution)/shard_map/ppermute | solution.py:25
  121.7 25.3 %collective-permute-start.34 = (f32[18,80,1]{1,2,0:T(1,128)}, f32[18,80,1]{1,2,0:T(1,128)}, u32[]{:S(2)}, u32[]{:S(2)}) collective-permute-start(f32[18,80,1]{1,2,0:T(1,128)} %copy.110), channel_id=1, source_target_pairs={{0,1},{2,3},{4,5},{6,7},{8,9},{10,11},{12,13},{14,15},{16,17},{18,... | collective-permute-start | bytes 17288 | tf_op jit(solution)/shard_map/ppermute | solution.py:24
  137.0 17.1 %all-to-all-start.1 = ((f32[16,2,128]{2,1,0:T(2,128)}), f32[16,2,128]{2,1,0:T(2,128)}, u32[]{:S(2)}, u32[]{:S(2)}) async-start(f32[16,2,128]{2,1,0:T(2,128)} %bitcast.15), calls=%async_computation.1 | async-start | bytes 32768 | tf_op jit(solution)/shard_map/all_to_all | solution.py:166
  169.3 12.1 %collective-permute-start.29 = (f32[2,10,128]{2,0,1:T(2,128)S(1)}, f32[2,10,128]{2,0,1:T(2,128)S(1)}, u32[]{:S(2)}, u32[]{:S(2)}) collective-permute-start(f32[2,10,128]{2,0,1:T(2,128)S(1)} %get-tuple-element.69), channel_id=1, source_target_pairs={{2,0},{4,2},{6,4},{8,6},{10,8},{12,10},{14,12},{16,14},{18,16},{20... | collective-permute-start | bytes 30728 | tf_op jit(solution)/shard_map/ppermute | solution.py:25
  174.7 12.7 %collective-permute-start.23 = (f32[2,10,128]{2,0,1:T(2,128)S(1)}, f32[2,10,128]{2,0,1:T(2,128)S(1)}, u32[]{:S(2)}, u32[]{:S(2)}) collective-permute-start(f32[2,10,128]{2,0,1:T(2,128)S(1)} %get-tuple-element.65), channel_id=1, source_target_pairs={{2,0},{4,2},{6,4},{8,6},{10,8},{12,10},{14,12},{16,14},{18,16},{20... | collective-permute-start | bytes 30728 | tf_op jit(solution)/shard_map/ppermute | solution.py:25
  181.5 12.1 %collective-permute-start.30 = (f32[20,10,2]{2,0,1:T(8,128)S(1)}, f32[20,10,2]{2,0,1:T(8,128)S(1)}, u32[]{:S(2)}, u32[]{:S(2)}) collective-permute-start(f32[20,10,2]{2,0,1:T(8,128)S(1)} %get-tuple-element.45), channel_id=1, source_target_pairs={{1,0},{3,2},{5,4},{7,6},{9,8},{11,10},{13,12},{15,14},{17,16},{19,... | collective-permute-start | bytes 4808 | tf_op jit(solution)/shard_map/ppermute | solution.py:25
  (80 other events, 923.3 us)
where the time goes:
time: 203 us; the launch traced here: 200 us
  starting transfers between devices  122 us (60%)
  local copies, waits for them, and re-layouts  31.4 us (15%)
  other arithmetic  25.8 us (13%)
  waiting for transfers between devices  13.5 us (7%)
  matrix products  5.34 us (3%)
  between operations  2.15 us (1%)
    ppermute x20, starting transfers between devices, padded_2(): before = lax.ppermute(last, axis, up)  82.5 us
    ppermute x20, starting transfers between devices, padded_2(): after = lax.ppermute(first, axis, down)  25.9 us
    slice x21, local copies, waits for them, and re-layouts, padded_2(): last = lax.slice_in_dim(shard, length - width, length, axis=dim)  11.1 us
    ppermute x20, waiting for transfers between devices, padded_2(): after = lax.ppermute(first, axis, down)  10.2 us
    another operation x4, other arithmetic, local(): ocean_state = jnp.stack([current_x, current_y, ocean_heat])  8.72 us
    all_to_all x1, starting transfers between devices, local(): lax.all_to_all(outgoing, 'wide', split_axis=0, concat_axis=0, tiled=True)  8.05 us
    all_to_all x1, starting transfers between devices, local(): lax.all_to_all(outgoing_melt, 'wide', split_axis=0, concat_axis=0, tiled=...  5.68 us
    ppermute x3, local copies, waits for them, and re-layouts, padded_2(): before = lax.ppermute(last, axis, up)  5.15 us
  transfers between devices with their start and end apart: 42, of which 12 were waited for; matrix products, arithmetic and copies ran while one was open for 28% of the time, Pallas kernels for 0%

commit v1 on v0

v1 whole, which is shorter than its diff:
```python
import functools

import jax
import jax.numpy as jnp
from jax import lax
from jax.experimental import pallas as pl
from jax.experimental.pallas import tpu as pltpu
from jax.sharding import PartitionSpec as P

PICARD = 2
DIFFUSE = 0.2
GAMMA_MELT = 0.5
TIME_STEP = 0.05
SLOPE_SCALE = 0.1
STRAIN_FLOOR = 0.01
HEATING_RATE = 0.01

LANES = 128
PLANE_ROWS = 8
HALO = 4
RIM = 3
VMEM = pltpu.CompilerParams(vmem_limit_bytes=48 * 1024 * 1024)
HIGHEST = lax.Precision.HIGHEST
F32 = jnp.float32

THICK, GROUNDED, OCEAN_T, WET, ICE_LINK, OCEAN_LINK, OWN_LINK = range(7)
PART, EDGE_T0, EDGE_T1, EDGE_W0, PART_WET, EDGE_W1 = range(6)


def pad8(n):
    return -(-n // 8) * 8


def iota(shape, axis):
    return lax.broadcasted_iota(jnp.int32, shape, axis)


def right_lanes(period):
    lane = iota((1, LANES), 1)
    return lane % period < HALO


def left_lanes(period):
    lane = iota((1, LANES), 1)
    return lane % period >= period - HALO


def spread(column, count=LANES):
    rows = column.shape[0]
    eye = iota((rows, count), 0) == iota((rows, count), 1)
    return jnp.sum(jnp.where(eye, column, 0.0), axis=0, keepdims=True)


def divide(whole, part):
    return jnp.floor((whole + 0.5) * (1.0 / part))


def dot(a, b):
    return jnp.dot(a, b, precision=HIGHEST, preferred_element_type=F32)


def narrow_sides(n_narrow):
    place = lax.axis_index("narrow")
    return place < n_narrow - 1, place > 0


def merged(parts, right, left, n_narrow):
    has_right, has_left = narrow_sides(n_narrow)
    from_right, from_left = parts[0], parts[-1]
    if len(parts) == 1:
        keep = (right & has_right) | (left & has_left)
        return jnp.where(keep, from_right, 0.0)
    return jnp.where(right, from_right, jnp.where(left, from_left, 0.0))


def edges_kernel(
    ice_x, ice_y, ice_t, ocean_x, ocean_y, ocean_t, thick, grounded, wet, ice_links, ocean_links,
    out, plane_t, held, sems,
):
    rows, layers, _ = ice_x.shape
    levels = ocean_x.shape[1]
    layer_rows = pad8(layers)
    half = rows // 2
    copies = []
    for f, field in enumerate((ocean_x, ocean_y, ocean_t)):
        for h in range(2):
            part = pl.ds(h * half, half)
            copies.append(pltpu.make_async_copy(field.at[part], held.at[f, part], sems.at[f, h]))
            copies[-1].start()
    lane = iota((1, LANES), 1)
    base = levels
    for f, field in enumerate((ice_x, ice_y, ice_t)):
        total = jnp.zeros((layers, LANES), F32)
        for i in range(rows):
            turned = pltpu.roll(field[i], 8 * i, 1) if i else field[i]
            total = jnp.where((lane + HALO) % LANES // 8 == i, turned, total)
        out[base : base + layer_rows, :] = jnp.zeros((layer_rows, LANES), F32)
        out[base : base + layers, :] = total
        base += layer_rows
    total = jnp.zeros((levels, LANES), F32)
    for f in range(3):
        for h in range(2):
            copies[2 * f + h].wait()
            for i in range(h * half, (h + 1) * half):
                j = f * rows + i
                tile = held[f, i]
                turned = pltpu.roll(tile, 2 * j, 1) if j else tile
                total = jnp.where((lane + 1) % LANES // 2 == j, turned, total)
                if f == 2:
                    plane_t[i : i + 1, :] = tile[0:1, :]
    out[0:levels, :] = total
    planes = (
        thick[...],
        grounded[...].astype(F32),
        plane_t[...],
        wet[...].astype(F32),
        jnp.broadcast_to(ice_links[...].astype(F32) + 1.0, (rows, LANES)),
        jnp.broadcast_to(ocean_links[...].astype(F32) + 1.0, (rows, LANES)),
    )
    total = jnp.zeros((rows, LANES), F32)
    for j, plane in enumerate(planes):
        turned = pltpu.roll(plane, 16 * j, 1) if j else plane
        total = jnp.where((lane + HALO) % LANES // 16 == j, turned, total)
    out[base : base + rows, :] = total


def plane_halo(block, group):
    lane = iota((1, LANES), 1)
    turned = pltpu.roll(block, LANES - 16 * group, 1) if group else block
    return jnp.where((lane < HALO) | (lane >= LANES - HALO), turned, 0.0)


def ranks(own_col, member_col, order_sub, order_lane, own_row):
    hits = (own_col == own_row) & member_col & (order_sub < order_lane)
    return jnp.sum(hits.astype(F32), axis=0, keepdims=True)


def ocean_slots(link_col, rows, n_wide, cap, block):
    link_row = spread(link_col)
    parts = []
    for link in (link_col, link_row):
        number = link - 1.0
        tile = divide(number, rows)
        inner = number - tile * rows
        ok = link > 0.5
        parts.append(
            (
                tile,
                (
                    ok,
                    ok & (inner >= rows - RIM) & (tile < n_wide - 1.5),
                    ok & (inner < RIM) & (tile > 0.5),
                ),
            )
        )
    (tile_col, member_col), (tile_row, member_row) = parts
    order_sub, order_lane = iota((rows, LANES), 0), iota((rows, LANES), 1)
    place = iota((n_wide * block, LANES), 0).astype(F32)
    total = jnp.zeros((n_wide * block, LANES), F32)
    for k, shift in enumerate((0.0, 1.0, -1.0)):
        rank = ranks(tile_col, member_col[k], order_sub, order_lane, tile_row)
        target = jnp.where(
            member_row[k], (tile_row + shift) * block + (k * cap + rank), -1.0
        )
        total = total + (place == target).astype(F32)
    return total[:, :rows]


def draft_slots(link_col, rows, n_wide, cap, block):
    link_row = spread(link_col)
    tile_col, tile_row = divide(link_col - 1.0, rows), divide(link_row - 1.0, rows)
    order_sub, order_lane = iota((rows, LANES), 0), iota((rows, LANES), 1)
    rank = ranks(tile_col, link_col > 0.5, order_sub, order_lane, tile_row)
    target = jnp.where(link_row > 0.5, tile_row * block + (3 * cap + rank), -1.0)
    place = iota((n_wide * block, LANES), 0).astype(F32)
    return (place == target).astype(F32)[:, :rows]


def send_kernel(
    n_wide, n_narrow, cap, block, n_parts, levels,
    *refs,
):
    parts, refs = refs[:n_parts], refs[n_parts:]
    (
        ice_x, ice_y, ice_t, x_first, x_last, y_first, y_last, t_first, t_last, plane_t,
        thick, grounded, wet, ice_links, ocean_links, up, down, blocks,
    ) = refs
    rows, layers, _ = ice_x.shape
    layer_rows = pad8(layers)
    lane = iota((1, LANES), 1)
    base = levels + 3 * layer_rows
    plane_block = merged(
        [p[base : base + rows, :] for p in parts], right_lanes(16), left_lanes(16), n_narrow
    )
    link_own = ice_links[...].astype(F32) + 1.0
    plane_block = jnp.where(
        (lane + HALO) % LANES // 16 == OWN_LINK, link_own, plane_block
    )
    thick_plane = thick[...]
    grounded_plane = grounded[...].astype(F32)
    wet_plane = wet[...].astype(F32)
    at = 0
    for lasts, firsts in ((x_last, x_first), (y_last, y_first), (t_last, t_first)):
        up[at : at + levels, :] = lasts[0]
        down[at : at + levels, :] = firsts[0]
        at += levels
    for field in (ice_x, ice_y, ice_t):
        for i in range(HALO):
            up[at : at + layer_rows, :] = jnp.zeros((layer_rows, LANES), F32)
            down[at : at + layer_rows, :] = jnp.zeros((layer_rows, LANES), F32)
            up[at : at + layers, :] = field[rows - HALO + i]
            down[at : at + layers, :] = field[i]
            at += layer_rows
    strip = merged(
        [p[levels:base, :] for p in parts], right_lanes(8), left_lanes(8), n_narrow
    )
    up[at : at + 3 * layer_rows, :] = strip
    down[at : at + 3 * layer_rows, :] = strip
    at += 3 * layer_rows
    for plane in (thick_plane, grounded_plane, wet_plane, plane_block):
        up[at : at + PLANE_ROWS, :] = plane[rows - PLANE_ROWS :, :]
        down[at : at + PLANE_ROWS, :] = plane[:PLANE_ROWS, :]
        at += PLANE_ROWS
    wet_all = jnp.concatenate([wet_plane, plane_halo(plane_block, WET)], axis=1)
    warm = wet_all * jnp.concatenate([plane_t[...], plane_halo(plane_block, OCEAN_T)], axis=1)
    width = 2 * LANES
    row = iota((rows, width), 0)
    sums = []
    for value in (wet_all, warm):
        total = pltpu.roll(value, 1, 1) + pltpu.roll(value, width - 1, 1)
        total = total + jnp.where(row > 0, pltpu.roll(value, 1, 0), 0.0)
        sums.append(total + jnp.where(row < rows - 1, pltpu.roll(value, rows - 1, 0), 0.0))
    mixed = warm + DIFFUSE * (wet_all * sums[1] - warm * sums[0])
    draft = 0.9 * thick_plane * (1.0 - grounded_plane)
    own_slots = ocean_slots(ocean_links[...].astype(F32) + 1.0, rows, n_wide, cap, block)
    main = dot(own_slots, jnp.concatenate([mixed[:, :LANES], wet_plane], axis=1))
    count = n_wide * block
    slot = iota((count, 1), 0) % block
    first = main[:, :LANES] + dot(draft_slots(link_own, rows, n_wide, cap, block), draft)
    second = jnp.where(
        slot == 3 * cap,
        wet_plane[0:1, :],
        jnp.where(slot == 3 * cap + 1, wet_plane[rows - 1 : rows, :], main[:, LANES:]),
    )
    edge = (lane < HALO) | (lane >= LANES - HALO)
    mixed_edge = jnp.where(edge, mixed[:, LANES:], 0.0)
    wet_edge = wet_all[:, LANES:]
    warm_edge = warm[:, LANES:]
    packed = mixed_edge + pltpu.roll(wet_edge, 16 * PART_WET, 1)
    links = plane_halo(plane_block, OCEAN_LINK)
    if n_narrow == 2:
        third = dot(
            ocean_slots(jnp.max(links, axis=1, keepdims=True), rows, n_wide, cap, block), packed
        )
    else:
        third = dot(
            ocean_slots(links[:, 0:1], rows, n_wide, cap, block),
            jnp.where(right_lanes(16), packed, 0.0),
        ) + dot(
            ocean_slots(links[:, LANES - 1 : LANES], rows, n_wide, cap, block),
            jnp.where(left_lanes(16), packed, 0.0),
        )
    last = rows - 1
    ends = (
        pltpu.roll(warm_edge[0:1, :], 16 * EDGE_T0, 1)
        + pltpu.roll(warm_edge[last:, :], 16 * EDGE_T1, 1)
        + pltpu.roll(wet_edge[0:1, :], 16 * EDGE_W0, 1)
        + pltpu.roll(wet_edge[last:, :], 16 * EDGE_W1, 1)
    )
    third = jnp.where(
        slot == 3 * cap,
        warm[0:1, :LANES],
        jnp.where(slot == 3 * cap + 1, warm[last:, :LANES], third + ends),
    )
    for k, value in enumerate((first, second, third)):
        blocks[:, k * block : (k + 1) * block, :] = value.reshape(n_wide, block, LANES)


def ocean_kernel(
    n_narrow, n_parts,
    *refs,
):
    parts, refs = refs[:n_parts], refs[n_parts:]
    ocean_x, ocean_y, ocean_t, up, down, wet, out, held, coef, in_sems, out_sems = refs
    rows, levels, _ = ocean_x.shape
    chunks = in_sems.shape[1]
    step = rows // chunks
    copies = {}
    for f, field in enumerate((ocean_x, ocean_y, ocean_t)):
        for h in range(chunks):
            copy = pltpu.make_async_copy(
                field.at[pl.ds(h * step, step)],
                held.at[f, pl.ds(1 + h * step, step)],
                in_sems.at[f, h],
            )
            copy.start()
            copies[f, h] = copy
    lane = iota((1, LANES), 1)
    strip_base = parts[0].shape[0] - rows
    plane_block = merged(
        [p[strip_base:, :] for p in parts], right_lanes(16), left_lanes(16), n_narrow
    )
    plane_at = up.shape[0] - 2 * PLANE_ROWS
    wet_plane = wet[...].astype(F32)
    wet_halo = plane_halo(plane_block, WET)
    row = iota((rows, LANES), 0)
    above = jnp.where(
        row == 0,
        up[plane_at + PLANE_ROWS - 1 : plane_at + PLANE_ROWS, :],
        pltpu.roll(wet_plane, 1, 0),
    )
    below = jnp.where(row == rows - 1, down[plane_at : plane_at + 1, :], pltpu.roll(wet_plane, rows - 1, 0))
    before = pltpu.roll(jnp.where(lane == LANES - 1, wet_halo, wet_plane), 1, 1)
    after = pltpu.roll(jnp.where(lane == 0, wet_halo, wet_plane), LANES - 1, 1)
    scale = DIFFUSE * wet_plane
    coef[0] = scale * above
    coef[1] = scale * below
    coef[2] = scale * before
    coef[3] = scale * after
    coef[4] = 1.0 - scale * (above + below + before + after)
    for f in range(3):
        held[f, 0] = up[f * levels : (f + 1) * levels, :]
        held[f, rows + 1] = down[f * levels : (f + 1) * levels, :]
    odd = lane % 2 == 1
    halo = merged([p[0:levels, :] for p in parts], ~odd, odd, n_narrow)
    first, last = lane == 0, lane == LANES - 1
    writes = []
    for f in range(3):
        for h in range(chunks):
            copies[f, h].wait()
        for h in range(chunks):
            for i in range(h * step, (h + 1) * step):
                j = f * rows + i
                side = pltpu.roll(halo, LANES - 2 * j, 1) if j else halo
                centre = held[f, i + 1]
                left = pltpu.roll(jnp.where(last, side, centre), 1, 1)
                right = pltpu.roll(jnp.where(first, side, centre), LANES - 1, 1)
                value = centre * coef[4, i : i + 1, :]
                value = value + held[f, i] * coef[0, i : i + 1, :]
                value = value + held[f, i + 2] * coef[1, i : i + 1, :]
                value = value + left * coef[2, i : i + 1, :]
                value = value + right * coef[3, i : i + 1, :]
                held[f + 3, i] = value
            part = pl.ds(h * step, step)
            copy = pltpu.make_async_copy(held.at[f + 3, part], out.at[f, part], out_sems.at[f, h])
            copy.start()
            writes.append(copy)
    for copy in writes:
        copy.wait()


def ice_slots(link_col, kind_col, rows, cap, block, count, n_wide):
    link_row = spread(link_col)
    kind_row = spread(kind_col)
    number = link_col - 1.0
    tile = divide(number, rows)
    inner = number - tile * rows
    tile_row = divide(link_row - 1.0, rows)
    ok = (link_col > 0.5) & (kind_col > -0.5)
    ok_row = (link_row > 0.5) & (kind_row > -0.5)
    hits = (tile == tile_row) & (kind_col == kind_row) & ok_row & (link_row < link_col)
    rank = jnp.sum(hits.astype(F32), axis=1, keepdims=True)
    place = iota((link_col.shape[0], count), 1).astype(F32)

    def hot(keep, target):
        return (place == jnp.where(keep, target, -1.0)).astype(F32)

    top, bottom = inner < 0.5, inner > rows - 1.5
    edge = ok & (top | bottom)
    near = jnp.where(top, tile - 1.0, tile + 1.0)
    near_ok = edge & (near > -0.5) & (near < n_wide - 0.5)
    slot = hot(ok, tile * block + kind_col * cap + rank)
    near_edge = hot(near_ok, near * block + jnp.where(top, 3.0 * cap + 1.0, 3.0 * cap))
    own_edge = hot(edge, tile * block + jnp.where(top, 3.0 * cap, 3.0 * cap + 1.0))
    near_slot = hot(near_ok, near * block)
    own_slot = hot(edge, tile * block)
    return slot, near_edge, own_edge, near_slot, own_slot, top


def final_kernel(
    n_wide, n_narrow, cap, block, n_parts, levels,
    *refs,
):
    parts, refs = refs[:n_parts], refs[n_parts:]
    (
        ice_x, ice_y, ice_t, up, down, blocks, thick, grounded, wet, ice_links, ocean_links, ocean_in,
        ice_out, ocean_out, thick_out, melt_out,
        vel, rate, eta, push, side, heat, flat, top_level, sems,
    ) = refs
    rows, layers, _ = ice_x.shape
    layer_rows = pad8(layers)
    fetch = pltpu.make_async_copy(ocean_in.at[2, :, pl.ds(0, 8), :], top_level, sems.at[0])
    fetch.start()
    width = 2 * LANES
    lane = iota((1, LANES), 1)
    wide_lane = iota((1, width), 1)
    place_wide = lax.axis_index("wide")
    has_right, has_left = narrow_sides(n_narrow)
    has_up, has_down = place_wide > 0, place_wide < n_wide - 1
    base = levels + 3 * layer_rows
    plane_block = merged(
        [p[base : base + rows, :] for p in parts], right_lanes(16), left_lanes(16), n_narrow
    )
    plane_at = up.shape[0] - 4 * PLANE_ROWS
    tall = rows + 2 * PLANE_ROWS

    def plane(k):
        at = plane_at + k * PLANE_ROWS
        return up[at : at + PLANE_ROWS, :], down[at : at + PLANE_ROWS, :]

    thick_up, thick_down = plane(0)
    grounded_up, grounded_down = plane(1)
    block_up, block_down = plane(3)
    block_tall = jnp.concatenate([block_up, plane_block, block_down], axis=0)
    thick_main = thick[...]
    thick_tall = jnp.concatenate(
        [
            jnp.concatenate([thick_up, thick_main, thick_down], axis=0),
            plane_halo(block_tall, THICK),
        ],
        axis=1,
    )
    grounded_tall = jnp.concatenate(
        [
            jnp.concatenate([grounded_up, grounded[...].astype(F32), grounded_down], axis=0),
            plane_halo(block_tall, GROUNDED),
        ],
        axis=1,
    )
    tall_row = iota((tall, 1), 0)
    kind = jnp.where(
        (tall_row >= PLANE_ROWS) & (tall_row < PLANE_ROWS + rows),
        0.0,
        jnp.where(
            (tall_row >= PLANE_ROWS - RIM) & (tall_row < PLANE_ROWS),
            1.0,
            jnp.where(
                (tall_row >= PLANE_ROWS + rows) & (tall_row < PLANE_ROWS + rows + RIM), 2.0, -1.0
            ),
        ),
    )
    count = n_wide * block
    first = blocks[:, 0:block, :].reshape(count, LANES)
    second = blocks[:, block : 2 * block, :].reshape(count, LANES)
    third = blocks[:, 2 * block : 3 * block, :].reshape(count, LANES)
    own_link = jnp.concatenate(
        [
            block_up[:, 16 * OWN_LINK : 16 * OWN_LINK + 1],
            ice_links[...].astype(F32) + 1.0,
            block_down[:, 16 * OWN_LINK : 16 * OWN_LINK + 1],
        ],
        axis=0,
    )
    slot, near_edge, own_edge, _, _, _ = ice_slots(
        own_link, kind, rows, cap, block, count, n_wide
    )
    got = dot(slot, jnp.concatenate([first, second], axis=1))
    near = dot(near_edge, jnp.concatenate([second, third], axis=1))
    own = dot(own_edge, third)
    wet_main = got[:, LANES:]
    mixed_main = got[:, :LANES] + DIFFUSE * (
        wet_main * near[:, LANES:] - near[:, :LANES] * own
    )

    def halo_melt(link_col):
        slot, _, _, near_slot, own_slot, top = ice_slots(
            link_col, kind, rows, cap, block, count, n_wide
        )
        got = dot(slot, third)
        near = dot(near_slot, third)
        own = dot(own_slot, third)

        def group(value, j):
            return pltpu.roll(value, LANES - 16 * j, 1) if j else value

        wet_got = group(got, PART_WET)
        near_warm = jnp.where(top, group(near, EDGE_T1), group(near, EDGE_T0))
        near_wet = jnp.where(top, group(near, EDGE_W1), group(near, EDGE_W0))
        own_warm = jnp.where(top, group(own, EDGE_T0), group(own, EDGE_T1))
        return got + DIFFUSE * (wet_got * near_warm - near_wet * own_warm), wet_got

    links = plane_halo(block_tall, ICE_LINK)
    if n_narrow == 2:
        mixed_side, wet_side = halo_melt(jnp.max(links, axis=1, keepdims=True))
    else:
        mixed_side, wet_side = (
            jnp.where(lane < HALO, a, b)
            for a, b in zip(halo_melt(links[:, 0:1]), halo_melt(links[:, LANES - 1 : LANES]))
        )
    mixed_tall = jnp.concatenate([mixed_main, mixed_side], axis=1)
    wet_tall = jnp.concatenate([wet_main, wet_side], axis=1)
    inside = (
        ((tall_row >= PLANE_ROWS) | has_up)
        & ((tall_row < PLANE_ROWS + rows) | has_down)
        & (
            (wide_lane < LANES)
            | ((wide_lane < LANES + HALO) & has_right)
            | ((wide_lane >= width - HALO) & has_left)
        )
    ).astype(F32)
    open_ice = 1.0 - grounded_tall
    draft_tall = 0.9 * thick_tall * open_ice
    melt_tall = GAMMA_MELT * (mixed_tall - wet_tall * (0.0832 - 0.761 * draft_tall))
    new_thick = (thick_tall - TIME_STEP * melt_tall * open_ice) * inside
    thick_out[...] = new_thick[PLANE_ROWS : PLANE_ROWS + rows, :LANES]
    surface = new_thick * (0.1 + 0.9 * grounded_tall)
    push_scale = (-0.5 * SLOPE_SCALE) * new_thick
    flat[0] = push_scale * (pltpu.roll(surface, tall - 1, 0) - pltpu.roll(surface, 1, 0))
    flat[1] = push_scale * (pltpu.roll(surface, width - 1, 1) - pltpu.roll(surface, 1, 1))
    flat[2] = 0.1 + 9.9 * grounded_tall
    flat[3] = inside
    ocean_link = ocean_links[...].astype(F32) + 1.0
    ocean_row = spread(ocean_link)
    tile = divide(ocean_link - 1.0, rows)
    tile_row = divide(ocean_row - 1.0, rows)
    hits = (tile == tile_row) & (ocean_row > 0.5) & (ocean_row < ocean_link)
    rank = jnp.sum(hits.astype(F32), axis=1, keepdims=True)
    coupled = ocean_link > 0.5
    target = jnp.where(coupled, tile * block + 3 * cap + rank, -1.0)
    ocean_draft = dot((iota((rows, count), 1).astype(F32) == target).astype(F32), first)
    fetch.wait()
    heat_top = jnp.concatenate([top_level[i, 0:1, :] for i in range(rows)], axis=0)
    melt = (
        GAMMA_MELT
        * (heat_top - (0.0832 - 0.761 * ocean_draft))
        * wet[...].astype(F32)
        * coupled.astype(F32)
    )
    melt_out[...] = melt
    new_top = heat_top - 0.2 * melt
    for i in range(rows):
        top_level[i, 0:1, :] = new_top[i : i + 1, :]
    store = pltpu.make_async_copy(top_level, ocean_out.at[2, :, pl.ds(0, 8), :], sems.at[1])
    store.start()
    n_ice = rows + 2 * HALO
    offset = PLANE_ROWS - HALO
    ice_at = 3 * levels
    strip_at = ice_at + 3 * HALO * layer_rows
    strip = merged(
        [p[levels:base, :] for p in parts], right_lanes(8), left_lanes(8), n_narrow
    )
    edge = (lane < HALO) | (lane >= LANES - HALO)
    for f, field in enumerate((ice_x, ice_y, ice_t)):
        strips = (
            up[strip_at + f * layer_rows : strip_at + (f + 1) * layer_rows, :],
            strip[f * layer_rows : (f + 1) * layer_rows, :],
            down[strip_at + f * layer_rows : strip_at + (f + 1) * layer_rows, :],
        )
        for b in range(n_ice):
            i = b - HALO
            if i < 0:
                at = ice_at + (f * HALO + b) * layer_rows
                main, source, i = up[at : at + layer_rows, :], strips[0], rows + i
            elif i < rows:
                main = jnp.concatenate(
                    [field[i], jnp.zeros((layer_rows - layers, LANES), F32)], axis=0
                )
                source = strips[1]
            else:
                at = ice_at + (f * HALO + i - rows) * layer_rows
                main, source, i = down[at : at + layer_rows, :], strips[2], i - rows
            turned = pltpu.roll(source, (LANES - 8 * i) % LANES, 1) if i else source
            beside = jnp.where(edge, turned, 0.0)
            if f < 2:
                vel[f, b, :, 0:LANES] = main
                vel[f, b, :, LANES:width] = beside
            else:
                mask = inside[b + offset : b + offset + 1, :]
                rate[b, :, 0:LANES] = jnp.exp(0.25 * main) * mask[:, :LANES]
                rate[b, :, LANES:width] = jnp.exp(0.25 * beside) * mask[:, LANES:]
    level = iota((layer_rows, 1), 0)
    not_last = (level < layers - 1).astype(F32)
    links_up_down = (level > 0).astype(F32) + not_last
    real = (level < layers).astype(F32)

    def strain(b, sweep):
        u, v = vel[2 * sweep, b], vel[2 * sweep + 1, b]
        u_left, u_right = pltpu.roll(u, 1, 1), pltpu.roll(u, width - 1, 1)
        v_left, v_right = pltpu.roll(v, 1, 1), pltpu.roll(v, width - 1, 1)
        ux = vel[2 * sweep, b + 1] - vel[2 * sweep, b - 1]
        vx = vel[2 * sweep + 1, b + 1] - vel[2 * sweep + 1, b - 1]
        uy, vy = u_right - u_left, v_right - v_left
        uz = (pltpu.roll(u, layer_rows - 1, 0) - u) * not_last
        vz = (pltpu.roll(v, layer_rows - 1, 0) - v) * not_last
        cross = uy + vx
        eps2 = 0.25 * (ux * (ux + vy) + vy * vy + 0.25 * (cross * cross) + (uz * uz + vz * vz))
        value = rate[b] * jnp.exp((-1.0 / 3.0) * jnp.log(eps2 + STRAIN_FLOOR))
        eta[b] = value
        push[0, b] = value * u
        push[1, b] = value * v
        side[0, b] = u_left + u_right
        side[1, b] = v_left + v_right
        if sweep == PICARD - 1:
            heat[b] = (value * eps2)[:, :LANES]

    def relax(b, sweep):
        last = sweep == PICARD - 1
        span = LANES if last else width
        a = b + offset
        centre = eta[b]
        around = eta[b - 1] + eta[b + 1] + pltpu.roll(centre, 1, 1) + pltpu.roll(centre, width - 1, 1)
        diagonal = centre * (2.0 + links_up_down) + 0.5 * around + flat[2, pl.ds(a, 1), :]
        inverse = 1.0 / diagonal[:, :span]
        for f in range(2):
            field = vel[2 * sweep + f, b]
            total = 0.5 * (vel[2 * sweep + f, b - 1] + vel[2 * sweep + f, b + 1] + side[f, b])
            total = total + pltpu.roll(field, 1, 0) + pltpu.roll(field, layer_rows - 1, 0)
            pushed = push[f, b]
            near = push[f, b - 1] + push[f, b + 1]
            near = near + pltpu.roll(pushed, 1, 1) + pltpu.roll(pushed, width - 1, 1)
            total = (centre * total + 0.5 * near + flat[f, pl.ds(a, 1), :])[:, :span] * inverse
            if last:
                ice_out[f, b - HALO] = total[:layers, :]
            else:
                vel[2 * sweep + 2 + f, b] = total * (real * flat[3, pl.ds(a, 1), :])
        if last:
            ice_out[2, b - HALO] = ice_t[b - HALO] + HEATING_RATE * heat[b][:layers, :]

    for sweep in range(PICARD):
        reach = 2 * (PICARD - 1 - sweep)
        low, high = HALO - reach, HALO + rows + reach
        lax.fori_loop(low - 1, high + 1, lambda b, c: (strain(b, sweep), c)[1], 0)
        lax.fori_loop(low, high, lambda b, c: (relax(b, sweep), c)[1], 0)
    store.wait()


def local(
    ice_x, ice_y, ice_temp, ocean_x, ocean_y, ocean_temp, thick, grounded_mask, wet_mask, ice_links, ocean_links,
):
    n_wide, n_narrow = lax.axis_size("wide"), lax.axis_size("narrow")
    rows, layers, columns = ice_x.shape
    levels = ocean_x.shape[1]
    layer_rows = pad8(layers)
    cap = max(1, 2 * rows // n_wide)
    block = pad8(max(4 * cap, 3 * cap + 2))
    assert columns == LANES and ice_links.shape[0] == rows
    whole = pl.BlockSpec(memory_space=pltpu.VMEM)
    anywhere = pl.BlockSpec(memory_space=pl.ANY)

    def edge_row(i):
        return pl.BlockSpec((1, levels, columns), lambda _: (i, 0, 0))

    message, plane_t = pl.pallas_call(
        edges_kernel,
        name="edges",
        out_shape=(
            jax.ShapeDtypeStruct((levels + 3 * layer_rows + rows, LANES), F32),
            jax.ShapeDtypeStruct((rows, LANES), F32),
        ),
        in_specs=[whole] * 3 + [anywhere] * 3 + [whole] * 5,
        out_specs=(whole, whole),
        scratch_shapes=[
            pltpu.VMEM((3, rows, levels, columns), F32),
            pltpu.SemaphoreType.DMA((3, 2)),
        ],
        compiler_params=VMEM,
    )(ice_x, ice_y, ice_temp, ocean_x, ocean_y, ocean_temp, thick, grounded_mask, wet_mask, ice_links, ocean_links)
    if n_narrow == 2:
        parts = [lax.ppermute(message, "narrow", [(0, 1), (1, 0)])]
    else:
        ahead = [(i, i + 1) for i in range(n_narrow - 1)]
        parts = [
            lax.ppermute(message, "narrow", [(j, i) for i, j in ahead]),
            lax.ppermute(message, "narrow", ahead),
        ]
    tall = 3 * levels + 3 * HALO * layer_rows + 3 * layer_rows + 4 * PLANE_ROWS
    to_down, to_up, blocks = pl.pallas_call(
        functools.partial(send_kernel, n_wide, n_narrow, cap, block, len(parts), levels),
        name="send",
        out_shape=(
            jax.ShapeDtypeStruct((tall, LANES), F32),
            jax.ShapeDtypeStruct((tall, LANES), F32),
            jax.ShapeDtypeStruct((n_wide, 3 * block, LANES), F32),
        ),
        in_specs=[whole] * (len(parts) + 3)
        + [edge_row(0), edge_row(rows - 1)] * 3
        + [whole] * 6,
        out_specs=(whole,) * 3,
        grid=(1,),
        compiler_params=VMEM,
    )(
        *parts, ice_x, ice_y, ice_temp, ocean_x, ocean_x, ocean_y, ocean_y, ocean_temp, ocean_temp,
        plane_t, thick, grounded_mask, wet_mask, ice_links, ocean_links,
    )
    blocks = lax.all_to_all(blocks, "wide", split_axis=0, concat_axis=0, tiled=True)
    ahead = [(i, i + 1) for i in range(n_wide - 1)]
    up = lax.ppermute(to_down, "wide", ahead)
    down = lax.ppermute(to_up, "wide", [(j, i) for i, j in ahead])
    chunks = 2
    ocean = pl.pallas_call(
        functools.partial(ocean_kernel, n_narrow, len(parts)),
        name="ocean",
        out_shape=jax.ShapeDtypeStruct((3, rows, levels, columns), F32),
        in_specs=[whole] * len(parts) + [anywhere] * 3 + [whole] * 3,
        out_specs=anywhere,
        scratch_shapes=[
            pltpu.VMEM((6, rows + 2, levels, columns), F32),
            pltpu.VMEM((5, rows, LANES), F32),
            pltpu.SemaphoreType.DMA((3, chunks)),
            pltpu.SemaphoreType.DMA((3, chunks)),
        ],
        compiler_params=VMEM,
        cost_estimate=pl.CostEstimate(flops=10_000_000, bytes_accessed=8_000_000, transcendentals=0),
    )(*parts, ocean_x, ocean_y, ocean_temp, up, down, wet_mask)
    n_ice = rows + 2 * HALO
    n_tall = rows + 2 * PLANE_ROWS
    wide = 2 * LANES
    return pl.pallas_call(
        functools.partial(final_kernel, n_wide, n_narrow, cap, block, len(parts), levels),
        name="final",
        out_shape=(
            jax.ShapeDtypeStruct((3, rows, layers, columns), F32),
            jax.ShapeDtypeStruct((3, rows, levels, columns), F32),
            jax.ShapeDtypeStruct((rows, columns), F32),
            jax.ShapeDtypeStruct((rows, columns), F32),
        ),
        in_specs=[whole] * (len(parts) + 11) + [anywhere],
        out_specs=(whole, anywhere, whole, whole),
        input_output_aliases={len(parts) + 11: 1},
        scratch_shapes=[
            pltpu.VMEM((2 * PICARD, n_ice, layer_rows, wide), F32),
            pltpu.VMEM((n_ice, layer_rows, wide), F32),
            pltpu.VMEM((n_ice, layer_rows, wide), F32),
            pltpu.VMEM((2, n_ice, layer_rows, wide), F32),
            pltpu.VMEM((2, n_ice, layer_rows, wide), F32),
            pltpu.VMEM((n_ice, layer_rows, LANES), F32),
            pltpu.VMEM((4, n_tall, wide), F32),
            pltpu.VMEM((rows, 8, LANES), F32),
            pltpu.SemaphoreType.DMA((2,)),
        ],
        compiler_params=VMEM,
    )(*parts, ice_x, ice_y, ice_temp, up, down, blocks, thick, grounded_mask, wet_mask, ice_links, ocean_links, ocean)


def solution(mesh):
    column = P("wide", None, "narrow")
    plane = P("wide", "narrow")
    return jax.shard_map(
        local,
        mesh=mesh,
        in_specs=(column,) * 6 + (plane,) * 5,
        out_specs=(P(None, "wide", None, "narrow"), P(None, "wide", None, "narrow"), plane, plane),
        check_vma=False,
    )
```

time: 203 us -> 53.6 us (0.26)
  the two profiles are of different devices: /device:TPU:0 before, /device:TPU:17 now
where the time goes in v1:
time: 53.6 us; the launch traced here: 52.9 us
  Pallas kernels  18.8 us (35%)
  starting transfers between devices  14.2 us (26%)
  local copies, waits for them, and re-layouts  10.4 us (19%)
  waiting for transfers between devices  8.84 us (16%)
  between operations  0.75 us (1%)
    pallas_call x1, Pallas kernels, local(): pl.pallas_call(functools.partial(final_kernel, n_wide, n_narrow, cap, blo...  10.2 us
    unnamed x29, local copies, waits for them, and re-layouts  9.59 us
    all_to_all x1, starting transfers between devices, local(): lax.all_to_all(blocks, 'wide', split_axis=0, concat_axis=0, tiled=True)  7.62 us
    pallas_call x1, Pallas kernels, local(): pl.pallas_call(functools.partial(ocean_kernel, n_narrow, len(parts)), nam...  5.58 us
    ppermute x1, waiting for transfers between devices, local(): down = lax.ppermute(to_up, 'wide', [(j, i) for i, j in ahead])  4.81 us
    ppermute x1, starting transfers between devices, local(): up = lax.ppermute(to_down, 'wide', ahead)  3.33 us
    ppermute x1, waiting for transfers between devices, local(): up = lax.ppermute(to_down, 'wide', ahead)  2.06 us
    ppermute x1, waiting for transfers between devices, local(): parts = [lax.ppermute(message, 'narrow', [(0, 1), (1, 0)])]  1.96 us
  transfers between devices with their start and end apart: 4, of which 3 were waited for; matrix products, arithmetic and copies ran while one was open for 0% of the time, Pallas kernels for 11%

profile of v1, /device:TPU:17, one launch (start us, length us, event | category | flops | bytes accessed | tf_op | source)
XLA Modules:
  0.0 52.9 jit_solution(8701473843715983593)
XLA Ops:
  0.6 0.7 %copy.19.ice_links.refs_14_.refs_10_ = s32[16,1]{1,0:T(8,128)S(1)} copy(s32[16,1]{0,1:T(1,128)} %param.20) | data formatting | bytes 128 | tf_op args[9]
  1.4 0.7 %copy.20.ocean_links.refs_15_.refs_11_ = s32[16,1]{1,0:T(8,128)S(1)} copy(s32[16,1]{0,1:T(1,128)} %param.21) | data formatting | bytes 128 | tf_op args[10]
  2.1 0.9 %copy.16.ice_x.refs_1_ = f32[16,10,128]{2,1,0:T(8,128)S(1)} copy(f32[16,10,128]{2,0,1:T(8,128)} %param.11) | data formatting | bytes 163840 | tf_op args[0]
  3.0 0.9 %copy.17.ice_y.refs_2_ = f32[16,10,128]{2,1,0:T(8,128)S(1)} copy(f32[16,10,128]{2,0,1:T(8,128)} %param.12) | data formatting | bytes 163840 | tf_op args[1]
  3.9 0.9 %copy.18.ice_t.refs_3_ = f32[16,10,128]{2,1,0:T(8,128)S(1)} copy(f32[16,10,128]{2,0,1:T(8,128)} %param.13) | data formatting | bytes 163840 | tf_op args[2]
  4.9 0.0 copy-start
  4.9 1.1 %copy-done = f32[16,80,128]{2,1,0:T(8,128)S(1)} copy-done((f32[16,80,128]{2,1,0:T(8,128)S(1)}, f32[16,80,128]{2,1,0:T(8,128)}, u32[]{:S(2)}) %copy-start) | copy-done | bytes 655384
  5.9 1.1 %copy-done.2 = f32[16,80,128]{2,1,0:T(8,128)S(1)} copy-done((f32[16,80,128]{2,1,0:T(8,128)S(1)}, f32[16,80,128]{2,1,0:T(8,128)}, u32[]{:S(2)}) %copy-start.2) | copy-done | bytes 655384
  7.0 1.1 %copy-done.4 = f32[16,80,128]{2,1,0:T(8,128)S(1)} copy-done((f32[16,80,128]{2,1,0:T(8,128)S(1)}, f32[16,80,128]{2,1,0:T(8,128)}, u32[]{:S(2)}) %copy-start.4) | copy-done | bytes 655384
  8.1 0.7 %copy-done.6 = s32[16,128]{1,0:T(8,128)S(1)} copy-done((s32[16,128]{1,0:T(8,128)S(1)}, s32[16,128]{1,0:T(8,128)}, u32[]{:S(2)}) %copy-start.6) | copy-done | bytes 8216
  8.8 0.7 %copy-done.8 = f32[16,128]{1,0:T(8,128)S(1)} copy-done((f32[16,128]{1,0:T(8,128)S(1)}, f32[16,128]{1,0:T(8,128)}, u32[]{:S(2)}) %copy-start.8) | copy-done | bytes 8216
  9.5 0.7 %copy-done.10 = s32[16,128]{1,0:T(8,128)S(1)} copy-done((s32[16,128]{1,0:T(8,128)S(1)}, s32[16,128]{1,0:T(8,128)}, u32[]{:S(2)}) %copy-start.10) | copy-done | bytes 8216
  10.2 1.8 %edges.1 = (f32[144,128]{1,0:T(8,128)S(1)}, f32[16,128]{1,0:T(8,128)S(1)}) custom-call(f32[16,10,128]{2,1,0:T(8,128)S(1)} %copy.16.ice_x.refs_1_, f32[16,10,128]{2,1,0:T(8,128)S(1)} %copy.17.ice_y.refs_2_, f32[16,10,128]{2,1,0:T(8,128)S(1)} %copy.18.ice_t.refs_3_, f32[16,80,128]{2,1,0:T(8,128)S(1)} %copy-done, f32[16,80,128]{2,1,0:T(8,128)S(1)} %copy-done.2, ...), custom_call_target="tpu_custom_call" | custom-call | tf_op jit(solution)/shard_map/edges/pallas_call | solution.py:643
  12.0 1.3 %collective-permute-start = (f32[144,128]{1,0:T(8,128)S(1)}, f32[144,128]{1,0:T(8,128)S(1)}, u32[]{:S(2)}, u32[]{:S(2)}) collective-permute-start(f32[144,128]{1,0:T(8,128)S(1)} %get-tuple-element.9), channel_id=1, source_target_pairs={{0,1},{1,0},{2,3},{3,2},{4,5},{5,4},{6,7},{7,6},{8,9},{9,8},{10,11... | collective-permute-start | bytes 221192 | tf_op jit(solution)/shard_map/ppermute | solution.py:659
  13.3 2.0 %collective-permute-done.refs_0_ = f32[144,128]{1,0:T(8,128)S(1)} collective-permute-done((f32[144,128]{1,0:T(8,128)S(1)}, f32[144,128]{1,0:T(8,128)S(1)}, u32[]{:S(2)}, u32[]{:S(2)}) %collective-permute-start) | collective-permute-done | bytes 73760 | tf_op jit(solution)/shard_map/ppermute | solution.py:659
  15.3 1.2 %send.1 = (f32[512,128]{1,0:T(8,128)}, f32[512,128]{1,0:T(8,128)S(1)}, f32[16,24,128]{2,1,0:T(8,128)}) custom-call(f32[144,128]{1,0:T(8,128)S(1)} %collective-permute-done.refs_0_, f32[16,10,128]{2,1,0:T(8,128)S(1)} %copy.16.ice_x.refs_1_, f32[16,10,128]{2,1,0:T(8,128)S(1)} %copy.17.ice_y.refs_2_, f32[16,10,128]{2,1,0:T(8,128)S(1)} %copy.18.ice_t.refs_3_, ...), custom_call_target="tpu_custom_call" | custom-call | tf_op jit(solution)/shard_map/send/pallas_call | solution.py:667
  16.5 7.6 %all-to-all-start = ((f32[16,24,128]{2,1,0:T(8,128)}), f32[16,24,128]{2,1,0:T(8,128)S(1)}, u32[]{:S(2)}, u32[]{:S(2)}) async-start(f32[16,24,128]{2,1,0:T(8,128)} %get-tuple-element.13), calls=%async_computation | async-start | bytes 393216 | tf_op jit(solution)/shard_map/all_to_all | solution.py:685
  24.1 3.3 %collective-permute-start.1 = (f32[512,128]{1,0:T(8,128)}, f32[512,128]{1,0:T(8,128)S(1)}, u32[]{:S(2)}, u32[]{:S(2)}) collective-permute-start(f32[512,128]{1,0:T(8,128)} %get-tuple-element.11), channel_id=1, source_target_pairs={{0,2},{2,4},{4,6},{6,8},{8,10},{10,12},{12,14},{14,16},{16,18},{18... | collective-permute-start | bytes 786440 | tf_op jit(solution)/shard_map/ppermute | solution.py:687
  27.5 1.9 %collective-permute-start.2 = (f32[512,128]{1,0:T(8,128)S(1)}, f32[512,128]{1,0:T(8,128)S(1)}, u32[]{:S(2)}, u32[]{:S(2)}) collective-permute-start(f32[512,128]{1,0:T(8,128)S(1)} %get-tuple-element.12), channel_id=1, source_target_pairs={{2,0},{4,2},{6,4},{8,6},{10,8},{12,10},{14,12},{16,14},{18,16},{20... | collective-permute-start | bytes 786440 | tf_op jit(solution)/shard_map/ppermute | solution.py:688
  29.4 2.1 %collective-permute-done.1.refs_4_ = f32[512,128]{1,0:T(8,128)S(1)} collective-permute-done((f32[512,128]{1,0:T(8,128)}, f32[512,128]{1,0:T(8,128)S(1)}, u32[]{:S(2)}, u32[]{:S(2)}) %collective-permute-start.1) | collective-permute-done | bytes 262176 | tf_op jit(solution)/shard_map/ppermute | solution.py:687
  31.5 4.8 %collective-permute-done.2.refs_5_ = f32[512,128]{1,0:T(8,128)S(1)} collective-permute-done((f32[512,128]{1,0:T(8,128)S(1)}, f32[512,128]{1,0:T(8,128)S(1)}, u32[]{:S(2)}, u32[]{:S(2)}) %collective-permute-start.2) | collective-permute-done | bytes 262176 | tf_op jit(solution)/shard_map/ppermute | solution.py:688
  36.3 5.6 %ocean.1.refs_12_ = f32[3,16,80,128]{3,2,1,0:T(8,128)} custom-call(f32[144,128]{1,0:T(8,128)S(1)} %collective-permute-done.refs_0_, f32[16,80,128]{2,1,0:T(8,128)S(1)} %copy-done.1, f32[16,80,128]{2,1,0:T(8,128)S(1)} %copy-done.3, f32[16,80,128]{2,1,0:T(8,128)S(1)} %copy-done.5, f32[512,128]{1,0:T(8,128)S(1)} %collective-permute-done.1.refs_4_, ...), custom_call_target="tpu_custom_call" | custom-call | flops 10000000 | bytes 8000000 | tf_op jit(solution)/shard_map/ocean/pallas_call | solution.py:690
  41.9 10.2 %final.1 = (f32[3,16,10,128]{3,2,1,0:T(8,128)S(1)}, f32[3,16,80,128]{3,2,1,0:T(8,128)}, f32[16,128]{1,0:T(8,128)}, f32[16,128]{1,0:T(8,128)}) custom-call(f32[144,128]{1,0:T(8,128)S(1)} %collective-permute-done.refs_0_, f32[16,10,128]{2,1,0:T(8,128)S(1)} %copy.16.ice_x.refs_1_, ...), custom_call_target="tpu_custom_call", output_to_operand_aliasing={{1}: (12, {})} | custom-call | tf_op jit(solution)/shard_map/final/pallas_call | solution.py:708
  52.1 0.8 %copy.31 = f32[3,16,10,128]{3,1,2,0:T(8,128)} copy(f32[3,16,10,128]{3,2,1,0:T(8,128)S(1)} %get-tuple-element.14) | data formatting | bytes 491520 | tf_op jit(solution)/shard_map/final/pallas_call | solution.py:708
  (18 shorter events, 0.0 us)
Async XLA Ops:
  4.9 1.1 %copy-start = (f32[16,80,128]{2,1,0:T(8,128)S(1)}, f32[16,80,128]{2,1,0:T(8,128)}, u32[]{:S(2)}) copy-start(f32[16,80,128]{2,1,0:T(8,128)} %refs_1_.3) | copy-start | bytes 1966084
  5.9 1.1 %copy-start.2 = (f32[16,80,128]{2,1,0:T(8,128)S(1)}, f32[16,80,128]{2,1,0:T(8,128)}, u32[]{:S(2)}) copy-start(f32[16,80,128]{2,1,0:T(8,128)} %refs_2_.3) | copy-start | bytes 1966084
  7.0 1.1 %copy-start.4 = (f32[16,80,128]{2,1,0:T(8,128)S(1)}, f32[16,80,128]{2,1,0:T(8,128)}, u32[]{:S(2)}) copy-start(f32[16,80,128]{2,1,0:T(8,128)} %refs_3_.3) | copy-start | bytes 1966084
  8.1 0.7 %copy-start.6 = (s32[16,128]{1,0:T(8,128)S(1)}, s32[16,128]{1,0:T(8,128)}, u32[]{:S(2)}) copy-start(s32[16,128]{1,0:T(8,128)} %refs_9_.3) | copy-start | bytes 24580
  8.8 0.7 %copy-start.8 = (f32[16,128]{1,0:T(8,128)S(1)}, f32[16,128]{1,0:T(8,128)}, u32[]{:S(2)}) copy-start(f32[16,128]{1,0:T(8,128)} %refs_7_.3) | copy-start | bytes 24580
  9.5 0.7 %copy-start.10 = (s32[16,128]{1,0:T(8,128)S(1)}, s32[16,128]{1,0:T(8,128)}, u32[]{:S(2)}) copy-start(s32[16,128]{1,0:T(8,128)} %refs_8_.3) | copy-start | bytes 24580
  12.0 3.3 %collective-permute-start = (f32[144,128]{1,0:T(8,128)S(1)}, f32[144,128]{1,0:T(8,128)S(1)}, u32[]{:S(2)}, u32[]{:S(2)}) collective-permute-start(f32[144,128]{1,0:T(8,128)S(1)} %get-tuple-element.9), channel_id=1, source_target_pairs={{0,1},{1,0},{2,3},{3,2},{4,5},{5,4},{6,7},{7,6},{8,9},{9,8},{10,11... | collective-permute-start | bytes 221192 | tf_op jit(solution)/shard_map/ppermute | solution.py:659
  15.3 21.0 %copy-start.1 = (f32[16,80,128]{2,1,0:T(8,128)S(1)}, f32[16,80,128]{2,1,0:T(8,128)}, u32[]{:S(2)}) copy-start(f32[16,80,128]{2,1,0:T(8,128)} %refs_1_.3) | copy-start | bytes 1966084
  15.3 21.0 %copy-start.3 = (f32[16,80,128]{2,1,0:T(8,128)S(1)}, f32[16,80,128]{2,1,0:T(8,128)}, u32[]{:S(2)}) copy-start(f32[16,80,128]{2,1,0:T(8,128)} %refs_2_.3) | copy-start | bytes 1966084
  15.3 21.0 %copy-start.5 = (f32[16,80,128]{2,1,0:T(8,128)S(1)}, f32[16,80,128]{2,1,0:T(8,128)}, u32[]{:S(2)}) copy-start(f32[16,80,128]{2,1,0:T(8,128)} %refs_3_.3) | copy-start | bytes 1966084
  15.3 21.0 %copy-start.7 = (s32[16,128]{1,0:T(8,128)S(1)}, s32[16,128]{1,0:T(8,128)}, u32[]{:S(2)}) copy-start(s32[16,128]{1,0:T(8,128)} %refs_9_.3) | copy-start | bytes 24580
  16.5 25.4 %all-to-all-start = ((f32[16,24,128]{2,1,0:T(8,128)}), f32[16,24,128]{2,1,0:T(8,128)S(1)}, u32[]{:S(2)}, u32[]{:S(2)}) async-start(f32[16,24,128]{2,1,0:T(8,128)} %get-tuple-element.13), calls=%async_computation | async-start | bytes 393216 | tf_op jit(solution)/shard_map/all_to_all | solution.py:685
  24.1 7.4 %collective-permute-start.1 = (f32[512,128]{1,0:T(8,128)}, f32[512,128]{1,0:T(8,128)S(1)}, u32[]{:S(2)}, u32[]{:S(2)}) collective-permute-start(f32[512,128]{1,0:T(8,128)} %get-tuple-element.11), channel_id=1, source_target_pairs={{0,2},{2,4},{4,6},{6,8},{8,10},{10,12},{12,14},{14,16},{16,18},{18... | collective-permute-start | bytes 786440 | tf_op jit(solution)/shard_map/ppermute | solution.py:687
  27.5 14.5 %copy-start.9 = (f32[16,128]{1,0:T(8,128)S(1)}, f32[16,128]{1,0:T(8,128)}, u32[]{:S(2)}) copy-start(f32[16,128]{1,0:T(8,128)} %refs_7_.3) | copy-start | bytes 24580
  27.5 14.5 %copy-start.11 = (s32[16,128]{1,0:T(8,128)S(1)}, s32[16,128]{1,0:T(8,128)}, u32[]{:S(2)}) copy-start(s32[16,128]{1,0:T(8,128)} %refs_8_.3) | copy-start | bytes 24580
  27.5 8.8 %collective-permute-start.2 = (f32[512,128]{1,0:T(8,128)S(1)}, f32[512,128]{1,0:T(8,128)S(1)}, u32[]{:S(2)}, u32[]{:S(2)}) collective-permute-start(f32[512,128]{1,0:T(8,128)S(1)} %get-tuple-element.12), channel_id=1, source_target_pairs={{2,0},{4,2},{6,4},{8,6},{10,8},{12,10},{14,12},{16,14},{18,16},{20... | collective-permute-start | bytes 786440 | tf_op jit(solution)/shard_map/ppermute | solution.py:688

commit v2 on v1

v2 whole, which is shorter than its diff:
```python
import functools

import jax
import jax.numpy as jnp
from jax import lax
from jax.experimental import pallas as pl
from jax.experimental.pallas import tpu as pltpu
from jax.sharding import PartitionSpec as P

PICARD = 2
DIFFUSE = 0.2
GAMMA_MELT = 0.5
TIME_STEP = 0.05
SLOPE_SCALE = 0.1
STRAIN_FLOOR = 0.01
HEATING_RATE = 0.01

LANES = 128
TILE = 8
HALO = 4
RIM = 3
VMEM = pltpu.CompilerParams(vmem_limit_bytes=48 * 1024 * 1024)
HIGHEST = lax.Precision.HIGHEST
F32 = jnp.float32

THICK, GROUNDED, OCEAN_T, WET, ICE_LINK, OCEAN_LINK, OWN_LINK = range(7)
PLANES = 6
PART, EDGE_T0, EDGE_T1, EDGE_W0, PART_WET, EDGE_W1 = range(6)


def iota(shape, axis):
    return lax.broadcasted_iota(jnp.int32, shape, axis)


def right_lanes(period):
    lane = iota((1, LANES), 1)
    return lane % period < HALO


def left_lanes(period):
    lane = iota((1, LANES), 1)
    return lane % period >= period - HALO


def spread(column, count=LANES):
    rows = column.shape[0]
    eye = iota((rows, count), 0) == iota((rows, count), 1)
    return jnp.sum(jnp.where(eye, column, 0.0), axis=0, keepdims=True)


def upright(row):
    count = row.shape[1]
    eye = iota((count, count), 0) == iota((count, count), 1)
    return jnp.sum(jnp.where(eye, row, 0.0), axis=1, keepdims=True)


def turn(value, shift, axis):
    shift %= value.shape[axis]
    return pltpu.roll(value, shift, axis) if shift else value


def fetch_all(pairs, sems):
    copies = [pltpu.make_async_copy(a, b, sems.at[i]) for i, (a, b) in enumerate(pairs)]
    for copy in copies:
        copy.start()
    return copies


def divide(whole, part):
    return jnp.floor((whole + 0.5) * (1.0 / part))


def dot(a, b):
    return jnp.dot(a, b, precision=HIGHEST, preferred_element_type=F32)


def narrow_sides(n_narrow):
    place = lax.axis_index("narrow")
    return place < n_narrow - 1, place > 0


def merged(parts, right, left, n_narrow):
    has_right, has_left = narrow_sides(n_narrow)
    from_right, from_left = parts[0], parts[-1]
    if len(parts) == 1:
        keep = (right & has_right) | (left & has_left)
        return jnp.where(keep, from_right, 0.0)
    return jnp.where(right, from_right, jnp.where(left, from_left, 0.0))


def ice_group(index):
    return divmod(index, LANES // 8)


def edges_kernel(
    ice_x, ice_y, ice_t, ocean_t, thick, grounded, wet, ice_links, ocean_links,
    out, planes, ice, top, thick_v, grounded_v, wet_v, links_v, sems,
):
    layers, rows, _ = ice_x.shape
    copies = fetch_all(
        (
            (thick, thick_v),
            (grounded, grounded_v),
            (wet, wet_v),
            (ice_links, links_v.at[0]),
            (ocean_links, links_v.at[1]),
            (ocean_t.at[:, pl.ds(0, TILE), :], top),
            (ice_x, ice.at[0]),
            (ice_y, ice.at[1]),
            (ice_t, ice.at[2]),
        ),
        sems,
    )
    lane = iota((1, LANES), 1)
    for copy in copies[:6]:
        copy.wait()
    planes[THICK] = thick_v[...]
    planes[GROUNDED] = grounded_v[...].astype(F32)
    for i in range(rows):
        planes[OCEAN_T, i : i + 1, :] = top[i, 0:1, :]
    planes[WET] = wet_v[...].astype(F32)
    for k in range(2):
        link = upright(links_v[k].astype(F32)) + 1.0
        planes[ICE_LINK + k] = jnp.broadcast_to(link, (rows, LANES))
    total = jnp.zeros((rows, LANES), F32)
    for j in range(PLANES):
        total = jnp.where((lane + HALO) % LANES // 16 == j, turn(planes[j], 16 * j, 1), total)
    out[0] = total
    for copy in copies[6:]:
        copy.wait()
    tiles = {}
    for index in range(3 * layers):
        tile, group = ice_group(index)
        turned = turn(ice[index // layers, index % layers], 8 * group, 1)
        before = tiles.get(tile, jnp.zeros((rows, LANES), F32))
        tiles[tile] = jnp.where((lane + HALO) % LANES // 8 == group, turned, before)
    for tile, value in tiles.items():
        out[1 + tile] = value


def plane_halo(block, group):
    lane = iota((1, LANES), 1)
    turned = turn(block, -16 * group, 1)
    return jnp.where((lane < HALO) | (lane >= LANES - HALO), turned, 0.0)


def mix_kernel(
    ocean_x, ocean_y, ocean_t, ice_x, ice_y, ice_t, planes,
    out, strip, up, down, held, ice, ocean_sems, ice_sems,
):
    rows, levels, _ = ocean_x.shape
    layers = ice_x.shape[0]
    chunks = ocean_sems.shape[0] // 3
    step = rows // chunks
    pairs = [
        (field.at[pl.ds(h * step, step)], held.at[f, pl.ds(h * step, step)])
        for f, field in enumerate((ocean_x, ocean_y, ocean_t))
        for h in range(chunks)
    ]
    copies = fetch_all(pairs, ocean_sems)
    ice_copies = fetch_all([(a, ice.at[f]) for f, a in enumerate((ice_x, ice_y, ice_t))], ice_sems)
    lane = iota((1, LANES), 1)
    row = iota((rows, LANES), 0)
    wet = planes[WET]
    around = (
        jnp.where(row > 0, turn(wet, 1, 0), 0.0),
        jnp.where(row < rows - 1, turn(wet, -1, 0), 0.0),
        jnp.where(lane > 0, turn(wet, 1, 1), 0.0),
        jnp.where(lane < LANES - 1, turn(wet, -1, 1), 0.0),
    )
    scale = DIFFUSE * wet
    coef = [scale * value for value in around]
    centre_coef = 1.0 - (coef[0] + coef[1] + coef[2] + coef[3])
    total = jnp.zeros((levels, LANES), F32)
    for f in range(3):
        for h in range(chunks):
            copies[f * chunks + h].wait()
        for i in range(rows):
            j = f * rows + i
            centre = held[f, i]
            total = jnp.where((lane + 1) % LANES // 2 == j, turn(centre, 2 * j, 1), total)
            value = centre * centre_coef[i : i + 1, :]
            value = value + turn(centre, 1, 1) * coef[2][i : i + 1, :]
            value = value + turn(centre, -1, 1) * coef[3][i : i + 1, :]
            if i > 0:
                value = value + held[f, i - 1] * coef[0][i : i + 1, :]
            if i < rows - 1:
                value = value + held[f, i + 1] * coef[1][i : i + 1, :]
            out[f, i] = value
        up[f * levels : (f + 1) * levels, :] = held[f, rows - 1]
        down[f * levels : (f + 1) * levels, :] = held[f, 0]
    strip[...] = total
    for copy in ice_copies:
        copy.wait()
    at = 3 * levels
    upper = iota((TILE, 1), 0) >= HALO
    half = ice_pairs(layers)
    for m in range(half):
        ends = []
        for index in (m, m + half):
            index = min(index, 3 * layers - 1)
            f, k = divmod(index, layers)
            ends.append((ice[f, k, rows - TILE :, :], ice[f, k, :TILE, :]))
        up[at : at + TILE, :] = jnp.where(upper, ends[0][0], turn(ends[1][0], HALO, 0))
        down[at : at + TILE, :] = jnp.where(upper, turn(ends[1][1], HALO, 0), ends[0][1])
        at += TILE
    for j in (THICK, GROUNDED, WET):
        up[at : at + TILE, :] = planes[j, rows - TILE :, :]
        down[at : at + TILE, :] = planes[j, :TILE, :]
        at += TILE


def ice_pairs(layers):
    return -(-3 * layers // 2)


def ranks(own_col, member_col, order_sub, order_lane, own_row):
    hits = (own_col == own_row) & member_col & (order_sub < order_lane)
    return jnp.sum(hits.astype(F32), axis=0, keepdims=True)


def ocean_slots(link_col, rows, n_wide, cap, block):
    link_row = spread(link_col)
    parts = []
    for link in (link_col, link_row):
        number = link - 1.0
        tile = divide(number, rows)
        inner = number - tile * rows
        ok = link > 0.5
        parts.append(
            (
                tile,
                (
                    ok,
                    ok & (inner >= rows - RIM) & (tile < n_wide - 1.5),
                    ok & (inner < RIM) & (tile > 0.5),
                ),
            )
        )
    (tile_col, member_col), (tile_row, member_row) = parts
    order_sub, order_lane = iota((rows, LANES), 0), iota((rows, LANES), 1)
    place = iota((n_wide * block, LANES), 0).astype(F32)
    total = jnp.zeros((n_wide * block, LANES), F32)
    for k, shift in enumerate((0.0, 1.0, -1.0)):
        rank = ranks(tile_col, member_col[k], order_sub, order_lane, tile_row)
        target = jnp.where(
            member_row[k], (tile_row + shift) * block + (k * cap + rank), -1.0
        )
        total = total + (place == target).astype(F32)
    return total[:, :rows]


def draft_slots(link_col, rows, n_wide, cap, block):
    link_row = spread(link_col)
    tile_col, tile_row = divide(link_col - 1.0, rows), divide(link_row - 1.0, rows)
    order_sub, order_lane = iota((rows, LANES), 0), iota((rows, LANES), 1)
    rank = ranks(tile_col, link_col > 0.5, order_sub, order_lane, tile_row)
    target = jnp.where(link_row > 0.5, tile_row * block + (3 * cap + rank), -1.0)
    place = iota((n_wide * block, LANES), 0).astype(F32)
    return (place == target).astype(F32)[:, :rows]


def send_kernel(
    n_wide, n_narrow, cap, block, n_parts, own_rows,
    *refs,
):
    parts, refs = refs[:n_parts], refs[n_parts:]
    planes, up_own, down_own, up, down, blocks = refs
    rows = planes.shape[1]
    lane = iota((1, LANES), 1)
    plane_block = merged([p[0] for p in parts], right_lanes(16), left_lanes(16), n_narrow)
    link_own = planes[ICE_LINK]
    sent_block = jnp.where((lane + HALO) % LANES // 16 == OWN_LINK, link_own, plane_block)
    thick_plane, grounded_plane, wet_plane = planes[THICK], planes[GROUNDED], planes[WET]
    up[0:own_rows, :] = up_own[...]
    down[0:own_rows, :] = down_own[...]
    strips = [
        merged([p[1 + t] for p in parts], right_lanes(8), left_lanes(8), n_narrow)
        for t in range(parts[0].shape[0] - 1)
    ]
    at = own_rows
    for value in (sent_block, *strips):
        up[at : at + TILE, :] = value[rows - TILE :, :]
        down[at : at + TILE, :] = value[:TILE, :]
        at += TILE
    wet_all = jnp.concatenate([wet_plane, plane_halo(plane_block, WET)], axis=1)
    warm = wet_all * jnp.concatenate([planes[OCEAN_T], plane_halo(plane_block, OCEAN_T)], axis=1)
    width = 2 * LANES
    row = iota((rows, width), 0)
    sums = []
    for value in (wet_all, warm):
        total = pltpu.roll(value, 1, 1) + pltpu.roll(value, width - 1, 1)
        total = total + jnp.where(row > 0, pltpu.roll(value, 1, 0), 0.0)
        sums.append(total + jnp.where(row < rows - 1, pltpu.roll(value, rows - 1, 0), 0.0))
    mixed = warm + DIFFUSE * (wet_all * sums[1] - warm * sums[0])
    draft = 0.9 * thick_plane * (1.0 - grounded_plane)
    own_slots = ocean_slots(planes[OCEAN_LINK][:, 0:1], rows, n_wide, cap, block)
    main = dot(own_slots, jnp.concatenate([mixed[:, :LANES], wet_plane], axis=1))
    count = n_wide * block
    slot = iota((count, 1), 0) % block
    first = main[:, :LANES] + dot(draft_slots(link_own[:, 0:1], rows, n_wide, cap, block), draft)
    second = jnp.where(
        slot == 3 * cap,
        wet_plane[0:1, :],
        jnp.where(slot == 3 * cap + 1, wet_plane[rows - 1 : rows, :], main[:, LANES:]),
    )
    edge = (lane < HALO) | (lane >= LANES - HALO)
    mixed_edge = jnp.where(edge, mixed[:, LANES:], 0.0)
    wet_edge = wet_all[:, LANES:]
    warm_edge = warm[:, LANES:]
    packed = mixed_edge + pltpu.roll(wet_edge, 16 * PART_WET, 1)
    links = plane_halo(plane_block, OCEAN_LINK)
    if n_narrow == 2:
        third = dot(
            ocean_slots(jnp.max(links, axis=1, keepdims=True), rows, n_wide, cap, block), packed
        )
    else:
        third = dot(
            ocean_slots(links[:, 0:1], rows, n_wide, cap, block),
            jnp.where(right_lanes(16), packed, 0.0),
        ) + dot(
            ocean_slots(links[:, LANES - 1 : LANES], rows, n_wide, cap, block),
            jnp.where(left_lanes(16), packed, 0.0),
        )
    last = rows - 1
    ends = (
        pltpu.roll(warm_edge[0:1, :], 16 * EDGE_T0, 1)
        + pltpu.roll(warm_edge[last:, :], 16 * EDGE_T1, 1)
        + pltpu.roll(wet_edge[0:1, :], 16 * EDGE_W0, 1)
        + pltpu.roll(wet_edge[last:, :], 16 * EDGE_W1, 1)
    )
    third = jnp.where(
        slot == 3 * cap,
        warm[0:1, :LANES],
        jnp.where(slot == 3 * cap + 1, warm[last:, :LANES], third + ends),
    )
    for k, value in enumerate((first, second, third)):
        blocks[:, k * block : (k + 1) * block, :] = value.reshape(n_wide, block, LANES)


def patch_kernel(
    n_narrow, n_strips, n_parts,
    *refs,
):
    strips, refs = refs[:n_strips], refs[n_strips:]
    parts, refs = refs[:n_parts], refs[n_parts:]
    mixed, own, up_own, down_own, up, down, planes, out, held, sems = refs
    _, rows, levels, _ = mixed.shape
    chunks = sems.shape[0] // 3
    step = rows // chunks
    lane = iota((1, LANES), 1)
    first, last = lane == 0, lane == LANES - 1
    wet = planes[WET]
    wet_at = up_own.shape[0] - TILE
    block = merged([p[0] for p in parts], right_lanes(16), left_lanes(16), n_narrow)
    wet_halo = plane_halo(block, WET)
    weight = DIFFUSE * wet * jnp.where(first, turn(wet_halo, 1, 1), turn(wet_halo, -1, 1))
    weight = jnp.where(first | last, weight, 0.0)
    even = lane % 2 == 0
    packed_weight = jnp.zeros((1, LANES), F32)
    for j in range(3 * rows):
        i = j % rows
        packed_weight = packed_weight + turn(weight[i : i + 1, :], 2 * j, 1)
    came = merged([p[...] for p in strips], even, ~even, n_narrow)
    extra = packed_weight * (jnp.where(even, turn(came, 1, 1), turn(came, -1, 1)) - own[...])
    above = DIFFUSE * wet[0:1, :] * up[wet_at + TILE - 1 : wet_at + TILE, :]
    below = DIFFUSE * wet[rows - 1 : rows, :] * down[wet_at : wet_at + 1, :]
    edge = first | last
    writes = []
    for f in range(3):
        for h in range(chunks):
            for i in range(h * step, (h + 1) * step):
                value = mixed[f, i] + jnp.where(edge, turn(extra, -2 * (f * rows + i), 1), 0.0)
                part = pl.ds(f * levels, levels)
                if i == 0:
                    value = value + above * (up[part, :] - down_own[part, :])
                if i == rows - 1:
                    value = value + below * (down[part, :] - up_own[part, :])
                held[f, i] = value
            part = pl.ds(h * step, step)
            writes.append(
                pltpu.make_async_copy(
                    held.at[f, part], out.at[f, part], sems.at[f * chunks + h]
                )
            )
            writes[-1].start()
    for copy in writes:
        copy.wait()


def ice_slots(link_col, kind_col, rows, cap, block, count, n_wide):
    link_row = spread(link_col)
    kind_row = spread(kind_col)
    number = link_col - 1.0
    tile = divide(number, rows)
    inner = number - tile * rows
    tile_row = divide(link_row - 1.0, rows)
    ok = (link_col > 0.5) & (kind_col > -0.5)
    ok_row = (link_row > 0.5) & (kind_row > -0.5)
    hits = (tile == tile_row) & (kind_col == kind_row) & ok_row & (link_row < link_col)
    rank = jnp.sum(hits.astype(F32), axis=1, keepdims=True)
    place = iota((link_col.shape[0], count), 1).astype(F32)

    def hot(keep, target):
        return (place == jnp.where(keep, target, -1.0)).astype(F32)

    top, bottom = inner < 0.5, inner > rows - 1.5
    edge = ok & (top | bottom)
    near = jnp.where(top, tile - 1.0, tile + 1.0)
    near_ok = edge & (near > -0.5) & (near < n_wide - 0.5)
    slot = hot(ok, tile * block + kind_col * cap + rank)
    near_edge = hot(near_ok, near * block + jnp.where(top, 3.0 * cap + 1.0, 3.0 * cap))
    own_edge = hot(edge, tile * block + jnp.where(top, 3.0 * cap, 3.0 * cap + 1.0))
    near_slot = hot(near_ok, near * block)
    own_slot = hot(edge, tile * block)
    return slot, near_edge, own_edge, near_slot, own_slot, top


def final_kernel(
    n_wide, n_narrow, cap, block, n_parts, levels, own_rows,
    *refs,
):
    parts, refs = refs[:n_parts], refs[n_parts:]
    (
        ice_x, ice_y, ice_t, up, down, blocks, planes, ocean_in,
        ice_out, ocean_out, thick_out, melt_out,
        ice, vel, rate, flat, top_level, sems,
    ) = refs
    layers, rows, _ = ice_x.shape
    copies = fetch_all(
        (
            (ocean_in.at[2, :, pl.ds(0, TILE), :], top_level),
            (ice_x, ice.at[0]),
            (ice_y, ice.at[1]),
            (ice_t, ice.at[2]),
        ),
        sems,
    )
    width = 2 * LANES
    tall = rows + TILE
    lane = iota((1, LANES), 1)
    wide_lane = iota((1, width), 1)
    place_wide = lax.axis_index("wide")
    has_right, has_left = narrow_sides(n_narrow)
    has_up, has_down = place_wide > 0, place_wide < n_wide - 1
    under = iota((TILE, 1), 0) < HALO
    ice_at = 3 * levels
    plane_at = own_rows - 3 * TILE

    def rim(at):
        part = pl.ds(at, TILE)
        return jnp.where(under, down[part, :], up[part, :])

    def extended(value, at):
        return jnp.concatenate([value, rim(at)], axis=0)

    plane_block = merged([p[0] for p in parts], right_lanes(16), left_lanes(16), n_narrow)
    block_tall = extended(plane_block, own_rows)
    thick_tall = jnp.concatenate(
        [extended(planes[THICK], plane_at), plane_halo(block_tall, THICK)], axis=1
    )
    grounded_tall = jnp.concatenate(
        [extended(planes[GROUNDED], plane_at + TILE), plane_halo(block_tall, GROUNDED)], axis=1
    )
    tall_row = iota((tall, 1), 0)
    kind = jnp.where(
        tall_row < rows,
        0.0,
        jnp.where(tall_row < rows + RIM, 2.0, jnp.where(tall_row >= tall - RIM, 1.0, -1.0)),
    )
    count = n_wide * block
    first = blocks[:, 0:block, :].reshape(count, LANES)
    second = blocks[:, block : 2 * block, :].reshape(count, LANES)
    third = blocks[:, 2 * block : 3 * block, :].reshape(count, LANES)
    own_link = jnp.concatenate(
        [
            planes[ICE_LINK][:, 0:1],
            rim(own_rows)[:, 16 * OWN_LINK : 16 * OWN_LINK + 1],
        ],
        axis=0,
    )
    slot, near_edge, own_edge, _, _, _ = ice_slots(
        own_link, kind, rows, cap, block, count, n_wide
    )
    got = dot(slot, jnp.concatenate([first, second], axis=1))
    near = dot(near_edge, jnp.concatenate([second, third], axis=1))
    own = dot(own_edge, third)
    wet_main = got[:, LANES:]
    mixed_main = got[:, :LANES] + DIFFUSE * (
        wet_main * near[:, LANES:] - near[:, :LANES] * own
    )

    def halo_melt(link_col):
        slot, _, _, near_slot, own_slot, top = ice_slots(
            link_col, kind, rows, cap, block, count, n_wide
        )
        got = dot(slot, third)
        near = dot(near_slot, third)
        own = dot(own_slot, third)

        def group(value, j):
            return pltpu.roll(value, LANES - 16 * j, 1) if j else value

        wet_got = group(got, PART_WET)
        near_warm = jnp.where(top, group(near, EDGE_T1), group(near, EDGE_T0))
        near_wet = jnp.where(top, group(near, EDGE_W1), group(near, EDGE_W0))
        own_warm = jnp.where(top, group(own, EDGE_T0), group(own, EDGE_T1))
        return got + DIFFUSE * (wet_got * near_warm - near_wet * own_warm), wet_got

    links = plane_halo(block_tall, ICE_LINK)
    if n_narrow == 2:
        mixed_side, wet_side = halo_melt(jnp.max(links, axis=1, keepdims=True))
    else:
        mixed_side, wet_side = (
            jnp.where(lane < HALO, a, b)
            for a, b in zip(halo_melt(links[:, 0:1]), halo_melt(links[:, LANES - 1 : LANES]))
        )
    mixed_tall = jnp.concatenate([mixed_main, mixed_side], axis=1)
    wet_tall = jnp.concatenate([wet_main, wet_side], axis=1)
    inside = (
        ((tall_row < rows) | ((tall_row < rows + HALO) & has_down) | ((tall_row >= rows + HALO) & has_up))
        & (
            (wide_lane < LANES)
            | ((wide_lane < LANES + HALO) & has_right)
            | ((wide_lane >= width - HALO) & has_left)
        )
    ).astype(F32)
    open_ice = 1.0 - grounded_tall
    draft_tall = 0.9 * thick_tall * open_ice
    melt_tall = GAMMA_MELT * (mixed_tall - wet_tall * (0.0832 - 0.761 * draft_tall))
    new_thick = (thick_tall - TIME_STEP * melt_tall * open_ice) * inside
    thick_out[...] = new_thick[:rows, :LANES]
    surface = new_thick * (0.1 + 0.9 * grounded_tall)
    push_scale = (-0.5 * SLOPE_SCALE) * new_thick
    flat[0] = push_scale * (turn(surface, -1, 0) - turn(surface, 1, 0))
    flat[1] = push_scale * (turn(surface, -1, 1) - turn(surface, 1, 1))
    flat[2] = 0.1 + 9.9 * grounded_tall
    flat[3] = inside
    ocean_link = planes[OCEAN_LINK][:, 0:1]
    ocean_row = spread(ocean_link)
    tile = divide(ocean_link - 1.0, rows)
    tile_row = divide(ocean_row - 1.0, rows)
    hits = (tile == tile_row) & (ocean_row > 0.5) & (ocean_row < ocean_link)
    rank = jnp.sum(hits.astype(F32), axis=1, keepdims=True)
    coupled = ocean_link > 0.5
    target = jnp.where(coupled, tile * block + 3 * cap + rank, -1.0)
    ocean_draft = dot((iota((rows, count), 1).astype(F32) == target).astype(F32), first)
    copies[0].wait()
    heat_top = jnp.concatenate([top_level[i, 0:1, :] for i in range(rows)], axis=0)
    melt = (
        GAMMA_MELT
        * (heat_top - (0.0832 - 0.761 * ocean_draft))
        * planes[WET]
        * coupled.astype(F32)
    )
    melt_out[...] = melt
    new_top = heat_top - 0.2 * melt
    for i in range(rows):
        top_level[i, 0:1, :] = new_top[i : i + 1, :]
    store = pltpu.make_async_copy(top_level, ocean_out.at[2, :, pl.ds(0, TILE), :], sems.at[4])
    store.start()
    strips = [
        extended(
            merged([p[1 + t] for p in parts], right_lanes(8), left_lanes(8), n_narrow),
            own_rows + (1 + t) * TILE,
        )
        for t in range(parts[0].shape[0] - 1)
    ]
    edge = (lane < HALO) | (lane >= LANES - HALO)
    half = ice_pairs(layers)
    for copy in copies[1:]:
        copy.wait()
    for index in range(3 * layers):
        f, k = divmod(index, layers)
        beyond = rim(ice_at + index % half * TILE)
        if index >= half:
            part = pl.ds(ice_at + index % half * TILE, TILE)
            beyond = turn(jnp.where(under, up[part, :], down[part, :]), HALO, 0)
        tile, group = ice_group(index)
        beside = jnp.where(edge, turn(strips[tile], -8 * group, 1), 0.0)
        value = jnp.concatenate(
            [jnp.concatenate([ice[f, k], beyond], axis=0), beside], axis=1
        )
        if f < 2:
            vel[f, k] = value
        else:
            rate[k] = jnp.exp(0.25 * value) * inside

    def around(value):
        return turn(value, 1, 0) + turn(value, -1, 0) + turn(value, 1, 1) + turn(value, -1, 1)

    for sweep in range(PICARD):
        last = sweep == PICARD - 1
        for k in range(layers):
            u, v = vel[2 * sweep, k], vel[2 * sweep + 1, k]
            ends = [
                [turn(w, s, axis) for axis in (0, 1) for s in (-1, 1)] for w in (u, v)
            ]
            ux, uy = ends[0][0] - ends[0][1], ends[0][2] - ends[0][3]
            vx, vy = ends[1][0] - ends[1][1], ends[1][2] - ends[1][3]
            cross = uy + vx
            eps2 = ux * (ux + vy) + vy * vy + 0.25 * (cross * cross)
            if k < layers - 1:
                uz, vz = vel[2 * sweep, k + 1] - u, vel[2 * sweep + 1, k + 1] - v
                eps2 = eps2 + (uz * uz + vz * vz)
            eps2 = 0.25 * eps2
            eta = rate[k] * jnp.exp((-1.0 / 3.0) * jnp.log(eps2 + STRAIN_FLOOR))
            links_up_down = float((k > 0) + (k < layers - 1))
            diagonal = eta * (2.0 + links_up_down) + 0.5 * around(eta) + flat[2]
            if last:
                diagonal = diagonal[:rows, :LANES]
            inverse = 1.0 / diagonal
            for f, w in enumerate((u, v)):
                total = 0.5 * (ends[f][0] + ends[f][1] + ends[f][2] + ends[f][3])
                if k > 0:
                    total = total + vel[2 * sweep + f, k - 1]
                if k < layers - 1:
                    total = total + vel[2 * sweep + f, k + 1]
                total = eta * total + 0.5 * around(eta * w) + flat[f]
                if last:
                    ice_out[f, k] = total[:rows, :LANES] * inverse
                else:
                    vel[2 * sweep + 2 + f, k] = total * inverse * flat[3]
            if last:
                ice_out[2, k] = ice[2, k] + HEATING_RATE * (eta * eps2)[:rows, :LANES]
    store.wait()


def local(
    ice_x, ice_y, ice_temp, ocean_x, ocean_y, ocean_temp, thick, grounded_mask, wet_mask, ice_links, ocean_links,
):
    n_wide, n_narrow = lax.axis_size("wide"), lax.axis_size("narrow")
    rows, layers, columns = ice_x.shape
    levels = ocean_x.shape[1]
    cap = max(1, 2 * rows // n_wide)
    block = -(-max(4 * cap, 3 * cap + 2) // TILE) * TILE
    assert columns == LANES and ice_links.shape[0] == rows
    ice_fields = [x.transpose(1, 0, 2) for x in (ice_x, ice_y, ice_temp)]
    links = [x.reshape(1, rows) for x in (ice_links, ocean_links)]
    fields = [ocean_x, ocean_y, ocean_temp]
    here = pl.BlockSpec(memory_space=pltpu.VMEM)
    far = pl.BlockSpec(memory_space=pltpu.HBM)

    def array(*shape):
        return jax.ShapeDtypeStruct(shape, F32)

    def cost(microseconds):
        return pl.CostEstimate(
            flops=0, bytes_accessed=int(microseconds * 3.0e6), transcendentals=0
        )

    n_tiles = ice_group(3 * layers - 1)[0] + 1
    dma = pltpu.SemaphoreType.DMA
    message, planes = pl.pallas_call(
        edges_kernel,
        name="edges",
        out_shape=(array(1 + n_tiles, rows, LANES), array(PLANES, rows, LANES)),
        in_specs=[far] * 9,
        out_specs=(here, here),
        scratch_shapes=[
            pltpu.VMEM((3, layers, rows, LANES), F32),
            pltpu.VMEM((rows, TILE, LANES), F32),
            pltpu.VMEM((rows, LANES), F32),
            pltpu.VMEM((rows, LANES), jnp.int32),
            pltpu.VMEM((rows, LANES), jnp.int32),
            pltpu.VMEM((2, 1, rows), jnp.int32),
            dma((9,)),
        ],
        compiler_params=VMEM,
        cost_estimate=cost(1.5),
    )(*ice_fields, ocean_temp, thick, grounded_mask, wet_mask, *links)

    def narrow(value):
        if n_narrow == 2:
            return [lax.ppermute(value, "narrow", [(0, 1), (1, 0)])]
        ahead = [(i, i + 1) for i in range(n_narrow - 1)]
        return [
            lax.ppermute(value, "narrow", [(j, i) for i, j in ahead]),
            lax.ppermute(value, "narrow", ahead),
        ]

    parts = narrow(message)
    n_parts = len(parts)
    own_rows = 3 * levels + ice_pairs(layers) * TILE + 3 * TILE
    chunks = 2
    mixed, own_strip, up_own, down_own = pl.pallas_call(
        mix_kernel,
        name="mix",
        out_shape=(
            array(3, rows, levels, LANES), array(levels, LANES), array(own_rows, LANES), array(own_rows, LANES),
        ),
        in_specs=[far] * 6 + [here],
        out_specs=(here,) * 4,
        scratch_shapes=[
            pltpu.VMEM((3, rows, levels, LANES), F32),
            pltpu.VMEM((3, layers, rows, LANES), F32),
            dma((3 * chunks,)),
            dma((3,)),
        ],
        compiler_params=VMEM,
        cost_estimate=cost(3.0),
    )(*fields, *ice_fields, planes)
    total_rows = own_rows + (1 + n_tiles) * TILE
    to_down, to_up, blocks = pl.pallas_call(
        functools.partial(send_kernel, n_wide, n_narrow, cap, block, n_parts, own_rows),
        name="send",
        out_shape=(
            array(total_rows, LANES), array(total_rows, LANES), array(n_wide, 3 * block, LANES),
        ),
        in_specs=[here] * (n_parts + 3),
        out_specs=(here,) * 3,
        compiler_params=VMEM,
        cost_estimate=cost(1.3),
    )(*parts, planes, up_own, down_own)
    blocks = lax.all_to_all(blocks, "wide", split_axis=0, concat_axis=0, tiled=True)
    ahead = [(i, i + 1) for i in range(n_wide - 1)]
    up = lax.ppermute(to_down, "wide", ahead)
    down = lax.ppermute(to_up, "wide", [(j, i) for i, j in ahead])
    strips = narrow(own_strip)
    ocean = pl.pallas_call(
        functools.partial(patch_kernel, n_narrow, len(strips), n_parts),
        name="patch",
        out_shape=array(3, rows, levels, LANES),
        in_specs=[here] * (len(strips) + n_parts + 7),
        out_specs=far,
        scratch_shapes=[
            pltpu.VMEM((3, rows, levels, LANES), F32),
            dma((3 * chunks,)),
        ],
        compiler_params=VMEM,
        cost_estimate=cost(2.0),
    )(*strips, *parts, mixed, own_strip, up_own, down_own, up, down, planes)
    wide = 2 * LANES
    tall = rows + TILE
    ice, ocean, thick_out, melt_out = pl.pallas_call(
        functools.partial(
            final_kernel, n_wide, n_narrow, cap, block, n_parts, levels, own_rows
        ),
        name="final",
        out_shape=(
            array(3, layers, rows, LANES), array(3, rows, levels, LANES), array(rows, LANES), array(rows, LANES),
        ),
        in_specs=[here] * n_parts + [far] * 3 + [here] * 4 + [far],
        out_specs=(here, far, here, here),
        input_output_aliases={n_parts + 7: 1},
        scratch_shapes=[
            pltpu.VMEM((3, layers, rows, LANES), F32),
            pltpu.VMEM((2 * PICARD, layers, tall, wide), F32),
            pltpu.VMEM((layers, tall, wide), F32),
            pltpu.VMEM((4, tall, wide), F32),
            pltpu.VMEM((rows, TILE, LANES), F32),
            dma((5,)),
        ],
        compiler_params=VMEM,
        cost_estimate=cost(7.0),
    )(*parts, *ice_fields, up, down, blocks, planes, ocean)
    return ice.transpose(0, 2, 1, 3), ocean, thick_out, melt_out


def solution(mesh):
    column = P("wide", None, "narrow")
    plane = P("wide", "narrow")
    return jax.shard_map(
        local,
        mesh=mesh,
        in_specs=(column,) * 6 + (plane,) * 5,
        out_specs=(P(None, "wide", None, "narrow"), P(None, "wide", None, "narrow"), plane, plane),
        check_vma=False,
    )
```

time: 53.6 us -> 41.8 us (0.78)
  the two profiles are of different devices: /device:TPU:17 before, /device:TPU:3 now
where the time goes in v2:
time: 41.8 us; the launch traced here: 41.2 us
  starting transfers between devices  13.8 us (33%)
  Pallas kernels  11.5 us (28%)
  local copies, waits for them, and re-layouts  9.32 us (22%)
  waiting for transfers between devices  5.8 us (14%)
  between operations  0.74 us (2%)
    unnamed x28, local copies, waits for them, and re-layouts  9.32 us
    all_to_all x1, starting transfers between devices, local(): lax.all_to_all(blocks, 'wide', split_axis=0, concat_axis=0, tiled=True)  6.95 us
    pallas_call x1, Pallas kernels, local(): pl.pallas_call(functools.partial(final_kernel, n_wide, n_narrow, cap, blo...  5.07 us
    ppermute x1, starting transfers between devices, local(): up = lax.ppermute(to_down, 'wide', ahead)  3.33 us
    ppermute x1, waiting for transfers between devices, local(): down = lax.ppermute(to_up, 'wide', [(j, i) for i, j in ahead])  3.17 us
    pallas_call x1, Pallas kernels, local(): pl.pallas_call(mix_kernel, name='mix', out_shape=(array(3, rows, levels,...  2.83 us
    ppermute x2, waiting for transfers between devices, narrow(): return [lax.ppermute(value, 'narrow', [(0, 1), (1, 0)])]  2.63 us
    ppermute x1, starting transfers between devices, local(): down = lax.ppermute(to_up, 'wide', [(j, i) for i, j in ahead])  1.92 us
  transfers between devices with their start and end apart: 5, of which 2 were waited for; matrix products, arithmetic and copies ran while one was open for 0% of the time, Pallas kernels for 11%

profile of v2, /device:TPU:3, one launch (start us, length us, event | category | flops | bytes accessed | tf_op | source)
XLA Modules:
  0.0 41.2 jit_solution(13282851190463232324)
XLA Ops:
  0.6 1.1 %copy-done = f32[16,80,128]{2,1,0:T(8,128)S(1)} copy-done((f32[16,80,128]{2,1,0:T(8,128)S(1)}, f32[16,80,128]{2,1,0:T(8,128)}, u32[]{:S(2)}) %copy-start) | copy-done | bytes 655384
  1.7 0.9 %copy-done.1 = f32[16,10,128]{2,0,1:T(8,128)S(1)} copy-done((f32[16,10,128]{2,0,1:T(8,128)S(1)}, f32[16,10,128]{2,0,1:T(8,128)}, u32[]{:S(2)}) %copy-start.1) | copy-done | bytes 81944
  2.6 0.9 %copy-done.3 = f32[16,10,128]{2,0,1:T(8,128)S(1)} copy-done((f32[16,10,128]{2,0,1:T(8,128)S(1)}, f32[16,10,128]{2,0,1:T(8,128)}, u32[]{:S(2)}) %copy-start.3) | copy-done | bytes 81944
  3.5 0.9 %copy-done.5 = f32[16,10,128]{2,0,1:T(8,128)S(1)} copy-done((f32[16,10,128]{2,0,1:T(8,128)S(1)}, f32[16,10,128]{2,0,1:T(8,128)}, u32[]{:S(2)}) %copy-start.5) | copy-done | bytes 81944
  4.4 0.7 %copy-done.9 = f32[16,128]{1,0:T(8,128)S(1)} copy-done((f32[16,128]{1,0:T(8,128)S(1)}, f32[16,128]{1,0:T(8,128)}, u32[]{:S(2)}) %copy-start.9) | copy-done | bytes 8216
  5.1 0.7 %copy-done.10 = s32[16,128]{1,0:T(8,128)S(1)} copy-done((s32[16,128]{1,0:T(8,128)S(1)}, s32[16,128]{1,0:T(8,128)}, u32[]{:S(2)}) %copy-start.10) | copy-done | bytes 8216
  5.8 0.7 %copy-done.11 = s32[16,128]{1,0:T(8,128)S(1)} copy-done((s32[16,128]{1,0:T(8,128)S(1)}, s32[16,128]{1,0:T(8,128)}, u32[]{:S(2)}) %copy-start.11) | copy-done | bytes 8216
  6.5 0.7 %copy-done.12 = s32[16,1]{0,1:T(1,128)S(1)} copy-done((s32[16,1]{0,1:T(1,128)S(1)}, s32[16,1]{0,1:T(1,128)}, u32[]{:S(2)}) %copy-start.12) | copy-done | bytes 88
  7.1 0.7 %copy-done.13 = s32[16,1]{0,1:T(1,128)S(1)} copy-done((s32[16,1]{0,1:T(1,128)S(1)}, s32[16,1]{0,1:T(1,128)}, u32[]{:S(2)}) %copy-start.13) | copy-done | bytes 88
  7.8 0.7 %edges.1 = (f32[3,16,128]{2,1,0:T(8,128)S(1)}, f32[6,16,128]{2,1,0:T(8,128)S(1)}) custom-call(f32[10,16,128]{2,1,0:T(8,128)S(1)} %bitcast.6, f32[10,16,128]{2,1,0:T(8,128)S(1)} %bitcast.9, f32[10,16,128]{2,1,0:T(8,128)S(1)} %bitcast.12, f32[16,80,128]{2,1,0:T(8,128)S(1)} %copy-done, f32[16,128]{1,0:T(8,128)S(1)} %copy-done.9, s32[16,128]{1,0:T(8,128)S(1)} %copy-done.10, ...), custom_call_target="tpu_custom_call" | custom-call | bytes 4500000 | tf_op jit(solution)/shard_map/edges/pallas_call | solution.py:654
  8.5 1.3 %collective-permute-start = (f32[3,16,128]{2,1,0:T(8,128)S(1)}, f32[3,16,128]{2,1,0:T(8,128)S(1)}, u32[]{:S(2)}, u32[]{:S(2)}) collective-permute-start(f32[3,16,128]{2,1,0:T(8,128)S(1)} %get-tuple-element.17), channel_id=1, source_target_pairs={{0,1},{1,0},{2,3},{3,2},{4,5},{5,4},{6,7},{7,6},{8,9},{9,8},{10,11... | collective-permute-start | bytes 73736 | tf_op jit(solution)/shard_map/ppermute | solution.py:675
  9.8 1.1 %copy-done.7 = f32[16,80,128]{2,1,0:T(8,128)S(1)} copy-done((f32[16,80,128]{2,1,0:T(8,128)S(1)}, f32[16,80,128]{2,1,0:T(8,128)}, u32[]{:S(2)}) %copy-start.7) | copy-done | bytes 655384
  10.9 1.1 %copy-done.8 = f32[16,80,128]{2,1,0:T(8,128)S(1)} copy-done((f32[16,80,128]{2,1,0:T(8,128)S(1)}, f32[16,80,128]{2,1,0:T(8,128)}, u32[]{:S(2)}) %copy-start.8) | copy-done | bytes 655384
  12.0 2.8 %mix.1 = (f32[3,16,80,128]{3,2,1,0:T(8,128)S(1)}, f32[80,128]{1,0:T(8,128)S(1)}, f32[384,128]{1,0:T(8,128)S(1)}, f32[384,128]{1,0:T(8,128)S(1)}) custom-call(f32[16,80,128]{2,1,0:T(8,128)S(1)} %copy-done.7, f32[16,80,128]{2,1,0:T(8,128)S(1)} %copy-done.8, f32[16,80,128]{2,1,0:T(8,128)S(1)} %copy-done, f32[10,16,128]{2,1,0:T(8,128)S(1)} %bitcast.7, ...), custom_call_target="tpu_custom_call" | custom-call | bytes 9000000 | tf_op jit(solution)/shard_map/mix/pallas_call | solution.py:686
  14.8 1.2 %send.1 = (f32[408,128]{1,0:T(8,128)S(1)}, f32[408,128]{1,0:T(8,128)S(1)}, f32[16,24,128]{2,1,0:T(8,128)}) custom-call(f32[3,16,128]{2,1,0:T(8,128)S(1)} %collective-permute-done.refs_0_.refs_1_, f32[6,16,128]{2,1,0:T(8,128)S(1)} %get-tuple-element.18.planes.refs_1_.refs_8_.refs_7_, f32[384,128]{1,0:T(8,128)S(1)} %get-tuple-element.19.refs_2_.refs_4_, ...), custom_call_target="tpu_custom_call" | custom-call | bytes 3900000 | tf_op jit(solution)/shard_map/send/pallas_call | solution.py:704
  16.0 6.9 %all-to-all-start = ((f32[16,24,128]{2,1,0:T(8,128)}), f32[16,24,128]{2,1,0:T(8,128)S(1)}, u32[]{:S(2)}, u32[]{:S(2)}) async-start(f32[16,24,128]{2,1,0:T(8,128)} %get-tuple-element.23), calls=%async_computation | async-start | bytes 393216 | tf_op jit(solution)/shard_map/all_to_all | solution.py:715
  23.0 3.3 %collective-permute-start.1 = (f32[408,128]{1,0:T(8,128)S(1)}, f32[408,128]{1,0:T(8,128)S(1)}, u32[]{:S(2)}, u32[]{:S(2)}) collective-permute-start(f32[408,128]{1,0:T(8,128)S(1)} %get-tuple-element.21), channel_id=1, source_target_pairs={{0,2},{2,4},{4,6},{6,8},{8,10},{10,12},{12,14},{14,16},{16,18},{18... | collective-permute-start | bytes 626696 | tf_op jit(solution)/shard_map/ppermute | solution.py:717
  26.3 1.9 %collective-permute-start.2 = (f32[408,128]{1,0:T(8,128)S(1)}, f32[408,128]{1,0:T(8,128)S(1)}, u32[]{:S(2)}, u32[]{:S(2)}) collective-permute-start(f32[408,128]{1,0:T(8,128)S(1)} %get-tuple-element.22), channel_id=1, source_target_pairs={{2,0},{4,2},{6,4},{8,6},{10,8},{12,10},{14,12},{16,14},{18,16},{20... | collective-permute-start | bytes 626696 | tf_op jit(solution)/shard_map/ppermute | solution.py:718
  28.2 0.3 collective-permute-start.3
  28.5 2.6 %collective-permute-done.3.refs_0_ = f32[80,128]{1,0:T(8,128)S(1)} collective-permute-done((f32[80,128]{1,0:T(8,128)S(1)}, f32[80,128]{1,0:T(8,128)S(1)}, u32[]{:S(2)}, u32[]{:S(2)}) %collective-permute-start.3) | collective-permute-done | bytes 40992 | tf_op jit(solution)/shard_map/ppermute | solution.py:675
  31.1 0.0 collective-permute-done.1.refs_6_.refs_4_
  31.1 3.2 %collective-permute-done.2.refs_7_.refs_5_ = f32[408,128]{1,0:T(8,128)S(1)} collective-permute-done((f32[408,128]{1,0:T(8,128)S(1)}, f32[408,128]{1,0:T(8,128)S(1)}, u32[]{:S(2)}, u32[]{:S(2)}) %collective-permute-start.2) | collective-permute-done | bytes 208928 | tf_op jit(solution)/shard_map/ppermute | solution.py:718
  34.3 1.7 %patch.1.refs_8_ = f32[3,16,80,128]{3,2,1,0:T(8,128)} custom-call(f32[80,128]{1,0:T(8,128)S(1)} %collective-permute-done.3.refs_0_, f32[3,16,128]{2,1,0:T(8,128)S(1)} %collective-permute-done.refs_0_.refs_1_, f32[3,16,80,128]{3,2,1,0:T(8,128)S(1)} %get-tuple-element.25.refs_2_, f32[80,128]{1,0:T(8,128)S(1)} %get-tuple-element.24.refs_3_, ...), custom_call_target="tpu_custom_call" | custom-call | bytes 6000000 | tf_op jit(solution)/shard_map/patch/pallas_call | solution.py:720
  36.1 5.1 %final.1 = (f32[3,10,16,128]{3,2,1,0:T(8,128)}, f32[3,16,80,128]{3,2,1,0:T(8,128)}, f32[16,128]{1,0:T(8,128)}, f32[16,128]{1,0:T(8,128)}) custom-call(f32[3,16,128]{2,1,0:T(8,128)S(1)} %collective-permute-done.refs_0_.refs_1_, f32[10,16,128]{2,1,0:T(8,128)S(1)} %bitcast.8, f32[10,16,128]{2,1,0:T(8,128)S(1)} %bitcast.11, ...), custom_call_target="tpu_custom_call", output_to_operand_aliasing={{1}: (8, {})} | custom-call | bytes 21000000 | tf_op jit(solution)/shard_map/final/pallas_call | solution.py:735
  (19 shorter events, 0.0 us)
Async XLA Ops:
  0.6 1.1 %copy-start = (f32[16,80,128]{2,1,0:T(8,128)S(1)}, f32[16,80,128]{2,1,0:T(8,128)}, u32[]{:S(2)}) copy-start(f32[16,80,128]{2,1,0:T(8,128)} %ocean_t.3) | copy-start | bytes 1966084
  1.7 0.9 %copy-start.1 = (f32[16,10,128]{2,0,1:T(8,128)S(1)}, f32[16,10,128]{2,0,1:T(8,128)}, u32[]{:S(2)}) copy-start(f32[16,10,128]{2,0,1:T(8,128)} %param.11) | copy-start | bytes 245764
  2.6 0.9 %copy-start.3 = (f32[16,10,128]{2,0,1:T(8,128)S(1)}, f32[16,10,128]{2,0,1:T(8,128)}, u32[]{:S(2)}) copy-start(f32[16,10,128]{2,0,1:T(8,128)} %param.12) | copy-start | bytes 245764
  3.5 0.9 %copy-start.5 = (f32[16,10,128]{2,0,1:T(8,128)S(1)}, f32[16,10,128]{2,0,1:T(8,128)}, u32[]{:S(2)}) copy-start(f32[16,10,128]{2,0,1:T(8,128)} %param.13) | copy-start | bytes 245764
  4.4 0.7 %copy-start.9 = (f32[16,128]{1,0:T(8,128)S(1)}, f32[16,128]{1,0:T(8,128)}, u32[]{:S(2)}) copy-start(f32[16,128]{1,0:T(8,128)} %thick.1) | copy-start | bytes 24580
  5.1 0.7 %copy-start.10 = (s32[16,128]{1,0:T(8,128)S(1)}, s32[16,128]{1,0:T(8,128)}, u32[]{:S(2)}) copy-start(s32[16,128]{1,0:T(8,128)} %grounded.1) | copy-start | bytes 24580
  5.8 0.7 %copy-start.11 = (s32[16,128]{1,0:T(8,128)S(1)}, s32[16,128]{1,0:T(8,128)}, u32[]{:S(2)}) copy-start(s32[16,128]{1,0:T(8,128)} %wet.1) | copy-start | bytes 24580
  6.5 0.7 %copy-start.12 = (s32[16,1]{0,1:T(1,128)S(1)}, s32[16,1]{0,1:T(1,128)}, u32[]{:S(2)}) copy-start(s32[16,1]{0,1:T(1,128)} %param.20) | copy-start | bytes 196
  7.1 0.7 %copy-start.13 = (s32[16,1]{0,1:T(1,128)S(1)}, s32[16,1]{0,1:T(1,128)}, u32[]{:S(2)}) copy-start(s32[16,1]{0,1:T(1,128)} %param.21) | copy-start | bytes 196
  8.5 6.3 %collective-permute-start = (f32[3,16,128]{2,1,0:T(8,128)S(1)}, f32[3,16,128]{2,1,0:T(8,128)S(1)}, u32[]{:S(2)}, u32[]{:S(2)}) collective-permute-start(f32[3,16,128]{2,1,0:T(8,128)S(1)} %get-tuple-element.17), channel_id=1, source_target_pairs={{0,1},{1,0},{2,3},{3,2},{4,5},{5,4},{6,7},{7,6},{8,9},{9,8},{10,11... | collective-permute-start | bytes 73736 | tf_op jit(solution)/shard_map/ppermute | solution.py:675
  9.8 1.1 %copy-start.7 = (f32[16,80,128]{2,1,0:T(8,128)S(1)}, f32[16,80,128]{2,1,0:T(8,128)}, u32[]{:S(2)}) copy-start(f32[16,80,128]{2,1,0:T(8,128)} %ocean_x.1) | copy-start | bytes 1966084
  10.9 1.1 %copy-start.8 = (f32[16,80,128]{2,1,0:T(8,128)S(1)}, f32[16,80,128]{2,1,0:T(8,128)}, u32[]{:S(2)}) copy-start(f32[16,80,128]{2,1,0:T(8,128)} %ocean_y.1) | copy-start | bytes 1966084
  16.0 20.1 %all-to-all-start = ((f32[16,24,128]{2,1,0:T(8,128)}), f32[16,24,128]{2,1,0:T(8,128)S(1)}, u32[]{:S(2)}, u32[]{:S(2)}) async-start(f32[16,24,128]{2,1,0:T(8,128)} %get-tuple-element.23), calls=%async_computation | async-start | bytes 393216 | tf_op jit(solution)/shard_map/all_to_all | solution.py:715
  23.0 8.2 %collective-permute-start.1 = (f32[408,128]{1,0:T(8,128)S(1)}, f32[408,128]{1,0:T(8,128)S(1)}, u32[]{:S(2)}, u32[]{:S(2)}) collective-permute-start(f32[408,128]{1,0:T(8,128)S(1)} %get-tuple-element.21), channel_id=1, source_target_pairs={{0,2},{2,4},{4,6},{6,8},{8,10},{10,12},{12,14},{14,16},{16,18},{18... | collective-permute-start | bytes 626696 | tf_op jit(solution)/shard_map/ppermute | solution.py:717
  26.3 8.0 %collective-permute-start.2 = (f32[408,128]{1,0:T(8,128)S(1)}, f32[408,128]{1,0:T(8,128)S(1)}, u32[]{:S(2)}, u32[]{:S(2)}) collective-permute-start(f32[408,128]{1,0:T(8,128)S(1)} %get-tuple-element.22), channel_id=1, source_target_pairs={{2,0},{4,2},{6,4},{8,6},{10,8},{12,10},{14,12},{16,14},{18,16},{20... | collective-permute-start | bytes 626696 | tf_op jit(solution)/shard_map/ppermute | solution.py:718
  28.2 2.9 %collective-permute-start.3 = (f32[80,128]{1,0:T(8,128)S(1)}, f32[80,128]{1,0:T(8,128)S(1)}, u32[]{:S(2)}, u32[]{:S(2)}) collective-permute-start(f32[80,128]{1,0:T(8,128)S(1)} %get-tuple-element.24.refs_3_), channel_id=1, source_target_pairs={{0,1},{1,0},{2,3},{3,2},{4,5},{5,4},{6,7},{7,6},{8,9},{9,8},{10,11... | collective-permute-start | bytes 122888 | tf_op jit(solution)/shard_map/ppermute | solution.py:675
  34.3 1.8 %copy-start.2 = (f32[16,10,128]{2,0,1:T(8,128)S(1)}, f32[16,10,128]{2,0,1:T(8,128)}, u32[]{:S(2)}) copy-start(f32[16,10,128]{2,0,1:T(8,128)} %param.11) | copy-start | bytes 245764
  34.3 1.8 %copy-start.4 = (f32[16,10,128]{2,0,1:T(8,128)S(1)}, f32[16,10,128]{2,0,1:T(8,128)}, u32[]{:S(2)}) copy-start(f32[16,10,128]{2,0,1:T(8,128)} %param.12) | copy-start | bytes 245764
  34.3 1.8 %copy-start.6 = (f32[16,10,128]{2,0,1:T(8,128)S(1)}, f32[16,10,128]{2,0,1:T(8,128)}, u32[]{:S(2)}) copy-start(f32[16,10,128]{2,0,1:T(8,128)} %param.13) | copy-start | bytes 245764

commit v3 on v2

v3 whole, which is shorter than its diff:
```python
import functools

import jax
import jax.numpy as jnp
from jax import lax
from jax.experimental import pallas as pl
from jax.experimental.pallas import tpu as pltpu
from jax.sharding import PartitionSpec as P

PICARD = 2
DIFFUSE = 0.2
GAMMA_MELT = 0.5
TIME_STEP = 0.05
SLOPE_SCALE = 0.1
STRAIN_FLOOR = 0.01
HEATING_RATE = 0.01

LANES = 128
TILE = 8
HALO = 4
RIM = 3
VMEM = pltpu.CompilerParams(vmem_limit_bytes=16 * 1024 * 1024)
F32 = jnp.float32

THICK, GROUNDED, OCEAN_T, WET, ICE_LINK, OCEAN_LINK = range(6)
PLANES = 6
CORNER = (THICK, GROUNDED, ICE_LINK)
PART, EDGE_T0, EDGE_T1, EDGE_W0, PART_WET, EDGE_W1 = range(6)


def iota(shape, axis):
    return lax.broadcasted_iota(jnp.int32, shape, axis)


def right_lanes(period):
    lane = iota((1, LANES), 1)
    return lane % period < HALO


def left_lanes(period):
    lane = iota((1, LANES), 1)
    return lane % period >= period - HALO


def spread(column, count=LANES):
    rows = column.shape[0]
    eye = iota((rows, count), 0) == iota((rows, count), 1)
    return jnp.sum(jnp.where(eye, column, 0.0), axis=0, keepdims=True)


def upright(row):
    count = row.shape[1]
    eye = iota((count, count), 0) == iota((count, count), 1)
    return jnp.sum(jnp.where(eye, row, 0.0), axis=1, keepdims=True)


def turn(value, shift, axis):
    shift %= value.shape[axis]
    return pltpu.roll(value, shift, axis) if shift else value


def fetch_all(pairs, sems):
    copies = [pltpu.make_async_copy(a, b, sems.at[i]) for i, (a, b) in enumerate(pairs)]
    for copy in copies:
        copy.start()
    return copies


def divide(whole, part):
    return jnp.floor((whole + 0.5) * (1.0 / part))


def pick(hot, value):
    hot = hot.astype(jnp.bfloat16)
    pieces = []
    for _ in range(3):
        pieces.append(value.astype(jnp.bfloat16))
        value = value - pieces[-1].astype(F32)
    a, b, c = (jnp.dot(hot, p, preferred_element_type=F32) for p in pieces)
    return (c + b) + a


def narrow_sides(n_narrow):
    place = lax.axis_index("narrow")
    return place < n_narrow - 1, place > 0


def merged(parts, right, left, n_narrow):
    has_right, has_left = narrow_sides(n_narrow)
    from_right, from_left = parts[0], parts[-1]
    if len(parts) == 1:
        keep = (right & has_right) | (left & has_left)
        return jnp.where(keep, from_right, 0.0)
    return jnp.where(right, from_right, jnp.where(left, from_left, 0.0))


def ice_group(index):
    return divmod(index, LANES // 8)


def ice_tiles(layers):
    return ice_group(3 * layers - 1)[0] + 1


def ice_pairs(layers):
    return -(-3 * layers // 2)


class Places:
    def __init__(self, levels, layers):
        self.ice = 3 * levels
        self.thick = self.ice + ice_pairs(layers) * TILE
        self.grounded = self.thick + TILE
        self.wet = self.grounded + TILE
        self.link = self.wet + TILE
        self.end = self.link + TILE


def odd_place():
    return lax.axis_index("wide") % 2 == 1


def pack_ice(tile_of, layers):
    lane = iota((1, LANES), 1)
    tiles = [None] * ice_tiles(layers)
    for index in range(3 * layers):
        tile, group = ice_group(index)
        turned = turn(tile_of(*divmod(index, layers)), 8 * group, 1)
        before = jnp.zeros_like(turned) if group == 0 else tiles[tile]
        tiles[tile] = jnp.where((lane + HALO) % LANES // 8 == group, turned, before)
    return tiles


def pack_planes(planes):
    lane = iota((1, LANES), 1)
    total = None
    for j, plane in planes.items():
        turned = turn(plane, 16 * j, 1)
        before = jnp.zeros_like(turned) if total is None else total
        total = jnp.where((lane + HALO) % LANES // 16 == j, turned, before)
    return total


def edges_kernel(
    ice_x, ice_y, ice_t, ocean_x, ocean_y, ocean_t, thick, grounded, wet, ice_links, ocean_links,
    out, pair, cross, planes, ice, field, thick_v, grounded_v, wet_v, links_v, sems, field_sems,
):
    layers, rows, _ = ice_x.shape
    levels = ocean_x.shape[1]
    chunks = field_sems.shape[0] // 3
    step = rows // chunks
    copies = fetch_all(
        (
            (ice_x, ice.at[0]),
            (ice_y, ice.at[1]),
            (ice_t, ice.at[2]),
            (thick, thick_v),
            (grounded, grounded_v),
            (wet, wet_v),
            (ice_links, links_v.at[0]),
            (ocean_links, links_v.at[1]),
        ),
        sems,
    )
    field_copies = fetch_all(
        [
            (source.at[pl.ds(h * step, step)], field.at[f, pl.ds(h * step, step)])
            for f, source in reversed(list(enumerate((ocean_x, ocean_y, ocean_t))))
            for h in range(chunks)
        ],
        field_sems,
    )
    places = Places(levels, layers)
    odd = odd_place()

    def send(at, size, lasts, firsts):
        pair[at : at + size, :] = jnp.where(odd, firsts, lasts)
        cross[at : at + size, :] = jnp.where(odd, lasts, firsts)

    lane = iota((1, LANES), 1)
    for copy in copies:
        copy.wait()
    for tile, value in enumerate(pack_ice(lambda f, k: ice[f, k], layers)):
        out[(1 + tile) * rows : (2 + tile) * rows, :] = value
    upper = iota((TILE, 1), 0) >= HALO
    half = ice_pairs(layers)
    for m in range(half):
        ends = []
        for index in (m, m + half):
            f, k = divmod(min(index, 3 * layers - 1), layers)
            ends.append((ice[f, k, rows - TILE :, :], ice[f, k, :TILE, :]))
        send(
            places.ice + m * TILE,
            TILE,
            jnp.where(upper, ends[0][0], turn(ends[1][0], HALO, 0)),
            jnp.where(upper, turn(ends[1][1], HALO, 0), ends[0][1]),
        )
    planes[THICK] = thick_v[...]
    planes[GROUNDED] = grounded_v[...].astype(F32)
    planes[WET] = wet_v[...].astype(F32)
    for k in range(2):
        link = upright(links_v[k].astype(F32)) + 1.0
        planes[ICE_LINK + k] = jnp.broadcast_to(link, (rows, LANES))
    for at, j in (
        (places.thick, THICK), (places.grounded, GROUNDED), (places.wet, WET), (places.link, ICE_LINK),
    ):
        send(at, TILE, planes[j, rows - TILE :, :], planes[j, :TILE, :])
    total = jnp.zeros((levels, LANES), F32)
    for n, f in enumerate((2, 1, 0)):
        for h in range(chunks):
            field_copies[n * chunks + h].wait()
            for i in range(h * step, (h + 1) * step):
                j = f * rows + i
                turned = turn(field[f, i], 2 * j, 1)
                total = jnp.where((lane + 1) % LANES // 2 == j, turned, total)
        send(f * levels, levels, field[f, rows - 1], field[f, 0])
        if f == 2:
            for i in range(rows):
                planes[OCEAN_T, i : i + 1, :] = field[2, i, 0:1, :]
            out[0:rows, :] = pack_planes({j: planes[j] for j in range(PLANES)})
    out[(1 + ice_tiles(layers)) * rows :, :] = total


def plane_halo(block, group):
    lane = iota((1, LANES), 1)
    turned = turn(block, -16 * group, 1)
    return jnp.where((lane < HALO) | (lane >= LANES - HALO), turned, 0.0)


def merged_planes(parts, rows, n_narrow):
    return merged([p[0:rows, :] for p in parts], right_lanes(16), left_lanes(16), n_narrow)


def merged_ice(parts, rows, n_tiles, n_narrow):
    return [
        merged(
            [p[(1 + t) * rows : (2 + t) * rows, :] for p in parts],
            right_lanes(8), left_lanes(8), n_narrow,
        )
        for t in range(n_tiles)
    ]


def ranks(own_col, member_col, order_sub, order_lane, own_row):
    hits = (own_col == own_row) & member_col & (order_sub < order_lane)
    return jnp.sum(hits.astype(F32), axis=0, keepdims=True)


def ocean_slots(link_col, rows, n_wide, cap, block):
    link_row = spread(link_col)
    parts = []
    for link in (link_col, link_row):
        number = link - 1.0
        tile = divide(number, rows)
        inner = number - tile * rows
        ok = link > 0.5
        parts.append(
            (
                tile,
                (
                    ok,
                    ok & (inner >= rows - RIM) & (tile < n_wide - 1.5),
                    ok & (inner < RIM) & (tile > 0.5),
                ),
            )
        )
    (tile_col, member_col), (tile_row, member_row) = parts
    order_sub, order_lane = iota((rows, LANES), 0), iota((rows, LANES), 1)
    place = iota((n_wide * block, LANES), 0).astype(F32)
    total = jnp.zeros((n_wide * block, LANES), F32)
    for k, shift in enumerate((0.0, 1.0, -1.0)):
        rank = ranks(tile_col, member_col[k], order_sub, order_lane, tile_row)
        target = jnp.where(
            member_row[k], (tile_row + shift) * block + (k * cap + rank), -1.0
        )
        total = total + (place == target).astype(F32)
    return total[:, :rows]


def draft_slots(link_col, rows, n_wide, cap, block):
    link_row = spread(link_col)
    tile_col, tile_row = divide(link_col - 1.0, rows), divide(link_row - 1.0, rows)
    order_sub, order_lane = iota((rows, LANES), 0), iota((rows, LANES), 1)
    rank = ranks(tile_col, link_col > 0.5, order_sub, order_lane, tile_row)
    target = jnp.where(link_row > 0.5, tile_row * block + (3 * cap + rank), -1.0)
    place = iota((n_wide * block, LANES), 0).astype(F32)
    return (place == target).astype(F32)[:, :rows]


def blocks_kernel(n_wide, n_narrow, cap, block, n_parts, *refs):
    parts, refs = refs[:n_parts], refs[n_parts:]
    planes, blocks = refs
    rows = planes.shape[1]
    lane = iota((1, LANES), 1)
    plane_block = merged_planes(parts, rows, n_narrow)
    thick_plane, grounded_plane, wet_plane = planes[THICK], planes[GROUNDED], planes[WET]
    wet_all = jnp.concatenate([wet_plane, plane_halo(plane_block, WET)], axis=1)
    warm = wet_all * jnp.concatenate([planes[OCEAN_T], plane_halo(plane_block, OCEAN_T)], axis=1)
    width = 2 * LANES
    row = iota((rows, width), 0)
    sums = []
    for value in (wet_all, warm):
        total = pltpu.roll(value, 1, 1) + pltpu.roll(value, width - 1, 1)
        total = total + jnp.where(row > 0, pltpu.roll(value, 1, 0), 0.0)
        sums.append(total + jnp.where(row < rows - 1, pltpu.roll(value, rows - 1, 0), 0.0))
    mixed = warm + DIFFUSE * (wet_all * sums[1] - warm * sums[0])
    draft = 0.9 * thick_plane * (1.0 - grounded_plane)
    own_slots = ocean_slots(planes[OCEAN_LINK][:, 0:1], rows, n_wide, cap, block)
    main = pick(own_slots, jnp.concatenate([mixed[:, :LANES], wet_plane], axis=1))
    count = n_wide * block
    slot = iota((count, 1), 0) % block
    first = main[:, :LANES] + pick(draft_slots(planes[ICE_LINK][:, 0:1], rows, n_wide, cap, block), draft)
    second = jnp.where(
        slot == 3 * cap,
        wet_plane[0:1, :],
        jnp.where(slot == 3 * cap + 1, wet_plane[rows - 1 : rows, :], main[:, LANES:]),
    )
    edge = (lane < HALO) | (lane >= LANES - HALO)
    mixed_edge = jnp.where(edge, mixed[:, LANES:], 0.0)
    wet_edge = wet_all[:, LANES:]
    warm_edge = warm[:, LANES:]
    packed = mixed_edge + pltpu.roll(wet_edge, 16 * PART_WET, 1)
    links = plane_halo(plane_block, OCEAN_LINK)
    if n_narrow == 2:
        third = pick(
            ocean_slots(jnp.max(links, axis=1, keepdims=True), rows, n_wide, cap, block), packed
        )
    else:
        third = pick(
            ocean_slots(links[:, 0:1], rows, n_wide, cap, block),
            jnp.where(right_lanes(16), packed, 0.0),
        ) + pick(
            ocean_slots(links[:, LANES - 1 : LANES], rows, n_wide, cap, block),
            jnp.where(left_lanes(16), packed, 0.0),
        )
    last = rows - 1
    ends = (
        pltpu.roll(warm_edge[0:1, :], 16 * EDGE_T0, 1)
        + pltpu.roll(warm_edge[last:, :], 16 * EDGE_T1, 1)
        + pltpu.roll(wet_edge[0:1, :], 16 * EDGE_W0, 1)
        + pltpu.roll(wet_edge[last:, :], 16 * EDGE_W1, 1)
    )
    third = jnp.where(
        slot == 3 * cap,
        warm[0:1, :LANES],
        jnp.where(slot == 3 * cap + 1, warm[last:, :LANES], third + ends),
    )
    for k, value in enumerate((first, second, third)):
        blocks[:, k * block : (k + 1) * block, :] = value.reshape(n_wide, block, LANES)


def beyond_ice(up, down, places, layers, f, k):
    under = iota((TILE, 1), 0) < HALO
    index, half = f * layers + k, ice_pairs(layers)
    at = places.ice + index % half * TILE
    if index < half:
        return jnp.where(under, down(at, TILE), up(at, TILE))
    return turn(jnp.where(under, up(at, TILE), down(at, TILE)), HALO, 0)


def came_from(pair, cross):
    odd = odd_place()

    def up(at, size):
        return jnp.where(odd, pair[pl.ds(at, size), :], cross[pl.ds(at, size), :])

    def down(at, size):
        return jnp.where(odd, cross[pl.ds(at, size), :], pair[pl.ds(at, size), :])

    return up, down


def corners_kernel(levels, layers, pair, cross, out):
    places = Places(levels, layers)
    up, down = came_from(pair, cross)
    under = iota((TILE, 1), 0) < HALO
    tiles = pack_ice(lambda f, k: beyond_ice(up, down, places, layers, f, k), layers)
    planes = {}
    for j, at in zip(CORNER, (places.thick, places.grounded, places.link)):
        planes[j] = jnp.where(under, down(at, TILE), up(at, TILE))
    for n, tile in enumerate((pack_planes(planes), *tiles)):
        out[n * TILE : (n + 1) * TILE, :] = tile


def ocean_kernel(n_narrow, n_parts, n_tiles, layers, *refs):
    parts, refs = refs[:n_parts], refs[n_parts:]
    ocean_x, ocean_y, ocean_t, pair, cross, planes, out, top, field, held, sems = refs
    rows, levels, _ = ocean_x.shape
    places = Places(levels, layers)
    chunks = sems.shape[0] // 6
    step = rows // chunks
    reads = fetch_all(
        [
            (source.at[pl.ds(h * step, step)], field.at[f, pl.ds(h * step, step)])
            for f, source in enumerate((ocean_x, ocean_y, ocean_t))
            for h in range(chunks)
        ],
        sems,
    )
    up, down = came_from(pair, cross)
    lane = iota((1, LANES), 1)
    row = iota((rows, LANES), 0)
    first, last = lane == 0, lane == LANES - 1
    wet = planes[WET]
    wet_halo = plane_halo(merged_planes(parts, rows, n_narrow), WET)
    scale = DIFFUSE * wet
    coef = (
        scale * jnp.where(row > 0, turn(wet, 1, 0), up(places.wet + TILE - 1, 1)),
        scale * jnp.where(row < rows - 1, turn(wet, -1, 0), down(places.wet, 1)),
        scale * turn(jnp.where(last, wet_halo, wet), 1, 1),
        scale * turn(jnp.where(first, wet_halo, wet), -1, 1),
    )
    centre_coef = 1.0 - (coef[0] + coef[1] + coef[2] + coef[3])
    even = lane % 2 == 0
    strip_at = (1 + n_tiles) * rows
    side = merged([p[strip_at:, :] for p in parts], even, ~even, n_narrow)
    writes = []
    for f in range(3):
        for h in range(chunks):
            reads[f * chunks + h].wait()
        for h in range(chunks):
            for i in range(h * step, (h + 1) * step):
                centre = field[f, i]
                halo = turn(side, -2 * (f * rows + i), 1)
                above = field[f, i - 1] if i > 0 else up(f * levels, levels)
                below = field[f, i + 1] if i < rows - 1 else down(f * levels, levels)
                value = centre * centre_coef[i : i + 1, :]
                value = value + above * coef[0][i : i + 1, :]
                value = value + below * coef[1][i : i + 1, :]
                value = value + turn(jnp.where(last, halo, centre), 1, 1) * coef[2][i : i + 1, :]
                value = value + turn(jnp.where(first, halo, centre), -1, 1) * coef[3][i : i + 1, :]
                held[f, i] = value
                if f == 2:
                    top[i] = value[0:TILE, :]
            part = pl.ds(h * step, step)
            level = pl.ds(TILE, levels - TILE) if f == 2 else pl.ds(0, levels)
            copy = pltpu.make_async_copy(
                held.at[f, part, level],
                out.at[f, part, level],
                sems.at[(3 + f) * chunks + h],
            )
            copy.start()
            writes.append(copy)
    for copy in writes:
        copy.wait()


def ice_slots(link_col, kind_col, rows, cap, block, count, n_wide):
    link_row = spread(link_col)
    kind_row = spread(kind_col)
    number = link_col - 1.0
    tile = divide(number, rows)
    inner = number - tile * rows
    tile_row = divide(link_row - 1.0, rows)
    ok = (link_col > 0.5) & (kind_col > -0.5)
    ok_row = (link_row > 0.5) & (kind_row > -0.5)
    hits = (tile == tile_row) & (kind_col == kind_row) & ok_row & (link_row < link_col)
    rank = jnp.sum(hits.astype(F32), axis=1, keepdims=True)
    place = iota((link_col.shape[0], count), 1).astype(F32)

    def hot(keep, target):
        return (place == jnp.where(keep, target, -1.0)).astype(F32)

    top, bottom = inner < 0.5, inner > rows - 1.5
    edge = ok & (top | bottom)
    near = jnp.where(top, tile - 1.0, tile + 1.0)
    near_ok = edge & (near > -0.5) & (near < n_wide - 0.5)
    slot = hot(ok, tile * block + kind_col * cap + rank)
    near_edge = hot(near_ok, near * block + jnp.where(top, 3.0 * cap + 1.0, 3.0 * cap))
    own_edge = hot(edge, tile * block + jnp.where(top, 3.0 * cap, 3.0 * cap + 1.0))
    near_slot = hot(near_ok, near * block)
    own_slot = hot(edge, tile * block)
    return slot, near_edge, own_edge, near_slot, own_slot, bottom.astype(F32)


def around(value):
    return turn(value, 1, 0) + turn(value, -1, 0) + turn(value, 1, 1) + turn(value, -1, 1)


def sweep_layer(vel, k, layers, rate, friction):
    u, v = vel(0, k), vel(1, k)
    ends = [[turn(w, s, axis) for axis in (0, 1) for s in (-1, 1)] for w in (u, v)]
    ux, uy = ends[0][0] - ends[0][1], ends[0][2] - ends[0][3]
    vx, vy = ends[1][0] - ends[1][1], ends[1][2] - ends[1][3]
    cross = uy + vx
    eps2 = ux * (ux + vy) + vy * vy + 0.25 * (cross * cross)
    if k < layers - 1:
        uz, vz = vel(0, k + 1) - u, vel(1, k + 1) - v
        eps2 = eps2 + (uz * uz + vz * vz)
    eps2 = 0.25 * eps2
    eta = rate * jnp.exp((-1.0 / 3.0) * jnp.log(eps2 + STRAIN_FLOOR))
    links_up_down = float((k > 0) + (k < layers - 1))
    diagonal = eta * (2.0 + links_up_down) + 0.5 * around(eta) + friction
    sums = []
    for f, w in enumerate((u, v)):
        total = 0.5 * (ends[f][0] + ends[f][1] + ends[f][2] + ends[f][3])
        if k > 0:
            total = total + vel(f, k - 1)
        if k < layers - 1:
            total = total + vel(f, k + 1)
        sums.append(eta * total + 0.5 * around(eta * w))
    return sums, 1.0 / diagonal, eta * eps2


FLAT = ("thick", "grounded", "inside")


def first_kernel(n_wide, n_narrow, cap, block, n_parts, levels, *refs):
    parts, refs = refs[:n_parts], refs[n_parts:]
    corners, refs = refs[:n_parts], refs[n_parts:]
    ice, pair, cross, planes, sums, inverse, rate, flat, hots, ends, vel = refs
    _, layers, rows, _ = ice.shape
    places = Places(levels, layers)
    n_tiles = ice_tiles(layers)
    up, down = came_from(pair, cross)
    lane = iota((1, LANES), 1)
    width = 2 * LANES
    tall = rows + TILE
    wide_lane = iota((1, width), 1)
    place_wide = lax.axis_index("wide")
    has_right, has_left = narrow_sides(n_narrow)
    has_up, has_down = place_wide > 0, place_wide < n_wide - 1
    under = iota((TILE, 1), 0) < HALO

    def rim(at):
        return jnp.where(under, down(at, TILE), up(at, TILE))

    def below(a, b):
        return jnp.concatenate([a, b], axis=0)

    corner_planes = merged(
        [c[0:TILE, :] for c in corners], right_lanes(16), left_lanes(16), n_narrow
    )
    corner_ice = [
        merged(
            [c[(1 + t) * TILE : (2 + t) * TILE, :] for c in corners],
            right_lanes(8), left_lanes(8), n_narrow,
        )
        for t in range(n_tiles)
    ]
    block_tall = below(merged_planes(parts, rows, n_narrow), corner_planes)
    flat[0] = jnp.concatenate(
        [below(planes[THICK], rim(places.thick)), plane_halo(block_tall, THICK)], axis=1
    )
    grounded_tall = jnp.concatenate(
        [below(planes[GROUNDED], rim(places.grounded)), plane_halo(block_tall, GROUNDED)], axis=1
    )
    flat[1] = grounded_tall
    tall_row = iota((tall, 1), 0)
    inside = (
        ((tall_row < rows) | ((tall_row < rows + HALO) & has_down) | ((tall_row >= rows + HALO) & has_up))
        & (
            (wide_lane < LANES)
            | ((wide_lane < LANES + HALO) & has_right)
            | ((wide_lane >= width - HALO) & has_left)
        )
    ).astype(F32)
    flat[2] = inside
    kind = jnp.where(
        tall_row < rows,
        0.0,
        jnp.where(tall_row < rows + RIM, 2.0, jnp.where(tall_row >= tall - RIM, 1.0, -1.0)),
    )
    count = n_wide * block
    own_link = below(planes[ICE_LINK], rim(places.link))[:, 0:1]
    slots = (rows, cap, block, count, n_wide)
    found = list(ice_slots(own_link, kind, *slots)[:3])
    links = plane_halo(block_tall, ICE_LINK)
    if n_narrow == 2:
        sides = [jnp.max(links, axis=1, keepdims=True)]
    else:
        sides = [links[:, 0:1], links[:, LANES - 1 : LANES]]
    for link in sides:
        slot, _, _, near_slot, own_slot, bottom = ice_slots(link, kind, *slots)
        ends[(len(found) - 3) // 3] = jnp.broadcast_to(bottom, (tall, LANES))
        found += [slot, near_slot, own_slot]
    for n, hot in enumerate(found):
        hots[n * tall : (n + 1) * tall, :] = hot
    ocean_link = planes[OCEAN_LINK][:, 0:1]
    ocean_row = spread(ocean_link)
    tile = divide(ocean_link - 1.0, rows)
    tile_row = divide(ocean_row - 1.0, rows)
    hits = (tile == tile_row) & (ocean_row > 0.5) & (ocean_row < ocean_link)
    rank = jnp.sum(hits.astype(F32), axis=1, keepdims=True)
    target = jnp.where(ocean_link > 0.5, tile * block + 3 * cap + rank, -1.0)
    hots[len(found) * tall :, :] = (iota((rows, count), 1).astype(F32) == target).astype(F32)
    strips = [
        below(a, b) for a, b in zip(merged_ice(parts, rows, n_tiles, n_narrow), corner_ice)
    ]
    edge = (lane < HALO) | (lane >= LANES - HALO)
    for index in range(3 * layers):
        f, k = divmod(index, layers)
        beyond = beyond_ice(up, down, places, layers, f, k)
        t, group = ice_group(index)
        beside = jnp.where(edge, turn(strips[t], -8 * group, 1), 0.0)
        value = jnp.concatenate([below(ice[f, k], beyond), beside], axis=1)
        if f < 2:
            vel[f, k] = value
        else:
            rate[k] = jnp.exp(0.25 * value) * inside
    friction = 0.1 + 9.9 * grounded_tall
    for k in range(layers):
        both, over, _ = sweep_layer(lambda f, n: vel[f, n], k, layers, rate[k], friction)
        for f in range(2):
            sums[f, k] = both[f]
        inverse[k] = over * inside


def final_kernel(n_wide, n_narrow, cap, block, *refs):
    (
        blocks, hots, ends, planes, ice, top, sums, inverse, rate, flat, ocean_in,
        ice_out, ocean_out, thick_out, melt_out,
        vel, result, thin, melted, new_top, sems,
    ) = refs
    _, layers, rows, _ = ice.shape
    tall, width = flat.shape[1:]
    lane = iota((1, LANES), 1)
    count = n_wide * block
    parts = [
        blocks[:, n * block : (n + 1) * block, :].reshape(count, LANES) for n in range(3)
    ]
    found = pick(hots[...], jnp.concatenate(parts, axis=1))

    def got(n, part):
        return found[n * tall : (n + 1) * tall, part * LANES : (part + 1) * LANES]

    wet_main = got(0, 1)
    mixed_main = got(0, 0) + DIFFUSE * (wet_main * got(1, 2) - got(1, 1) * got(2, 2))
    sides = []
    for n in range(3, 3 * (1 if n_narrow == 2 else 2) + 3, 3):
        value, near, own = got(n, 2), got(n + 1, 2), got(n + 2, 2)

        def group(row, j):
            return turn(row, -16 * j, 1)

        wet_got = group(value, PART_WET)
        bottom = ends[n // 3 - 1] > 0.5
        near_warm = jnp.where(bottom, group(near, EDGE_T0), group(near, EDGE_T1))
        near_wet = jnp.where(bottom, group(near, EDGE_W0), group(near, EDGE_W1))
        own_warm = jnp.where(bottom, group(own, EDGE_T1), group(own, EDGE_T0))
        sides.append((value + DIFFUSE * (wet_got * near_warm - near_wet * own_warm), wet_got))
    if len(sides) == 1:
        mixed_side, wet_side = sides[0]
    else:
        mixed_side, wet_side = (jnp.where(lane < HALO, a, b) for a, b in zip(*sides))
    mixed_tall = jnp.concatenate([mixed_main, mixed_side], axis=1)
    wet_tall = jnp.concatenate([wet_main, wet_side], axis=1)
    thick_tall, grounded_tall, inside = flat[0], flat[1], flat[2]
    open_ice = 1.0 - grounded_tall
    draft_tall = 0.9 * thick_tall * open_ice
    melt_tall = GAMMA_MELT * (mixed_tall - wet_tall * (0.0832 - 0.761 * draft_tall))
    new_thick = (thick_tall - TIME_STEP * melt_tall * open_ice) * inside
    thin[...] = new_thick[:rows, :LANES]
    n_hots = hots.shape[0] - rows
    ocean_draft = found[n_hots:, :LANES]
    heat_top = jnp.concatenate([top[i, 0:1, :] for i in range(rows)], axis=0)
    coupled = (planes[OCEAN_LINK] > 0.5).astype(F32)
    melt = GAMMA_MELT * (heat_top - (0.0832 - 0.761 * ocean_draft)) * planes[WET] * coupled
    melted[...] = melt
    cooled = heat_top - 0.2 * melt
    new_top[...] = top[...]
    for i in range(rows):
        new_top[i, 0:1, :] = cooled[i : i + 1, :]
    writes = fetch_all(
        (
            (new_top, ocean_out.at[2, :, pl.ds(0, TILE), :]),
            (thin, thick_out),
            (melted, melt_out),
        ),
        sems,
    )
    surface = new_thick * (0.1 + 0.9 * grounded_tall)
    scale = (-0.5 * SLOPE_SCALE) * new_thick
    stress = (
        scale * (turn(surface, -1, 0) - turn(surface, 1, 0)),
        scale * (turn(surface, -1, 1) - turn(surface, 1, 1)),
    )
    friction = 0.1 + 9.9 * grounded_tall
    for f in range(2):
        for k in range(layers):
            vel[0, f, k] = (sums[f, k] + stress[f]) * inverse[k]
    for sweep in range(1, PICARD):
        last = sweep == PICARD - 1
        old = sweep - 1
        for k in range(layers):
            both, over, heat = sweep_layer(
                lambda f, n: vel[old, f, n], k, layers, rate[k], friction
            )
            for f in range(2):
                value = (both[f] + stress[f]) * over
                if last:
                    result[f, k] = value[:rows, :LANES]
                else:
                    vel[sweep, f, k] = value * inside
            if last:
                result[2, k] = ice[2, k] + HEATING_RATE * heat[:rows, :LANES]
                copy = pltpu.make_async_copy(
                    result.at[:, k], ice_out.at[:, k], sems.at[len(writes)]
                )
                copy.start()
                writes.append(copy)
    for copy in writes:
        copy.wait()


def local(
    ice_x, ice_y, ice_temp, ocean_x, ocean_y, ocean_temp, thick, grounded_mask, wet_mask, ice_links, ocean_links,
):
    n_wide, n_narrow = lax.axis_size("wide"), lax.axis_size("narrow")
    rows, layers, columns = ice_x.shape
    levels = ocean_x.shape[1]
    cap = max(1, 2 * rows // n_wide)
    block = -(-max(4 * cap, 3 * cap + 2) // TILE) * TILE
    assert columns == LANES and ice_links.shape[0] == rows

    def stay(value):
        return pltpu.with_memory_space_constraint(value, pltpu.HBM)

    ice_fields = [stay(x.transpose(1, 0, 2)) for x in (ice_x, ice_y, ice_temp)]
    links = [stay(x.reshape(1, rows)) for x in (ice_links, ocean_links)]
    fields = [stay(x) for x in (ocean_x, ocean_y, ocean_temp)]
    planes_in = [stay(x) for x in (thick, grounded_mask, wet_mask)]
    here = pl.BlockSpec(memory_space=pltpu.VMEM)
    far = pl.BlockSpec(memory_space=pltpu.HBM)
    unread = pl.BlockSpec(memory_space=pl.ANY)
    dma = pltpu.SemaphoreType.DMA

    def array(*shape):
        return jax.ShapeDtypeStruct(shape, F32)

    def kept(*shape):
        return pltpu.VMEM(shape, F32)

    def near(*values):
        return [pltpu.with_memory_space_constraint(value, pltpu.VMEM) for value in values]

    def call(kernel, name, microseconds, out_shape, in_specs, out_specs, scratch=(), **more):
        estimate = pl.CostEstimate(
            flops=int(microseconds * 1.0e9), bytes_accessed=int(microseconds * 3.0e6), transcendentals=0
        )
        return pl.pallas_call(
            kernel, name=name, out_shape=out_shape, in_specs=in_specs, out_specs=out_specs,
            scratch_shapes=scratch, compiler_params=VMEM, cost_estimate=estimate, **more,
        )

    n_tiles = ice_tiles(layers)
    places = Places(levels, layers)
    chunks = 2
    message, to_pair, to_cross, planes, ice = call(
        edges_kernel, "edges", 100.0,
        (
            kept((1 + n_tiles) * rows + levels, LANES), kept(places.end, LANES), kept(places.end, LANES),
            kept(PLANES, rows, LANES), kept(3, layers, rows, LANES),
        ),
        [far] * 11, (here,) * 5,
        [
            pltpu.VMEM((3, rows, levels, LANES), F32),
            pltpu.VMEM((rows, LANES), F32),
            pltpu.VMEM((rows, LANES), jnp.int32),
            pltpu.VMEM((rows, LANES), jnp.int32),
            pltpu.VMEM((2, 1, rows), jnp.int32),
            dma((8,)),
            dma((3 * chunks,)),
        ],
    )(*ice_fields, *fields, *planes_in, *links)

    def narrow(value):
        if n_narrow == 2:
            return [lax.ppermute(value, "narrow", [(0, 1), (1, 0)])]
        ahead = [(i, i + 1) for i in range(n_narrow - 1)]
        return [
            lax.ppermute(value, "narrow", [(j, i) for i, j in ahead]),
            lax.ppermute(value, "narrow", ahead),
        ]

    parts = narrow(message)
    n_parts = len(parts)
    assert n_wide % 2 == 0
    swaps = [[(i, i + 1) for i in range(start, n_wide - 1, 2)] for start in (0, 1)]
    pair, cross = (
        lax.ppermute(value, "wide", swap + [(j, i) for i, j in swap])
        for value, swap in zip((to_pair, to_cross), swaps)
    )
    blocks = call(
        functools.partial(blocks_kernel, n_wide, n_narrow, cap, block, n_parts), "blocks", 100.0,
        kept(n_wide, 3 * block, LANES), [here] * (n_parts + 1), here,
    )(*near(*parts, planes))
    blocks = lax.all_to_all(blocks, "wide", split_axis=0, concat_axis=0, tiled=True)
    corners = narrow(
        call(
            functools.partial(corners_kernel, levels, layers), "corners", 1.0,
            kept((1 + n_tiles) * TILE, LANES), [here] * 2, here,
        )(*near(pair, cross))
    )
    ocean, top = call(
        functools.partial(ocean_kernel, n_narrow, n_parts, n_tiles, layers), "ocean", 100.0,
        (array(3, rows, levels, LANES), kept(rows, TILE, LANES)),
        [here] * n_parts + [far] * 3 + [here] * 3, (far, here),
        [
            pltpu.VMEM((3, rows, levels, LANES), F32),
            pltpu.VMEM((3, rows, levels, LANES), F32),
            dma((6 * chunks,)),
        ],
    )(*near(*parts), *fields, *near(pair, cross, planes))
    wide = 2 * LANES
    tall = rows + TILE
    n_sides = 1 if n_narrow == 2 else 2
    sums, inverse, rate, flat, hots, ends = call(
        functools.partial(first_kernel, n_wide, n_narrow, cap, block, n_parts, levels), "first", 100.0,
        (
            kept(2, layers, tall, wide), kept(layers, tall, wide), kept(layers, tall, wide), kept(3, tall, wide),
            kept((3 + 3 * n_sides) * tall + rows, n_wide * block), kept(n_sides, tall, LANES),
        ),
        [here] * (2 * n_parts + 4), (here,) * 6,
        [pltpu.VMEM((2, layers, tall, wide), F32)],
    )(*near(*parts, *corners, ice, pair, cross, planes))
    ice, ocean, thick_out, melt_out = call(
        functools.partial(final_kernel, n_wide, n_narrow, cap, block), "final", 3.0,
        (
            array(3, layers, rows, LANES), array(3, rows, levels, LANES),
            array(rows, LANES), array(rows, LANES),
        ),
        [here] * 10 + [far], (far,) * 4,
        [
            pltpu.VMEM((PICARD - 1, 2, layers, tall, wide), F32),
            pltpu.VMEM((3, layers, rows, LANES), F32),
            pltpu.VMEM((rows, LANES), F32),
            pltpu.VMEM((rows, LANES), F32),
            pltpu.VMEM((rows, TILE, LANES), F32),
            dma((3 + layers,)),
        ],
        input_output_aliases={10: 1},
    )(*near(blocks, hots, ends, planes, ice, top, sums, inverse, rate, flat), ocean)
    return ice.transpose(0, 2, 1, 3), ocean, thick_out, melt_out


def solution(mesh):
    column = P("wide", None, "narrow")
    plane = P("wide", "narrow")
    return jax.shard_map(
        local,
        mesh=mesh,
        in_specs=(column,) * 6 + (plane,) * 5,
        out_specs=(P(None, "wide", None, "narrow"), P(None, "wide", None, "narrow"), plane, plane),
        check_vma=False,
    )
```

time: 41.8 us -> 28.3 us (0.68)
  the two profiles are of different devices: /device:TPU:3 before, /device:TPU:0 now
where the time goes in v3:
time: 28.3 us; the launch traced here: 28 us
  Pallas kernels  13.9 us (49%)
  starting transfers between devices  11.8 us (42%)
  waiting for transfers between devices  1.58 us (6%)
  between operations  0.71 us (3%)
    all_to_all x1, starting transfers between devices, local(): lax.all_to_all(blocks, 'wide', split_axis=0, concat_axis=0, tiled=True)  6.46 us
    pallas_call x1, Pallas kernels, local(): call(functools.partial(ocean_kernel, n_narrow, n_parts, n_tiles, layers),...  5.87 us
    ppermute x2, starting transfers between devices, narrow(): return [lax.ppermute(value, 'narrow', [(0, 1), (1, 0)])]  4.63 us
    pallas_call x1, Pallas kernels, local(): call(functools.partial(final_kernel, n_wide, n_narrow, cap, block), 'fina...  2.64 us
    pallas_call x1, Pallas kernels, local(): call(edges_kernel, 'edges', 100.0, (kept((1 + n_tiles) * rows + levels, L...  2.52 us
    pallas_call x1, Pallas kernels, local(): call(functools.partial(first_kernel, n_wide, n_narrow, cap, block, n_part...  1.75 us
    ppermute x2, waiting for transfers between devices, narrow(): return [lax.ppermute(value, 'narrow', [(0, 1), (1, 0)])]  1.57 us
    pallas_call x1, Pallas kernels, local(): call(functools.partial(blocks_kernel, n_wide, n_narrow, cap, block, n_par...  1.06 us
  transfers between devices with their start and end apart: 5, of which 1 were waited for; matrix products, arithmetic and copies ran while one was open for 0% of the time, Pallas kernels for 31%

profile of v3, /device:TPU:0, one launch (start us, length us, event | category | flops | bytes accessed | tf_op | source)
XLA Modules:
  0.0 28.0 jit_solution(11864135492312890804)
XLA Ops:
  0.6 2.5 %edges.1 = (f32[128,128]{1,0:T(8,128)S(1)}, f32[392,128]{1,0:T(8,128)S(1)}, f32[392,128]{1,0:T(8,128)S(1)}, f32[6,16,128]{2,1,0:T(8,128)S(1)}, f32[3,10,16,128]{3,2,1,0:T(8,128)S(1)}) custom-call(f32[10,16,128]{2,1,0:T(8,128)} %bitcast.6, f32[10,16,128]{2,1,0:T(8,128)} %bitcast.7, f32[10,16,128]{2,1,0:T(8,128)} %bitcast.8, f32[16,80,128]{2,1,0:T(8,128)} %refs_1_.1, ...), custom_call_target="tpu_custom_call" | custom-call | flops 99999997952 | bytes 300000000 | tf_op jit(solution)/shard_map/edges/pallas_call | solution.py:749
  3.2 3.0 %collective-permute-start = (f32[128,128]{1,0:T(8,128)S(1)}, f32[128,128]{1,0:T(8,128)S(1)}, u32[]{:S(2)}, u32[]{:S(2)}) collective-permute-start(f32[128,128]{1,0:T(8,128)S(1)} %get-tuple-element.21), channel_id=1, source_target_pairs={{0,1},{1,0},{2,3},{3,2},{4,5},{5,4},{6,7},{7,6},{8,9},{9,8},{10,11... | collective-permute-start | bytes 196616 | tf_op jit(solution)/shard_map/ppermute | solution.py:769
  6.2 0.0 collective-permute-start.1
  6.2 0.7 %collective-permute-start.2 = (f32[392,128]{1,0:T(8,128)S(1)}, f32[392,128]{1,0:T(8,128)S(1)}, u32[]{:S(2)}, u32[]{:S(2)}) collective-permute-start(f32[392,128]{1,0:T(8,128)S(1)} %get-tuple-element.24), channel_id=1, source_target_pairs={{2,4},{6,8},{10,12},{14,16},{18,20},{22,24},{26,28},{4,2},{8,6},{1... | collective-permute-start | bytes 602120 | tf_op jit(solution)/shard_map/ppermute | solution.py:781
  6.9 1.6 %collective-permute-done.refs_0_ = f32[128,128]{1,0:T(8,128)S(1)} collective-permute-done((f32[128,128]{1,0:T(8,128)S(1)}, f32[128,128]{1,0:T(8,128)S(1)}, u32[]{:S(2)}, u32[]{:S(2)}) %collective-permute-start) | collective-permute-done | bytes 65568 | tf_op jit(solution)/shard_map/ppermute | solution.py:769
  8.4 1.1 %blocks.1 = f32[16,24,128]{2,1,0:T(8,128)} custom-call(f32[128,128]{1,0:T(8,128)S(1)} %collective-permute-done.refs_0_, f32[6,16,128]{2,1,0:T(8,128)S(1)} %get-tuple-element.22.refs_1_.refs_5_.refs_6_.refs_3_), custom_call_target="tpu_custom_call" | custom-call | flops 99999997952 | bytes 300000000 | tf_op jit(solution)/shard_map/blocks/pallas_call | solution.py:784
  9.5 6.5 %all-to-all-start = ((f32[16,24,128]{2,1,0:T(8,128)}), f32[16,24,128]{2,1,0:T(8,128)}, u32[]{:S(2)}, u32[]{:S(2)}) async-start(f32[16,24,128]{2,1,0:T(8,128)} %blocks.1), calls=%async_computation | async-start | bytes 393216 | tf_op jit(solution)/shard_map/all_to_all | solution.py:788
  16.0 0.0 collective-permute-done.1.pair.refs_3_.refs_4_
  16.0 0.0 collective-permute-done.2.cross.refs_4_.refs_5_
  16.0 0.1 corners.1
  16.1 1.6 %collective-permute-start.3 = (f32[24,128]{1,0:T(8,128)S(1)}, f32[24,128]{1,0:T(8,128)S(1)}, u32[]{:S(2)}, u32[]{:S(2)}) collective-permute-start(f32[24,128]{1,0:T(8,128)S(1)} %corners.1), channel_id=1, source_target_pairs={{0,1},{1,0},{2,3},{3,2},{4,5},{5,4},{6,7},{7,6},{8,9},{9,8},{10,11... | collective-permute-start | bytes 36872 | tf_op jit(solution)/shard_map/ppermute | solution.py:769
  17.7 5.9 %ocean.1 = (f32[3,16,80,128]{3,2,1,0:T(8,128)}, f32[16,8,128]{2,1,0:T(8,128)S(1)}) custom-call(f32[128,128]{1,0:T(8,128)S(1)} %collective-permute-done.refs_0_, f32[16,80,128]{2,1,0:T(8,128)} %refs_1_.1, f32[16,80,128]{2,1,0:T(8,128)} %refs_2_.1, f32[16,80,128]{2,1,0:T(8,128)} %refs_3_.1, f32[392,128]{1,0:T(8,128)S(1)} %collective-permute-done.1.pair.refs_3_.refs_4_, ...), custom_call_target="tpu_custom_call" | custom-call | flops 99999997952 | bytes 300000000 | tf_op jit(solution)/shard_map/ocean/pallas_call | solution.py:795
  23.6 0.0 collective-permute-done.3.refs_1_
  23.6 1.7 %first.1 = (f32[2,10,24,256]{3,2,1,0:T(8,128)S(1)}, f32[10,24,256]{2,1,0:T(8,128)S(1)}, f32[10,24,256]{2,1,0:T(8,128)S(1)}, f32[3,24,256]{2,1,0:T(8,128)S(1)}, f...) custom-call(f32[128,128]{1,0:T(8,128)S(1)} %collective-permute-done.refs_0_, ...), custom_call_target="tpu_custom_call" | custom-call | flops 99999997952 | bytes 300000000 | tf_op jit(solution)/shard_map/first/pallas_call | solution.py:808
  25.3 0.0 all-to-all-done.refs_0_
  25.4 2.6 %final.1 = (f32[3,10,16,128]{3,2,1,0:T(8,128)}, f32[3,16,80,128]{3,2,1,0:T(8,128)}, f32[16,128]{1,0:T(8,128)}, f32[16,128]{1,0:T(8,128)}) custom-call(f32[16,24,128]{2,1,0:T(8,128)} %all-to-all-done.refs_0_, f32[160,128]{1,0:T(8,128)S(1)} %get-tuple-element.26.refs_1_, ...), custom_call_target="tpu_custom_call", output_to_operand_aliasing={{1}: (10, {})} | custom-call | flops 3000000000 | bytes 9000000 | tf_op jit(solution)/shard_map/final/pallas_call | solution.py:817
Async XLA Ops:
  3.2 5.3 %collective-permute-start = (f32[128,128]{1,0:T(8,128)S(1)}, f32[128,128]{1,0:T(8,128)S(1)}, u32[]{:S(2)}, u32[]{:S(2)}) collective-permute-start(f32[128,128]{1,0:T(8,128)S(1)} %get-tuple-element.21), channel_id=1, source_target_pairs={{0,1},{1,0},{2,3},{3,2},{4,5},{5,4},{6,7},{7,6},{8,9},{9,8},{10,11... | collective-permute-start | bytes 196616 | tf_op jit(solution)/shard_map/ppermute | solution.py:769
  6.2 9.8 %collective-permute-start.1 = (f32[392,128]{1,0:T(8,128)S(1)}, f32[392,128]{1,0:T(8,128)S(1)}, u32[]{:S(2)}, u32[]{:S(2)}) collective-permute-start(f32[392,128]{1,0:T(8,128)S(1)} %get-tuple-element.23), channel_id=1, source_target_pairs={{0,2},{4,6},{8,10},{12,14},{16,18},{20,22},{24,26},{28,30},{2,0},{... | collective-permute-start | bytes 602120 | tf_op jit(solution)/shard_map/ppermute | solution.py:781
  6.2 9.8 %collective-permute-start.2 = (f32[392,128]{1,0:T(8,128)S(1)}, f32[392,128]{1,0:T(8,128)S(1)}, u32[]{:S(2)}, u32[]{:S(2)}) collective-permute-start(f32[392,128]{1,0:T(8,128)S(1)} %get-tuple-element.24), channel_id=1, source_target_pairs={{2,4},{6,8},{10,12},{14,16},{18,20},{22,24},{26,28},{4,2},{8,6},{1... | collective-permute-start | bytes 602120 | tf_op jit(solution)/shard_map/ppermute | solution.py:781
  9.5 15.8 %all-to-all-start = ((f32[16,24,128]{2,1,0:T(8,128)}), f32[16,24,128]{2,1,0:T(8,128)}, u32[]{:S(2)}, u32[]{:S(2)}) async-start(f32[16,24,128]{2,1,0:T(8,128)} %blocks.1), calls=%async_computation | async-start | bytes 393216 | tf_op jit(solution)/shard_map/all_to_all | solution.py:788
  16.1 7.5 %collective-permute-start.3 = (f32[24,128]{1,0:T(8,128)S(1)}, f32[24,128]{1,0:T(8,128)S(1)}, u32[]{:S(2)}, u32[]{:S(2)}) collective-permute-start(f32[24,128]{1,0:T(8,128)S(1)} %corners.1), channel_id=1, source_target_pairs={{0,1},{1,0},{2,3},{3,2},{4,5},{5,4},{6,7},{7,6},{8,9},{9,8},{10,11... | collective-permute-start | bytes 36872 | tf_op jit(solution)/shard_map/ppermute | solution.py:769

commit v4 on v3

--- a/solution.py
+++ b/solution.py
@@ -407,28 +407,37 @@
     coef = (
         scale * jnp.where(row > 0, turn(wet, 1, 0), up(places.wet + TILE - 1, 1)),
         scale * jnp.where(row < rows - 1, turn(wet, -1, 0), down(places.wet, 1)),
-        scale * turn(jnp.where(last, wet_halo, wet), 1, 1),
-        scale * turn(jnp.where(first, wet_halo, wet), -1, 1),
-    )
-    centre_coef = 1.0 - (coef[0] + coef[1] + coef[2] + coef[3])
+        scale * jnp.where(first, 0.0, turn(wet, 1, 1)),
+        scale * jnp.where(last, 0.0, turn(wet, -1, 1)),
+    )
+    edge = first | last
+    weight = jnp.where(first, turn(wet_halo, 1, 1), turn(wet_halo, -1, 1))
+    weight = scale * jnp.where(edge, weight, 0.0)
+    centre_coef = 1.0 - (coef[0] + coef[1] + coef[2] + coef[3] + weight)
     even = lane % 2 == 0
     strip_at = (1 + n_tiles) * rows
-    side = merged([p[strip_at:, :] for p in parts], even, ~even, n_narrow)
+    came = merged([p[strip_at:, :] for p in parts], even, ~even, n_narrow)
+    came = jnp.where(even, turn(came, 1, 1), turn(came, -1, 1))
+    packed = [turn(weight[i : i + 1, :], 2 * i, 1) for i in range(rows)]
+    packed = functools.reduce(lambda a, b: a + b, packed)
+    packed = packed + turn(packed, 2 * rows, 1) + turn(packed, 4 * rows, 1)
+    side = packed * came
     writes = []
     for f in range(3):
-        for h in range(chunks):
-            reads[f * chunks + h].wait()
+        reads[f * chunks].wait()
         for h in range(chunks):
             for i in range(h * step, (h + 1) * step):
+                if i == (h + 1) * step - 1 and h < chunks - 1:
+                    reads[f * chunks + h + 1].wait()
                 centre = field[f, i]
-                halo = turn(side, -2 * (f * rows + i), 1)
                 above = field[f, i - 1] if i > 0 else up(f * levels, levels)
                 below = field[f, i + 1] if i < rows - 1 else down(f * levels, levels)
                 value = centre * centre_coef[i : i + 1, :]
                 value = value + above * coef[0][i : i + 1, :]
                 value = value + below * coef[1][i : i + 1, :]
-                value = value + turn(jnp.where(last, halo, centre), 1, 1) * coef[2][i : i + 1, :]
-                value = value + turn(jnp.where(first, halo, centre), -1, 1) * coef[3][i : i + 1, :]
+                value = value + turn(centre, 1, 1) * coef[2][i : i + 1, :]
+                value = value + turn(centre, -1, 1) * coef[3][i : i + 1, :]
+                value = value + jnp.where(edge, turn(side, -2 * (f * rows + i), 1), 0.0)
                 held[f, i] = value
                 if f == 2:
                     top[i] = value[0:TILE, :]
@@ -745,7 +754,7 @@
 
     n_tiles = ice_tiles(layers)
     places = Places(levels, layers)
-    chunks = 2
+    chunks = 1
     message, to_pair, to_cross, planes, ice = call(
         edges_kernel, "edges", 100.0,
         (

time: 28.3 us -> 27.6 us (0.975)
  Pallas kernels: 13.9 us -> 11.5 us
  waiting for transfers between devices: 1.58 us -> 3.45 us
    pallas_call x1, Pallas kernels: 5.87 us -> 3.68 us  [local(): call(functools.partial(ocean_kernel, n_narrow, n_parts, n_tiles, layers),...]
    all_to_all x1, waiting for transfers between devices: 0.01 us -> 1.87 us  [local(): lax.all_to_all(blocks, 'wide', split_axis=0, concat_axis=0, tiled=True)]
    pallas_call x1, Pallas kernels: 2.52 us -> 2.22 us  [local(): call(edges_kernel, 'edges', 100.0, (kept((1 + n_tiles) * rows + levels, L...]
  transfers between devices with their start and end apart: 5 -> 5, of which waited for: 1 -> 2; matrix products, arithmetic and copies ran while one was open for 0% -> 0% of each run, Pallas kernels for 31% -> 24%
where the time goes in v4:
time: 27.6 us; the launch traced here: 27.4 us
  starting transfers between devices  11.7 us (42%)
  Pallas kernels  11.5 us (42%)
  waiting for transfers between devices  3.45 us (12%)
  between operations  0.71 us (3%)
    all_to_all x1, starting transfers between devices, local(): lax.all_to_all(blocks, 'wide', split_axis=0, concat_axis=0, tiled=True)  6.45 us
    ppermute x2, starting transfers between devices, narrow(): return [lax.ppermute(value, 'narrow', [(0, 1), (1, 0)])]  4.63 us
    pallas_call x1, Pallas kernels, local(): call(functools.partial(ocean_kernel, n_narrow, n_parts, n_tiles, layers),...  3.68 us
    pallas_call x1, Pallas kernels, local(): call(functools.partial(final_kernel, n_wide, n_narrow, cap, block), 'fina...  2.64 us
    pallas_call x1, Pallas kernels, local(): call(edges_kernel, 'edges', 100.0, (kept((1 + n_tiles) * rows + levels, L...  2.22 us
    all_to_all x1, waiting for transfers between devices, local(): lax.all_to_all(blocks, 'wide', split_axis=0, concat_axis=0, tiled=True)  1.87 us
    pallas_call x1, Pallas kernels, local(): call(functools.partial(first_kernel, n_wide, n_narrow, cap, block, n_part...  1.75 us
    ppermute x2, waiting for transfers between devices, narrow(): return [lax.ppermute(value, 'narrow', [(0, 1), (1, 0)])]  1.57 us
  transfers between devices with their start and end apart: 5, of which 2 were waited for; matrix products, arithmetic and copies ran while one was open for 0% of the time, Pallas kernels for 24%

profile of v4, /device:TPU:0, one launch (start us, length us, event | category | flops | bytes accessed | tf_op | source)
XLA Modules:
  0.0 27.4 jit_solution(18353993201753416596)
XLA Ops:
  0.6 2.2 %edges.1 = (f32[128,128]{1,0:T(8,128)S(1)}, f32[392,128]{1,0:T(8,128)S(1)}, f32[392,128]{1,0:T(8,128)S(1)}, f32[6,16,128]{2,1,0:T(8,128)S(1)}, f32[3,10,16,128]{3,2,1,0:T(8,128)S(1)}) custom-call(f32[10,16,128]{2,1,0:T(8,128)} %bitcast.6, f32[10,16,128]{2,1,0:T(8,128)} %bitcast.7, f32[10,16,128]{2,1,0:T(8,128)} %bitcast.8, f32[16,80,128]{2,1,0:T(8,128)} %refs_1_.1, ...), custom_call_target="tpu_custom_call" | custom-call | flops 99999997952 | bytes 300000000 | tf_op jit(solution)/shard_map/edges/pallas_call | solution.py:758
  2.9 3.0 %collective-permute-start = (f32[128,128]{1,0:T(8,128)S(1)}, f32[128,128]{1,0:T(8,128)S(1)}, u32[]{:S(2)}, u32[]{:S(2)}) collective-permute-start(f32[128,128]{1,0:T(8,128)S(1)} %get-tuple-element.21), channel_id=1, source_target_pairs={{0,1},{1,0},{2,3},{3,2},{4,5},{5,4},{6,7},{7,6},{8,9},{9,8},{10,11... | collective-permute-start | bytes 196616 | tf_op jit(solution)/shard_map/ppermute | solution.py:778
  5.9 0.0 collective-permute-start.1
  5.9 0.7 %collective-permute-start.2 = (f32[392,128]{1,0:T(8,128)S(1)}, f32[392,128]{1,0:T(8,128)S(1)}, u32[]{:S(2)}, u32[]{:S(2)}) collective-permute-start(f32[392,128]{1,0:T(8,128)S(1)} %get-tuple-element.24), channel_id=1, source_target_pairs={{2,4},{6,8},{10,12},{14,16},{18,20},{22,24},{26,28},{4,2},{8,6},{1... | collective-permute-start | bytes 602120 | tf_op jit(solution)/shard_map/ppermute | solution.py:790
  6.6 1.6 %collective-permute-done.refs_0_ = f32[128,128]{1,0:T(8,128)S(1)} collective-permute-done((f32[128,128]{1,0:T(8,128)S(1)}, f32[128,128]{1,0:T(8,128)S(1)}, u32[]{:S(2)}, u32[]{:S(2)}) %collective-permute-start) | collective-permute-done | bytes 65568 | tf_op jit(solution)/shard_map/ppermute | solution.py:778
  8.1 1.1 %blocks.1 = f32[16,24,128]{2,1,0:T(8,128)} custom-call(f32[128,128]{1,0:T(8,128)S(1)} %collective-permute-done.refs_0_, f32[6,16,128]{2,1,0:T(8,128)S(1)} %get-tuple-element.22.refs_1_.refs_5_.refs_6_.refs_3_), custom_call_target="tpu_custom_call" | custom-call | flops 99999997952 | bytes 300000000 | tf_op jit(solution)/shard_map/blocks/pallas_call | solution.py:793
  9.2 6.5 %all-to-all-start = ((f32[16,24,128]{2,1,0:T(8,128)}), f32[16,24,128]{2,1,0:T(8,128)}, u32[]{:S(2)}, u32[]{:S(2)}) async-start(f32[16,24,128]{2,1,0:T(8,128)} %blocks.1), calls=%async_computation | async-start | bytes 393216 | tf_op jit(solution)/shard_map/all_to_all | solution.py:797
  15.7 0.0 collective-permute-done.1.pair.refs_3_.refs_4_
  15.7 0.0 collective-permute-done.2.cross.refs_4_.refs_5_
  15.7 0.1 corners.1
  15.8 1.6 %collective-permute-start.3 = (f32[24,128]{1,0:T(8,128)S(1)}, f32[24,128]{1,0:T(8,128)S(1)}, u32[]{:S(2)}, u32[]{:S(2)}) collective-permute-start(f32[24,128]{1,0:T(8,128)S(1)} %corners.1), channel_id=1, source_target_pairs={{0,1},{1,0},{2,3},{3,2},{4,5},{5,4},{6,7},{7,6},{8,9},{9,8},{10,11... | collective-permute-start | bytes 36872 | tf_op jit(solution)/shard_map/ppermute | solution.py:778
  17.4 3.7 %ocean.1 = (f32[3,16,80,128]{3,2,1,0:T(8,128)}, f32[16,8,128]{2,1,0:T(8,128)S(1)}) custom-call(f32[128,128]{1,0:T(8,128)S(1)} %collective-permute-done.refs_0_, f32[16,80,128]{2,1,0:T(8,128)} %refs_1_.1, f32[16,80,128]{2,1,0:T(8,128)} %refs_2_.1, f32[16,80,128]{2,1,0:T(8,128)} %refs_3_.1, f32[392,128]{1,0:T(8,128)S(1)} %collective-permute-done.1.pair.refs_3_.refs_4_, ...), custom_call_target="tpu_custom_call" | custom-call | flops 99999997952 | bytes 300000000 | tf_op jit(solution)/shard_map/ocean/pallas_call | solution.py:804
  21.1 0.0 collective-permute-done.3.refs_1_
  21.1 1.7 %first.1 = (f32[2,10,24,256]{3,2,1,0:T(8,128)S(1)}, f32[10,24,256]{2,1,0:T(8,128)S(1)}, f32[10,24,256]{2,1,0:T(8,128)S(1)}, f32[3,24,256]{2,1,0:T(8,128)S(1)}, f...) custom-call(f32[128,128]{1,0:T(8,128)S(1)} %collective-permute-done.refs_0_, ...), custom_call_target="tpu_custom_call" | custom-call | flops 99999997952 | bytes 300000000 | tf_op jit(solution)/shard_map/first/pallas_call | solution.py:817
  22.8 1.9 %all-to-all-done.refs_0_ = f32[16,24,128]{2,1,0:T(8,128)} async-done(((f32[16,24,128]{2,1,0:T(8,128)}), f32[16,24,128]{2,1,0:T(8,128)}, u32[]{:S(2)}, u32[]{:S(2)}) %all-to-all-start) | async-done | bytes 196640 | tf_op jit(solution)/shard_map/all_to_all | solution.py:797
  24.7 2.6 %final.1 = (f32[3,10,16,128]{3,2,1,0:T(8,128)}, f32[3,16,80,128]{3,2,1,0:T(8,128)}, f32[16,128]{1,0:T(8,128)}, f32[16,128]{1,0:T(8,128)}) custom-call(f32[16,24,128]{2,1,0:T(8,128)} %all-to-all-done.refs_0_, f32[160,128]{1,0:T(8,128)S(1)} %get-tuple-element.26.refs_1_, ...), custom_call_target="tpu_custom_call", output_to_operand_aliasing={{1}: (10, {})} | custom-call | flops 3000000000 | bytes 9000000 | tf_op jit(solution)/shard_map/final/pallas_call | solution.py:826
Async XLA Ops:
  2.9 5.3 %collective-permute-start = (f32[128,128]{1,0:T(8,128)S(1)}, f32[128,128]{1,0:T(8,128)S(1)}, u32[]{:S(2)}, u32[]{:S(2)}) collective-permute-start(f32[128,128]{1,0:T(8,128)S(1)} %get-tuple-element.21), channel_id=1, source_target_pairs={{0,1},{1,0},{2,3},{3,2},{4,5},{5,4},{6,7},{7,6},{8,9},{9,8},{10,11... | collective-permute-start | bytes 196616 | tf_op jit(solution)/shard_map/ppermute | solution.py:778
  5.9 9.8 %collective-permute-start.1 = (f32[392,128]{1,0:T(8,128)S(1)}, f32[392,128]{1,0:T(8,128)S(1)}, u32[]{:S(2)}, u32[]{:S(2)}) collective-permute-start(f32[392,128]{1,0:T(8,128)S(1)} %get-tuple-element.23), channel_id=1, source_target_pairs={{0,2},{4,6},{8,10},{12,14},{16,18},{20,22},{24,26},{28,30},{2,0},{... | collective-permute-start | bytes 602120 | tf_op jit(solution)/shard_map/ppermute | solution.py:790
  5.9 9.8 %collective-permute-start.2 = (f32[392,128]{1,0:T(8,128)S(1)}, f32[392,128]{1,0:T(8,128)S(1)}, u32[]{:S(2)}, u32[]{:S(2)}) collective-permute-start(f32[392,128]{1,0:T(8,128)S(1)} %get-tuple-element.24), channel_id=1, source_target_pairs={{2,4},{6,8},{10,12},{14,16},{18,20},{22,24},{26,28},{4,2},{8,6},{1... | collective-permute-start | bytes 602120 | tf_op jit(solution)/shard_map/ppermute | solution.py:790
  9.2 15.5 %all-to-all-start = ((f32[16,24,128]{2,1,0:T(8,128)}), f32[16,24,128]{2,1,0:T(8,128)}, u32[]{:S(2)}, u32[]{:S(2)}) async-start(f32[16,24,128]{2,1,0:T(8,128)} %blocks.1), calls=%async_computation | async-start | bytes 393216 | tf_op jit(solution)/shard_map/all_to_all | solution.py:797
  15.8 5.3 %collective-permute-start.3 = (f32[24,128]{1,0:T(8,128)S(1)}, f32[24,128]{1,0:T(8,128)S(1)}, u32[]{:S(2)}, u32[]{:S(2)}) collective-permute-start(f32[24,128]{1,0:T(8,128)S(1)} %corners.1), channel_id=1, source_target_pairs={{0,1},{1,0},{2,3},{3,2},{4,5},{5,4},{6,7},{7,6},{8,9},{9,8},{10,11... | collective-permute-start | bytes 36872 | tf_op jit(solution)/shard_map/ppermute | solution.py:778

commit v5 on v4

--- a/solution.py
+++ b/solution.py
@@ -17,6 +17,7 @@
 
 LANES = 128
 TILE = 8
+ORDER = (2, 1, 3, 0)
 HALO = 4
 RIM = 3
 VMEM = pltpu.CompilerParams(vmem_limit_bytes=16 * 1024 * 1024)
@@ -287,6 +288,13 @@
     return (place == target).astype(F32)[:, :rows]
 
 
+def exchange_order(n_wide):
+    quarter = n_wide // 4
+    if n_wide % 4:
+        return list(range(n_wide))
+    return [q * quarter + j for q in ORDER for j in reversed(range(quarter))]
+
+
 def blocks_kernel(n_wide, n_narrow, cap, block, n_parts, *refs):
     parts, refs = refs[:n_parts], refs[n_parts:]
     planes, blocks = refs
@@ -346,7 +354,8 @@
         jnp.where(slot == 3 * cap + 1, warm[last:, :LANES], third + ends),
     )
     for k, value in enumerate((first, second, third)):
-        blocks[:, k * block : (k + 1) * block, :] = value.reshape(n_wide, block, LANES)
+        for j, tile in enumerate(exchange_order(n_wide)):
+            blocks[j, k * block : (k + 1) * block, :] = value[tile * block : (tile + 1) * block, :]
 
 
 def beyond_ice(up, down, places, layers, f, k):
@@ -624,9 +633,12 @@
     _, layers, rows, _ = ice.shape
     tall, width = flat.shape[1:]
     lane = iota((1, LANES), 1)
-    count = n_wide * block
+    order = exchange_order(n_wide)
     parts = [
-        blocks[:, n * block : (n + 1) * block, :].reshape(count, LANES) for n in range(3)
+        jnp.concatenate(
+            [blocks[order.index(t), n * block : (n + 1) * block, :] for t in range(n_wide)], axis=0
+        )
+        for n in range(3)
     ]
     found = pick(hots[...], jnp.concatenate(parts, axis=1))
 
@@ -756,7 +768,7 @@
     places = Places(levels, layers)
     chunks = 1
     message, to_pair, to_cross, planes, ice = call(
-        edges_kernel, "edges", 100.0,
+        edges_kernel, "edges", 4.0,
         (
             kept((1 + n_tiles) * rows + levels, LANES), kept(places.end, LANES), kept(places.end, LANES),
             kept(PLANES, rows, LANES), kept(3, layers, rows, LANES),
@@ -791,10 +803,12 @@
         for value, swap in zip((to_pair, to_cross), swaps)
     )
     blocks = call(
-        functools.partial(blocks_kernel, n_wide, n_narrow, cap, block, n_parts), "blocks", 100.0,
+        functools.partial(blocks_kernel, n_wide, n_narrow, cap, block, n_parts), "blocks", 4.0,
         kept(n_wide, 3 * block, LANES), [here] * (n_parts + 1), here,
     )(*near(*parts, planes))
-    blocks = lax.all_to_all(blocks, "wide", split_axis=0, concat_axis=0, tiled=True)
+    blocks = lax.all_to_all(
+        blocks, "wide", split_axis=0, concat_axis=0, tiled=True, axis_index_groups=[exchange_order(n_wide)]
+    )
     corners = narrow(
         call(
             functools.partial(corners_kernel, levels, layers), "corners", 1.0,
@@ -802,7 +816,7 @@
         )(*near(pair, cross))
     )
     ocean, top = call(
-        functools.partial(ocean_kernel, n_narrow, n_parts, n_tiles, layers), "ocean", 100.0,
+        functools.partial(ocean_kernel, n_narrow, n_parts, n_tiles, layers), "ocean", 4.0,
         (array(3, rows, levels, LANES), kept(rows, TILE, LANES)),
         [here] * n_parts + [far] * 3 + [here] * 3, (far, here),
         [
@@ -815,7 +829,7 @@
     tall = rows + TILE
     n_sides = 1 if n_narrow == 2 else 2
     sums, inverse, rate, flat, hots, ends = call(
-        functools.partial(first_kernel, n_wide, n_narrow, cap, block, n_parts, levels), "first", 100.0,
+        functools.partial(first_kernel, n_wide, n_narrow, cap, block, n_parts, levels), "first", 4.0,
         (
             kept(2, layers, tall, wide), kept(layers, tall, wide), kept(layers, tall, wide), kept(3, tall, wide),
             kept((3 + 3 * n_sides) * tall + rows, n_wide * block), kept(n_sides, tall, LANES),

time: 27.6 us -> 25.3 us (0.917)
  waiting for transfers between devices: 3.45 us -> 1.58 us
  Pallas kernels: 11.5 us -> 10.6 us
  starting transfers between devices: 11.7 us -> 12.2 us
    all_to_all x1, waiting for transfers between devices: 1.87 us -> 0.01 us  [local(): lax.all_to_all(blocks, 'wide', split_axis=0, concat_axis=0, tiled=True, a...]
    all_to_all x1, starting transfers between devices: 6.45 us -> 7.89 us  [local(): lax.all_to_all(blocks, 'wide', split_axis=0, concat_axis=0, tiled=True, a...]
    ppermute x2, starting transfers between devices: 4.63 us -> 3.6 us  [narrow(): return [lax.ppermute(value, 'narrow', [(0, 1), (1, 0)])]]
    pallas_call x1, Pallas kernels: 2.64 us -> 1.77 us  [local(): call(functools.partial(final_kernel, n_wide, n_narrow, cap, block), 'fina...]
  transfers between devices with their start and end apart: 5 -> 5, of which waited for: 2 -> 1; matrix products, arithmetic and copies ran while one was open for 0% -> 0% of each run, Pallas kernels for 24% -> 26%
where the time goes in v5:
time: 25.3 us; the launch traced here: 25 us
  starting transfers between devices  12.2 us (48%)
  Pallas kernels  10.6 us (42%)
  waiting for transfers between devices  1.58 us (6%)
  between operations  0.7 us (3%)
    all_to_all x1, starting transfers between devices, local(): lax.all_to_all(blocks, 'wide', split_axis=0, concat_axis=0, tiled=True, a...  7.89 us
    pallas_call x1, Pallas kernels, local(): call(functools.partial(ocean_kernel, n_narrow, n_parts, n_tiles, layers),...  3.68 us
    ppermute x2, starting transfers between devices, narrow(): return [lax.ppermute(value, 'narrow', [(0, 1), (1, 0)])]  3.6 us
    pallas_call x1, Pallas kernels, local(): call(edges_kernel, 'edges', 4.0, (kept((1 + n_tiles) * rows + levels, LAN...  2.22 us
    pallas_call x1, Pallas kernels, local(): call(functools.partial(final_kernel, n_wide, n_narrow, cap, block), 'fina...  1.77 us
    pallas_call x1, Pallas kernels, local(): call(functools.partial(first_kernel, n_wide, n_narrow, cap, block, n_part...  1.75 us
    ppermute x2, waiting for transfers between devices, narrow(): return [lax.ppermute(value, 'narrow', [(0, 1), (1, 0)])]  1.57 us
    pallas_call x1, Pallas kernels, local(): call(functools.partial(blocks_kernel, n_wide, n_narrow, cap, block, n_par...  1.06 us
  transfers between devices with their start and end apart: 5, of which 1 were waited for; matrix products, arithmetic and copies ran while one was open for 0% of the time, Pallas kernels for 26%

profile of v5, /device:TPU:0, one launch (start us, length us, event | category | flops | bytes accessed | tf_op | source)
XLA Modules:
  0.0 25.0 jit_solution(4382807240867286948)
XLA Ops:
  0.6 2.2 %edges.1 = (f32[128,128]{1,0:T(8,128)S(1)}, f32[392,128]{1,0:T(8,128)S(1)}, f32[392,128]{1,0:T(8,128)S(1)}, f32[6,16,128]{2,1,0:T(8,128)S(1)}, f32[3,10,16,128]{3,2,1,0:T(8,128)S(1)}) custom-call(f32[10,16,128]{2,1,0:T(8,128)} %bitcast.6, f32[10,16,128]{2,1,0:T(8,128)} %bitcast.7, f32[10,16,128]{2,1,0:T(8,128)} %bitcast.8, f32[16,80,128]{2,1,0:T(8,128)} %refs_1_.1, ...), custom_call_target="tpu_custom_call" | custom-call | flops 4000000000 | bytes 12000000 | tf_op jit(solution)/shard_map/edges/pallas_call | solution.py:770
  2.9 3.0 %collective-permute-start = (f32[128,128]{1,0:T(8,128)S(1)}, f32[128,128]{1,0:T(8,128)S(1)}, u32[]{:S(2)}, u32[]{:S(2)}) collective-permute-start(f32[128,128]{1,0:T(8,128)S(1)} %get-tuple-element.21), channel_id=1, source_target_pairs={{0,1},{1,0},{2,3},{3,2},{4,5},{5,4},{6,7},{7,6},{8,9},{9,8},{10,11... | collective-permute-start | bytes 196616 | tf_op jit(solution)/shard_map/ppermute | solution.py:790
  5.9 0.0 collective-permute-start.1
  5.9 0.7 %collective-permute-start.2 = (f32[392,128]{1,0:T(8,128)S(1)}, f32[392,128]{1,0:T(8,128)S(1)}, u32[]{:S(2)}, u32[]{:S(2)}) collective-permute-start(f32[392,128]{1,0:T(8,128)S(1)} %get-tuple-element.24), channel_id=1, source_target_pairs={{2,4},{6,8},{10,12},{14,16},{18,20},{22,24},{26,28},{4,2},{8,6},{1... | collective-permute-start | bytes 602120 | tf_op jit(solution)/shard_map/ppermute | solution.py:802
  6.6 1.6 %collective-permute-done.refs_0_ = f32[128,128]{1,0:T(8,128)S(1)} collective-permute-done((f32[128,128]{1,0:T(8,128)S(1)}, f32[128,128]{1,0:T(8,128)S(1)}, u32[]{:S(2)}, u32[]{:S(2)}) %collective-permute-start) | collective-permute-done | bytes 65568 | tf_op jit(solution)/shard_map/ppermute | solution.py:790
  8.1 1.1 %blocks.1 = f32[16,24,128]{2,1,0:T(8,128)} custom-call(f32[128,128]{1,0:T(8,128)S(1)} %collective-permute-done.refs_0_, f32[6,16,128]{2,1,0:T(8,128)S(1)} %get-tuple-element.22.refs_1_.refs_5_.refs_6_.refs_3_), custom_call_target="tpu_custom_call" | custom-call | flops 4000000000 | bytes 12000000 | tf_op jit(solution)/shard_map/blocks/pallas_call | solution.py:805
  9.2 7.9 %all-to-all-start = ((f32[16,24,128]{2,1,0:T(8,128)}), f32[16,24,128]{2,1,0:T(8,128)S(1)}, u32[]{:S(2)}, u32[]{:S(2)}) async-start(f32[16,24,128]{2,1,0:T(8,128)} %blocks.1), calls=%async_computation | async-start | bytes 393216 | tf_op jit(solution)/shard_map/all_to_all | solution.py:809
  17.1 0.0 collective-permute-done.1.pair.refs_3_.refs_4_
  17.1 0.0 collective-permute-done.2.cross.refs_4_.refs_5_
  17.1 0.1 corners.1
  17.2 0.6 %collective-permute-start.3 = (f32[24,128]{1,0:T(8,128)S(1)}, f32[24,128]{1,0:T(8,128)S(1)}, u32[]{:S(2)}, u32[]{:S(2)}) collective-permute-start(f32[24,128]{1,0:T(8,128)S(1)} %corners.1), channel_id=1, source_target_pairs={{0,1},{1,0},{2,3},{3,2},{4,5},{5,4},{6,7},{7,6},{8,9},{9,8},{10,11... | collective-permute-start | bytes 36872 | tf_op jit(solution)/shard_map/ppermute | solution.py:790
  17.8 3.7 %ocean.1 = (f32[3,16,80,128]{3,2,1,0:T(8,128)}, f32[16,8,128]{2,1,0:T(8,128)S(1)}) custom-call(f32[128,128]{1,0:T(8,128)S(1)} %collective-permute-done.refs_0_, f32[16,80,128]{2,1,0:T(8,128)} %refs_1_.1, f32[16,80,128]{2,1,0:T(8,128)} %refs_2_.1, f32[16,80,128]{2,1,0:T(8,128)} %refs_3_.1, f32[392,128]{1,0:T(8,128)S(1)} %collective-permute-done.1.pair.refs_3_.refs_4_, ...), custom_call_target="tpu_custom_call" | custom-call | flops 4000000000 | bytes 12000000 | tf_op jit(solution)/shard_map/ocean/pallas_call | solution.py:818
  21.5 0.0 collective-permute-done.3.refs_1_
  21.5 1.7 %first.1 = (f32[2,10,24,256]{3,2,1,0:T(8,128)S(1)}, f32[10,24,256]{2,1,0:T(8,128)S(1)}, f32[10,24,256]{2,1,0:T(8,128)S(1)}, f32[3,24,256]{2,1,0:T(8,128)S(1)}, f...) custom-call(f32[128,128]{1,0:T(8,128)S(1)} %collective-permute-done.refs_0_, ...), custom_call_target="tpu_custom_call" | custom-call | flops 4000000000 | bytes 12000000 | tf_op jit(solution)/shard_map/first/pallas_call | solution.py:831
  23.2 0.0 all-to-all-done.refs_0_
  23.3 1.8 %final.1 = (f32[3,10,16,128]{3,2,1,0:T(8,128)}, f32[3,16,80,128]{3,2,1,0:T(8,128)}, f32[16,128]{1,0:T(8,128)}, f32[16,128]{1,0:T(8,128)}) custom-call(f32[16,24,128]{2,1,0:T(8,128)S(1)} %all-to-all-done.refs_0_, f32[160,128]{1,0:T(8,128)S(1)} %get-tuple-element.26.refs_1_, ...), custom_call_target="tpu_custom_call", output_to_operand_aliasing={{1}: (10, {})} | custom-call | flops 3000000000 | bytes 9000000 | tf_op jit(solution)/shard_map/final/pallas_call | solution.py:840
Async XLA Ops:
  2.9 5.3 %collective-permute-start = (f32[128,128]{1,0:T(8,128)S(1)}, f32[128,128]{1,0:T(8,128)S(1)}, u32[]{:S(2)}, u32[]{:S(2)}) collective-permute-start(f32[128,128]{1,0:T(8,128)S(1)} %get-tuple-element.21), channel_id=1, source_target_pairs={{0,1},{1,0},{2,3},{3,2},{4,5},{5,4},{6,7},{7,6},{8,9},{9,8},{10,11... | collective-permute-start | bytes 196616 | tf_op jit(solution)/shard_map/ppermute | solution.py:790
  5.9 11.2 %collective-permute-start.1 = (f32[392,128]{1,0:T(8,128)S(1)}, f32[392,128]{1,0:T(8,128)S(1)}, u32[]{:S(2)}, u32[]{:S(2)}) collective-permute-start(f32[392,128]{1,0:T(8,128)S(1)} %get-tuple-element.23), channel_id=1, source_target_pairs={{0,2},{4,6},{8,10},{12,14},{16,18},{20,22},{24,26},{28,30},{2,0},{... | collective-permute-start | bytes 602120 | tf_op jit(solution)/shard_map/ppermute | solution.py:802
  5.9 11.2 %collective-permute-start.2 = (f32[392,128]{1,0:T(8,128)S(1)}, f32[392,128]{1,0:T(8,128)S(1)}, u32[]{:S(2)}, u32[]{:S(2)}) collective-permute-start(f32[392,128]{1,0:T(8,128)S(1)} %get-tuple-element.24), channel_id=1, source_target_pairs={{2,4},{6,8},{10,12},{14,16},{18,20},{22,24},{26,28},{4,2},{8,6},{1... | collective-permute-start | bytes 602120 | tf_op jit(solution)/shard_map/ppermute | solution.py:802
  9.2 14.0 %all-to-all-start = ((f32[16,24,128]{2,1,0:T(8,128)}), f32[16,24,128]{2,1,0:T(8,128)S(1)}, u32[]{:S(2)}, u32[]{:S(2)}) async-start(f32[16,24,128]{2,1,0:T(8,128)} %blocks.1), calls=%async_computation | async-start | bytes 393216 | tf_op jit(solution)/shard_map/all_to_all | solution.py:809
  17.2 4.3 %collective-permute-start.3 = (f32[24,128]{1,0:T(8,128)S(1)}, f32[24,128]{1,0:T(8,128)S(1)}, u32[]{:S(2)}, u32[]{:S(2)}) collective-permute-start(f32[24,128]{1,0:T(8,128)S(1)} %corners.1), channel_id=1, source_target_pairs={{0,1},{1,0},{2,3},{3,2},{4,5},{5,4},{6,7},{7,6},{8,9},{9,8},{10,11... | collective-permute-start | bytes 36872 | tf_op jit(solution)/shard_map/ppermute | solution.py:790

commit v6 on v5

--- a/solution.py
+++ b/solution.py
@@ -17,7 +17,7 @@
 
 LANES = 128
 TILE = 8
-ORDER = (2, 1, 3, 0)
+ORDER = (2, 3, 0, 1)
 HALO = 4
 RIM = 3
 VMEM = pltpu.CompilerParams(vmem_limit_bytes=16 * 1024 * 1024)
@@ -393,19 +393,11 @@
 
 def ocean_kernel(n_narrow, n_parts, n_tiles, layers, *refs):
     parts, refs = refs[:n_parts], refs[n_parts:]
-    ocean_x, ocean_y, ocean_t, pair, cross, planes, out, top, field, held, sems = refs
-    rows, levels, _ = ocean_x.shape
+    field, pair, cross, planes, out, top, held, sems = refs
+    _, rows, levels, _ = field.shape
     places = Places(levels, layers)
-    chunks = sems.shape[0] // 6
+    chunks = sems.shape[0] // 3
     step = rows // chunks
-    reads = fetch_all(
-        [
-            (source.at[pl.ds(h * step, step)], field.at[f, pl.ds(h * step, step)])
-            for f, source in enumerate((ocean_x, ocean_y, ocean_t))
-            for h in range(chunks)
-        ],
-        sems,
-    )
     up, down = came_from(pair, cross)
     lane = iota((1, LANES), 1)
     row = iota((rows, LANES), 0)
@@ -433,11 +425,8 @@
     side = packed * came
     writes = []
     for f in range(3):
-        reads[f * chunks].wait()
         for h in range(chunks):
             for i in range(h * step, (h + 1) * step):
-                if i == (h + 1) * step - 1 and h < chunks - 1:
-                    reads[f * chunks + h + 1].wait()
                 centre = field[f, i]
                 above = field[f, i - 1] if i > 0 else up(f * levels, levels)
                 below = field[f, i + 1] if i < rows - 1 else down(f * levels, levels)
@@ -455,7 +444,7 @@
             copy = pltpu.make_async_copy(
                 held.at[f, part, level],
                 out.at[f, part, level],
-                sems.at[(3 + f) * chunks + h],
+                sems.at[f * chunks + h],
             )
             copy.start()
             writes.append(copy)
@@ -767,15 +756,14 @@
     n_tiles = ice_tiles(layers)
     places = Places(levels, layers)
     chunks = 1
-    message, to_pair, to_cross, planes, ice = call(
+    message, to_pair, to_cross, planes, ice, field = call(
         edges_kernel, "edges", 4.0,
         (
             kept((1 + n_tiles) * rows + levels, LANES), kept(places.end, LANES), kept(places.end, LANES),
-            kept(PLANES, rows, LANES), kept(3, layers, rows, LANES),
+            kept(PLANES, rows, LANES), kept(3, layers, rows, LANES), kept(3, rows, levels, LANES),
         ),
-        [far] * 11, (here,) * 5,
+        [far] * 11, (here,) * 6,
         [
-            pltpu.VMEM((3, rows, levels, LANES), F32),
             pltpu.VMEM((rows, LANES), F32),
             pltpu.VMEM((rows, LANES), jnp.int32),
             pltpu.VMEM((rows, LANES), jnp.int32),
@@ -818,13 +806,12 @@
     ocean, top = call(
         functools.partial(ocean_kernel, n_narrow, n_parts, n_tiles, layers), "ocean", 4.0,
         (array(3, rows, levels, LANES), kept(rows, TILE, LANES)),
-        [here] * n_parts + [far] * 3 + [here] * 3, (far, here),
+        [here] * (n_parts + 4), (far, here),
         [
             pltpu.VMEM((3, rows, levels, LANES), F32),
-            pltpu.VMEM((3, rows, levels, LANES), F32),
-            dma((6 * chunks,)),
+            dma((3 * chunks,)),
         ],
-    )(*near(*parts), *fields, *near(pair, cross, planes))
+    )(*near(*parts, field, pair, cross, planes))
     wide = 2 * LANES
     tall = rows + TILE
     n_sides = 1 if n_narrow == 2 else 2

time: 25.3 us -> 24.7 us (0.976)
  Pallas kernels: 10.6 us -> 9.47 us
  waiting for transfers between devices: 1.58 us -> 2.19 us
    pallas_call x1, Pallas kernels: 3.68 us -> 2.57 us  [local(): call(functools.partial(ocean_kernel, n_narrow, n_parts, n_tiles, layers),...]
    ppermute x2, waiting for transfers between devices: 1.57 us -> 2.18 us  [narrow(): return [lax.ppermute(value, 'narrow', [(0, 1), (1, 0)])]]
  transfers between devices with their start and end apart: 5 -> 5, of which waited for: 1 -> 2; matrix products, arithmetic and copies ran while one was open for 0% -> 0% of each run, Pallas kernels for 26% -> 22%
where the time goes in v6:
time: 24.7 us; the launch traced here: 24.5 us
  starting transfers between devices  12.1 us (49%)
  Pallas kernels  9.47 us (38%)
  waiting for transfers between devices  2.19 us (9%)
  between operations  0.7 us (3%)
    all_to_all x1, starting transfers between devices, local(): lax.all_to_all(blocks, 'wide', split_axis=0, concat_axis=0, tiled=True, a...  7.87 us
    ppermute x2, starting transfers between devices, narrow(): return [lax.ppermute(value, 'narrow', [(0, 1), (1, 0)])]  3.6 us
    pallas_call x1, Pallas kernels, local(): call(functools.partial(ocean_kernel, n_narrow, n_parts, n_tiles, layers),...  2.57 us
    pallas_call x1, Pallas kernels, local(): call(edges_kernel, 'edges', 4.0, (kept((1 + n_tiles) * rows + levels, LAN...  2.23 us
    ppermute x2, waiting for transfers between devices, narrow(): return [lax.ppermute(value, 'narrow', [(0, 1), (1, 0)])]  2.18 us
    pallas_call x1, Pallas kernels, local(): call(functools.partial(final_kernel, n_wide, n_narrow, cap, block), 'fina...  1.77 us
    pallas_call x1, Pallas kernels, local(): call(functools.partial(first_kernel, n_wide, n_narrow, cap, block, n_part...  1.74 us
    pallas_call x1, Pallas kernels, local(): call(functools.partial(blocks_kernel, n_wide, n_narrow, cap, block, n_par...  1.06 us
  transfers between devices with their start and end apart: 5, of which 2 were waited for; matrix products, arithmetic and copies ran while one was open for 0% of the time, Pallas kernels for 22%

profile of v6, /device:TPU:0, one launch (start us, length us, event | category | flops | bytes accessed | tf_op | source)
XLA Modules:
  0.0 24.5 jit_solution(14270409945431503512)
XLA Ops:
  0.6 2.2 %edges.1 = (f32[128,128]{1,0:T(8,128)S(1)}, f32[392,128]{1,0:T(8,128)S(1)}, f32[392,128]{1,0:T(8,128)S(1)}, f32[6,16,128]{2,1,0:T(8,128)S(1)}, f32[3,10,16,128]{...) custom-call(f32[10,16,128]{2,1,0:T(8,128)} %bitcast.6, f32[10,16,128]{2,1,0:T(8,128)} %bitcast.7, f32[10,16,128]{2,1,0:T(8,128)} %bitcast.8, ...), custom_call_target="tpu_custom_call" | custom-call | flops 4000000000 | bytes 12000000 | tf_op jit(solution)/shard_map/edges/pallas_call | solution.py:759
  2.9 3.0 %collective-permute-start = (f32[128,128]{1,0:T(8,128)S(1)}, f32[128,128]{1,0:T(8,128)S(1)}, u32[]{:S(2)}, u32[]{:S(2)}) collective-permute-start(f32[128,128]{1,0:T(8,128)S(1)} %get-tuple-element.22), channel_id=1, source_target_pairs={{0,1},{1,0},{2,3},{3,2},{4,5},{5,4},{6,7},{7,6},{8,9},{9,8},{10,11... | collective-permute-start | bytes 196616 | tf_op jit(solution)/shard_map/ppermute | solution.py:778
  5.9 0.0 collective-permute-start.1
  5.9 0.7 %collective-permute-start.2 = (f32[392,128]{1,0:T(8,128)S(1)}, f32[392,128]{1,0:T(8,128)S(1)}, u32[]{:S(2)}, u32[]{:S(2)}) collective-permute-start(f32[392,128]{1,0:T(8,128)S(1)} %get-tuple-element.25), channel_id=1, source_target_pairs={{2,4},{6,8},{10,12},{14,16},{18,20},{22,24},{26,28},{4,2},{8,6},{1... | collective-permute-start | bytes 602120 | tf_op jit(solution)/shard_map/ppermute | solution.py:790
  6.6 1.6 %collective-permute-done.refs_0_ = f32[128,128]{1,0:T(8,128)S(1)} collective-permute-done((f32[128,128]{1,0:T(8,128)S(1)}, f32[128,128]{1,0:T(8,128)S(1)}, u32[]{:S(2)}, u32[]{:S(2)}) %collective-permute-start) | collective-permute-done | bytes 65568 | tf_op jit(solution)/shard_map/ppermute | solution.py:778
  8.1 1.1 %blocks.1 = f32[16,24,128]{2,1,0:T(8,128)} custom-call(f32[128,128]{1,0:T(8,128)S(1)} %collective-permute-done.refs_0_, f32[6,16,128]{2,1,0:T(8,128)S(1)} %get-tuple-element.23.refs_1_.refs_5_.refs_4_.refs_3_), custom_call_target="tpu_custom_call" | custom-call | flops 4000000000 | bytes 12000000 | tf_op jit(solution)/shard_map/blocks/pallas_call | solution.py:793
  9.2 7.9 %all-to-all-start = ((f32[16,24,128]{2,1,0:T(8,128)}), f32[16,24,128]{2,1,0:T(8,128)S(1)}, u32[]{:S(2)}, u32[]{:S(2)}) async-start(f32[16,24,128]{2,1,0:T(8,128)} %blocks.1), calls=%async_computation | async-start | bytes 393216 | tf_op jit(solution)/shard_map/all_to_all | solution.py:797
  17.1 0.0 collective-permute-done.1.pair.refs_3_.refs_2_
  17.1 0.0 collective-permute-done.2.cross.refs_4_.refs_3_
  17.1 0.1 corners.1
  17.2 0.6 %collective-permute-start.3 = (f32[24,128]{1,0:T(8,128)S(1)}, f32[24,128]{1,0:T(8,128)S(1)}, u32[]{:S(2)}, u32[]{:S(2)}) collective-permute-start(f32[24,128]{1,0:T(8,128)S(1)} %corners.1), channel_id=1, source_target_pairs={{0,1},{1,0},{2,3},{3,2},{4,5},{5,4},{6,7},{7,6},{8,9},{9,8},{10,11... | collective-permute-start | bytes 36872 | tf_op jit(solution)/shard_map/ppermute | solution.py:778
  17.8 2.6 %ocean.1 = (f32[3,16,80,128]{3,2,1,0:T(8,128)}, f32[16,8,128]{2,1,0:T(8,128)S(1)}) custom-call(f32[128,128]{1,0:T(8,128)S(1)} %collective-permute-done.refs_0_, f32[3,16,80,128]{3,2,1,0:T(8,128)S(1)} %get-tuple-element.29.refs_1_, f32[392,128]{1,0:T(8,128)S(1)} %collective-permute-done.1.pair.refs_3_.refs_2_, ...), custom_call_target="tpu_custom_call" | custom-call | flops 4000000000 | bytes 12000000 | tf_op jit(solution)/shard_map/ocean/pallas_call | solution.py:806
  20.4 0.6 %collective-permute-done.3.refs_1_ = f32[24,128]{1,0:T(8,128)S(1)} collective-permute-done((f32[24,128]{1,0:T(8,128)S(1)}, f32[24,128]{1,0:T(8,128)S(1)}, u32[]{:S(2)}, u32[]{:S(2)}) %collective-permute-start.3) | collective-permute-done | bytes 12320 | tf_op jit(solution)/shard_map/ppermute | solution.py:778
  21.0 1.7 %first.1 = (f32[2,10,24,256]{3,2,1,0:T(8,128)S(1)}, f32[10,24,256]{2,1,0:T(8,128)S(1)}, f32[10,24,256]{2,1,0:T(8,128)S(1)}, f32[3,24,256]{2,1,0:T(8,128)S(1)}, f...) custom-call(f32[128,128]{1,0:T(8,128)S(1)} %collective-permute-done.refs_0_, ...), custom_call_target="tpu_custom_call" | custom-call | flops 4000000000 | bytes 12000000 | tf_op jit(solution)/shard_map/first/pallas_call | solution.py:818
  22.7 0.0 all-to-all-done.refs_0_
  22.7 1.8 %final.1 = (f32[3,10,16,128]{3,2,1,0:T(8,128)}, f32[3,16,80,128]{3,2,1,0:T(8,128)}, f32[16,128]{1,0:T(8,128)}, f32[16,128]{1,0:T(8,128)}) custom-call(f32[16,24,128]{2,1,0:T(8,128)S(1)} %all-to-all-done.refs_0_, f32[160,128]{1,0:T(8,128)S(1)} %get-tuple-element.27.refs_1_, ...), custom_call_target="tpu_custom_call", output_to_operand_aliasing={{1}: (10, {})} | custom-call | flops 3000000000 | bytes 9000000 | tf_op jit(solution)/shard_map/final/pallas_call | solution.py:827
Async XLA Ops:
  2.9 5.3 %collective-permute-start = (f32[128,128]{1,0:T(8,128)S(1)}, f32[128,128]{1,0:T(8,128)S(1)}, u32[]{:S(2)}, u32[]{:S(2)}) collective-permute-start(f32[128,128]{1,0:T(8,128)S(1)} %get-tuple-element.22), channel_id=1, source_target_pairs={{0,1},{1,0},{2,3},{3,2},{4,5},{5,4},{6,7},{7,6},{8,9},{9,8},{10,11... | collective-permute-start | bytes 196616 | tf_op jit(solution)/shard_map/ppermute | solution.py:778
  5.9 11.2 %collective-permute-start.1 = (f32[392,128]{1,0:T(8,128)S(1)}, f32[392,128]{1,0:T(8,128)S(1)}, u32[]{:S(2)}, u32[]{:S(2)}) collective-permute-start(f32[392,128]{1,0:T(8,128)S(1)} %get-tuple-element.24), channel_id=1, source_target_pairs={{0,2},{4,6},{8,10},{12,14},{16,18},{20,22},{24,26},{28,30},{2,0},{... | collective-permute-start | bytes 602120 | tf_op jit(solution)/shard_map/ppermute | solution.py:790
  5.9 11.2 %collective-permute-start.2 = (f32[392,128]{1,0:T(8,128)S(1)}, f32[392,128]{1,0:T(8,128)S(1)}, u32[]{:S(2)}, u32[]{:S(2)}) collective-permute-start(f32[392,128]{1,0:T(8,128)S(1)} %get-tuple-element.25), channel_id=1, source_target_pairs={{2,4},{6,8},{10,12},{14,16},{18,20},{22,24},{26,28},{4,2},{8,6},{1... | collective-permute-start | bytes 602120 | tf_op jit(solution)/shard_map/ppermute | solution.py:790
  9.2 13.5 %all-to-all-start = ((f32[16,24,128]{2,1,0:T(8,128)}), f32[16,24,128]{2,1,0:T(8,128)S(1)}, u32[]{:S(2)}, u32[]{:S(2)}) async-start(f32[16,24,128]{2,1,0:T(8,128)} %blocks.1), calls=%async_computation | async-start | bytes 393216 | tf_op jit(solution)/shard_map/all_to_all | solution.py:797
  17.2 3.8 %collective-permute-start.3 = (f32[24,128]{1,0:T(8,128)S(1)}, f32[24,128]{1,0:T(8,128)S(1)}, u32[]{:S(2)}, u32[]{:S(2)}) collective-permute-start(f32[24,128]{1,0:T(8,128)S(1)} %corners.1), channel_id=1, source_target_pairs={{0,1},{1,0},{2,3},{3,2},{4,5},{5,4},{6,7},{7,6},{8,9},{9,8},{10,11... | collective-permute-start | bytes 36872 | tf_op jit(solution)/shard_map/ppermute | solution.py:778

commit v7 on v6

--- a/solution.py
+++ b/solution.py
@@ -391,9 +391,34 @@
         out[n * TILE : (n + 1) * TILE, :] = tile
 
 
-def ocean_kernel(n_narrow, n_parts, n_tiles, layers, *refs):
+def own_hots(planes, rim_link, n_wide, cap, block, hots):
+    rows = planes.shape[1]
+    tall = rows + TILE
+    tall_row = iota((tall, 1), 0)
+    kind = jnp.where(
+        tall_row < rows,
+        0.0,
+        jnp.where(tall_row < rows + RIM, 2.0, jnp.where(tall_row >= tall - RIM, 1.0, -1.0)),
+    )
+    count = n_wide * block
+    own_link = jnp.concatenate([planes[ICE_LINK], rim_link], axis=0)[:, 0:1]
+    slots = (rows, cap, block, count, n_wide)
+    found = list(ice_slots(own_link, kind, *slots)[:3])
+    for n, hot in enumerate(found):
+        hots[n * tall : (n + 1) * tall, :] = hot
+    ocean_link = planes[OCEAN_LINK][:, 0:1]
+    ocean_row = spread(ocean_link)
+    tile = divide(ocean_link - 1.0, rows)
+    tile_row = divide(ocean_row - 1.0, rows)
+    hits = (tile == tile_row) & (ocean_row > 0.5) & (ocean_row < ocean_link)
+    rank = jnp.sum(hits.astype(F32), axis=1, keepdims=True)
+    target = jnp.where(ocean_link > 0.5, tile * block + 3 * cap + rank, -1.0)
+    hots[len(found) * tall :, :] = (iota((rows, count), 1).astype(F32) == target).astype(F32)
+
+
+def ocean_kernel(n_wide, n_narrow, cap, block, n_parts, n_tiles, layers, *refs):
     parts, refs = refs[:n_parts], refs[n_parts:]
-    field, pair, cross, planes, out, top, held, sems = refs
+    field, pair, cross, planes, out, top, hots, held, sems = refs
     _, rows, levels, _ = field.shape
     places = Places(levels, layers)
     chunks = sems.shape[0] // 3
@@ -448,6 +473,9 @@
             )
             copy.start()
             writes.append(copy)
+    under = iota((TILE, 1), 0) < HALO
+    rim_link = jnp.where(under, down(places.link, TILE), up(places.link, TILE))
+    own_hots(planes, rim_link, n_wide, cap, block, hots)
     for copy in writes:
         copy.wait()
 
@@ -569,9 +597,8 @@
         jnp.where(tall_row < rows + RIM, 2.0, jnp.where(tall_row >= tall - RIM, 1.0, -1.0)),
     )
     count = n_wide * block
-    own_link = below(planes[ICE_LINK], rim(places.link))[:, 0:1]
+    found = []
     slots = (rows, cap, block, count, n_wide)
-    found = list(ice_slots(own_link, kind, *slots)[:3])
     links = plane_halo(block_tall, ICE_LINK)
     if n_narrow == 2:
         sides = [jnp.max(links, axis=1, keepdims=True)]
@@ -579,18 +606,10 @@
         sides = [links[:, 0:1], links[:, LANES - 1 : LANES]]
     for link in sides:
         slot, _, _, near_slot, own_slot, bottom = ice_slots(link, kind, *slots)
-        ends[(len(found) - 3) // 3] = jnp.broadcast_to(bottom, (tall, LANES))
+        ends[len(found) // 3] = jnp.broadcast_to(bottom, (tall, LANES))
         found += [slot, near_slot, own_slot]
     for n, hot in enumerate(found):
         hots[n * tall : (n + 1) * tall, :] = hot
-    ocean_link = planes[OCEAN_LINK][:, 0:1]
-    ocean_row = spread(ocean_link)
-    tile = divide(ocean_link - 1.0, rows)
-    tile_row = divide(ocean_row - 1.0, rows)
-    hits = (tile == tile_row) & (ocean_row > 0.5) & (ocean_row < ocean_link)
-    rank = jnp.sum(hits.astype(F32), axis=1, keepdims=True)
-    target = jnp.where(ocean_link > 0.5, tile * block + 3 * cap + rank, -1.0)
-    hots[len(found) * tall :, :] = (iota((rows, count), 1).astype(F32) == target).astype(F32)
     strips = [
         below(a, b) for a, b in zip(merged_ice(parts, rows, n_tiles, n_narrow), corner_ice)
     ]
@@ -615,7 +634,7 @@
 
 def final_kernel(n_wide, n_narrow, cap, block, *refs):
     (
-        blocks, hots, ends, planes, ice, top, sums, inverse, rate, flat, ocean_in,
+        blocks, own, hots, ends, planes, ice, top, sums, inverse, rate, flat, ocean_in,
         ice_out, ocean_out, thick_out, melt_out,
         vel, result, thin, melted, new_top, sems,
     ) = refs
@@ -629,7 +648,9 @@
         )
         for n in range(3)
     ]
-    found = pick(hots[...], jnp.concatenate(parts, axis=1))
+    n_own = 3 * tall
+    hot = jnp.concatenate([own[0:n_own, :], hots[...], own[n_own:, :]], axis=0)
+    found = pick(hot, jnp.concatenate(parts, axis=1))
 
     def got(n, part):
         return found[n * tall : (n + 1) * tall, part * LANES : (part + 1) * LANES]
@@ -661,7 +682,7 @@
     melt_tall = GAMMA_MELT * (mixed_tall - wet_tall * (0.0832 - 0.761 * draft_tall))
     new_thick = (thick_tall - TIME_STEP * melt_tall * open_ice) * inside
     thin[...] = new_thick[:rows, :LANES]
-    n_hots = hots.shape[0] - rows
+    n_hots = n_own + hots.shape[0]
     ocean_draft = found[n_hots:, :LANES]
     heat_top = jnp.concatenate([top[i, 0:1, :] for i in range(rows)], axis=0)
     coupled = (planes[OCEAN_LINK] > 0.5).astype(F32)
@@ -803,10 +824,11 @@
             kept((1 + n_tiles) * TILE, LANES), [here] * 2, here,
         )(*near(pair, cross))
     )
-    ocean, top = call(
-        functools.partial(ocean_kernel, n_narrow, n_parts, n_tiles, layers), "ocean", 4.0,
-        (array(3, rows, levels, LANES), kept(rows, TILE, LANES)),
-        [here] * (n_parts + 4), (far, here),
+    tall = rows + TILE
+    ocean, top, own = call(
+        functools.partial(ocean_kernel, n_wide, n_narrow, cap, block, n_parts, n_tiles, layers), "ocean", 4.0,
+        (array(3, rows, levels, LANES), kept(rows, TILE, LANES), kept(3 * tall + rows, n_wide * block)),
+        [here] * (n_parts + 4), (far, here, here),
         [
             pltpu.VMEM((3, rows, levels, LANES), F32),
             dma((3 * chunks,)),
@@ -819,7 +841,7 @@
         functools.partial(first_kernel, n_wide, n_narrow, cap, block, n_parts, levels), "first", 4.0,
         (
             kept(2, layers, tall, wide), kept(layers, tall, wide), kept(layers, tall, wide), kept(3, tall, wide),
-            kept((3 + 3 * n_sides) * tall + rows, n_wide * block), kept(n_sides, tall, LANES),
+            kept(3 * n_sides * tall, n_wide * block), kept(n_sides, tall, LANES),
         ),
         [here] * (2 * n_parts + 4), (here,) * 6,
         [pltpu.VMEM((2, layers, tall, wide), F32)],
@@ -830,7 +852,7 @@
             array(3, layers, rows, LANES), array(3, rows, levels, LANES),
             array(rows, LANES), array(rows, LANES),
         ),
-        [here] * 10 + [far], (far,) * 4,
+        [here] * 11 + [far], (far,) * 4,
         [
             pltpu.VMEM((PICARD - 1, 2, layers, tall, wide), F32),
             pltpu.VMEM((3, layers, rows, LANES), F32),
@@ -839,8 +861,8 @@
             pltpu.VMEM((rows, TILE, LANES), F32),
             dma((3 + layers,)),
         ],
-        input_output_aliases={10: 1},
-    )(*near(blocks, hots, ends, planes, ice, top, sums, inverse, rate, flat), ocean)
+        input_output_aliases={11: 1},
+    )(*near(blocks, own, hots, ends, planes, ice, top, sums, inverse, rate, flat), ocean)
     return ice.transpose(0, 2, 1, 3), ocean, thick_out, melt_out
 
 

time: 24.7 us -> 24.6 us (level)
  no operation moved by 1% of the time
where the time goes in v7:
time: 24.6 us; the launch traced here: 24.4 us
  starting transfers between devices  12.1 us (49%)
  Pallas kernels  9.43 us (38%)
  waiting for transfers between devices  2.12 us (9%)
  between operations  0.7 us (3%)
    all_to_all x1, starting transfers between devices, local(): lax.all_to_all(blocks, 'wide', split_axis=0, concat_axis=0, tiled=True, a...  7.87 us
    ppermute x2, starting transfers between devices, narrow(): return [lax.ppermute(value, 'narrow', [(0, 1), (1, 0)])]  3.6 us
    pallas_call x1, Pallas kernels, local(): call(functools.partial(ocean_kernel, n_wide, n_narrow, cap, block, n_part...  2.64 us
    pallas_call x1, Pallas kernels, local(): call(edges_kernel, 'edges', 4.0, (kept((1 + n_tiles) * rows + levels, LAN...  2.23 us
    ppermute x2, waiting for transfers between devices, narrow(): return [lax.ppermute(value, 'narrow', [(0, 1), (1, 0)])]  2.11 us
    pallas_call x1, Pallas kernels, local(): call(functools.partial(final_kernel, n_wide, n_narrow, cap, block), 'fina...  1.77 us
    pallas_call x1, Pallas kernels, local(): call(functools.partial(first_kernel, n_wide, n_narrow, cap, block, n_part...  1.63 us
    pallas_call x1, Pallas kernels, local(): call(functools.partial(blocks_kernel, n_wide, n_narrow, cap, block, n_par...  1.06 us
  transfers between devices with their start and end apart: 5, of which 2 were waited for; matrix products, arithmetic and copies ran while one was open for 0% of the time, Pallas kernels for 22%

profile of v7, /device:TPU:0, one launch (start us, length us, event | category | flops | bytes accessed | tf_op | source)
XLA Modules:
  0.0 24.4 jit_solution(11119119808865784862)
XLA Ops:
  0.6 2.2 %edges.1 = (f32[128,128]{1,0:T(8,128)S(1)}, f32[392,128]{1,0:T(8,128)S(1)}, f32[392,128]{1,0:T(8,128)S(1)}, f32[6,16,128]{2,1,0:T(8,128)S(1)}, f32[3,10,16,128]{...) custom-call(f32[10,16,128]{2,1,0:T(8,128)} %bitcast.6, f32[10,16,128]{2,1,0:T(8,128)} %bitcast.7, f32[10,16,128]{2,1,0:T(8,128)} %bitcast.8, ...), custom_call_target="tpu_custom_call" | custom-call | flops 4000000000 | bytes 12000000 | tf_op jit(solution)/shard_map/edges/pallas_call | solution.py:780
  2.9 3.0 %collective-permute-start = (f32[128,128]{1,0:T(8,128)S(1)}, f32[128,128]{1,0:T(8,128)S(1)}, u32[]{:S(2)}, u32[]{:S(2)}) collective-permute-start(f32[128,128]{1,0:T(8,128)S(1)} %get-tuple-element.23), channel_id=1, source_target_pairs={{0,1},{1,0},{2,3},{3,2},{4,5},{5,4},{6,7},{7,6},{8,9},{9,8},{10,11... | collective-permute-start | bytes 196616 | tf_op jit(solution)/shard_map/ppermute | solution.py:799
  5.9 0.0 collective-permute-start.1
  5.9 0.7 %collective-permute-start.2 = (f32[392,128]{1,0:T(8,128)S(1)}, f32[392,128]{1,0:T(8,128)S(1)}, u32[]{:S(2)}, u32[]{:S(2)}) collective-permute-start(f32[392,128]{1,0:T(8,128)S(1)} %get-tuple-element.27), channel_id=1, source_target_pairs={{2,4},{6,8},{10,12},{14,16},{18,20},{22,24},{26,28},{4,2},{8,6},{1... | collective-permute-start | bytes 602120 | tf_op jit(solution)/shard_map/ppermute | solution.py:811
  6.6 1.6 %collective-permute-done.refs_0_ = f32[128,128]{1,0:T(8,128)S(1)} collective-permute-done((f32[128,128]{1,0:T(8,128)S(1)}, f32[128,128]{1,0:T(8,128)S(1)}, u32[]{:S(2)}, u32[]{:S(2)}) %collective-permute-start) | collective-permute-done | bytes 65568 | tf_op jit(solution)/shard_map/ppermute | solution.py:799
  8.1 1.1 %blocks.1 = f32[16,24,128]{2,1,0:T(8,128)} custom-call(f32[128,128]{1,0:T(8,128)S(1)} %collective-permute-done.refs_0_, f32[6,16,128]{2,1,0:T(8,128)S(1)} %get-tuple-element.24.refs_1_.refs_4_.refs_5_), custom_call_target="tpu_custom_call" | custom-call | flops 4000000000 | bytes 12000000 | tf_op jit(solution)/shard_map/blocks/pallas_call | solution.py:814
  9.2 7.9 %all-to-all-start = ((f32[16,24,128]{2,1,0:T(8,128)}), f32[16,24,128]{2,1,0:T(8,128)S(1)}, u32[]{:S(2)}, u32[]{:S(2)}) async-start(f32[16,24,128]{2,1,0:T(8,128)} %blocks.1), calls=%async_computation | async-start | bytes 393216 | tf_op jit(solution)/shard_map/all_to_all | solution.py:818
  17.1 0.0 collective-permute-done.1.refs_2_.pair.refs_3_
  17.1 0.0 collective-permute-done.2.refs_3_.cross.refs_4_
  17.1 0.1 corners.1
  17.2 0.6 %collective-permute-start.3 = (f32[24,128]{1,0:T(8,128)S(1)}, f32[24,128]{1,0:T(8,128)S(1)}, u32[]{:S(2)}, u32[]{:S(2)}) collective-permute-start(f32[24,128]{1,0:T(8,128)S(1)} %corners.1), channel_id=1, source_target_pairs={{0,1},{1,0},{2,3},{3,2},{4,5},{5,4},{6,7},{7,6},{8,9},{9,8},{10,11... | collective-permute-start | bytes 36872 | tf_op jit(solution)/shard_map/ppermute | solution.py:799
  17.8 2.6 %ocean.1 = (f32[3,16,80,128]{3,2,1,0:T(8,128)}, f32[16,8,128]{2,1,0:T(8,128)S(1)}, f32[88,128]{1,0:T(8,128)S(1)}) custom-call(f32[128,128]{1,0:T(8,128)S(1)} %collective-permute-done.refs_0_, f32[3,16,80,128]{3,2,1,0:T(8,128)S(1)} %get-tuple-element.25.refs_1_, f32[392,128]{1,0:T(8,128)S(1)} %collective-permute-done.1.refs_2_.pair.refs_3_, ...), custom_call_target="tpu_custom_call" | custom-call | flops 4000000000 | bytes 12000000 | tf_op jit(solution)/shard_map/ocean/pallas_call | solution.py:828
  20.4 0.5 %collective-permute-done.3.refs_1_ = f32[24,128]{1,0:T(8,128)S(1)} collective-permute-done((f32[24,128]{1,0:T(8,128)S(1)}, f32[24,128]{1,0:T(8,128)S(1)}, u32[]{:S(2)}, u32[]{:S(2)}) %collective-permute-start.3) | collective-permute-done | bytes 12320 | tf_op jit(solution)/shard_map/ppermute | solution.py:799
  21.0 1.6 %first.1 = (f32[2,10,24,256]{3,2,1,0:T(8,128)S(1)}, f32[10,24,256]{2,1,0:T(8,128)S(1)}, f32[10,24,256]{2,1,0:T(8,128)S(1)}, f32[3,24,256]{2,1,0:T(8,128)S(1)}, f...) custom-call(f32[128,128]{1,0:T(8,128)S(1)} %collective-permute-done.refs_0_, ...), custom_call_target="tpu_custom_call" | custom-call | flops 4000000000 | bytes 12000000 | tf_op jit(solution)/shard_map/first/pallas_call | solution.py:840
  22.6 0.0 all-to-all-done.refs_0_
  22.6 1.8 %final.1 = (f32[3,10,16,128]{3,2,1,0:T(8,128)}, f32[3,16,80,128]{3,2,1,0:T(8,128)}, f32[16,128]{1,0:T(8,128)}, f32[16,128]{1,0:T(8,128)}) custom-call(f32[16,24,128]{2,1,0:T(8,128)S(1)} %all-to-all-done.refs_0_, f32[88,128]{1,0:T(8,128)S(1)} %get-tuple-element.28.refs_1_, f32[72,128]{1,0:T(8,128)S(1)} %get-tuple-element.30.refs_2_, ...), custom_call_target="tpu_custom_call", output_to_operand_aliasing={{1}: (11, {})} | custom-call | flops 3000000000 | bytes 9000000 | tf_op jit(solution)/shard_map/final/pallas_call | solution.py:849
Async XLA Ops:
  2.9 5.3 %collective-permute-start = (f32[128,128]{1,0:T(8,128)S(1)}, f32[128,128]{1,0:T(8,128)S(1)}, u32[]{:S(2)}, u32[]{:S(2)}) collective-permute-start(f32[128,128]{1,0:T(8,128)S(1)} %get-tuple-element.23), channel_id=1, source_target_pairs={{0,1},{1,0},{2,3},{3,2},{4,5},{5,4},{6,7},{7,6},{8,9},{9,8},{10,11... | collective-permute-start | bytes 196616 | tf_op jit(solution)/shard_map/ppermute | solution.py:799
  5.9 11.2 %collective-permute-start.1 = (f32[392,128]{1,0:T(8,128)S(1)}, f32[392,128]{1,0:T(8,128)S(1)}, u32[]{:S(2)}, u32[]{:S(2)}) collective-permute-start(f32[392,128]{1,0:T(8,128)S(1)} %get-tuple-element.26), channel_id=1, source_target_pairs={{0,2},{4,6},{8,10},{12,14},{16,18},{20,22},{24,26},{28,30},{2,0},{... | collective-permute-start | bytes 602120 | tf_op jit(solution)/shard_map/ppermute | solution.py:811
  5.9 11.2 %collective-permute-start.2 = (f32[392,128]{1,0:T(8,128)S(1)}, f32[392,128]{1,0:T(8,128)S(1)}, u32[]{:S(2)}, u32[]{:S(2)}) collective-permute-start(f32[392,128]{1,0:T(8,128)S(1)} %get-tuple-element.27), channel_id=1, source_target_pairs={{2,4},{6,8},{10,12},{14,16},{18,20},{22,24},{26,28},{4,2},{8,6},{1... | collective-permute-start | bytes 602120 | tf_op jit(solution)/shard_map/ppermute | solution.py:811
  9.2 13.4 %all-to-all-start = ((f32[16,24,128]{2,1,0:T(8,128)}), f32[16,24,128]{2,1,0:T(8,128)S(1)}, u32[]{:S(2)}, u32[]{:S(2)}) async-start(f32[16,24,128]{2,1,0:T(8,128)} %blocks.1), calls=%async_computation | async-start | bytes 393216 | tf_op jit(solution)/shard_map/all_to_all | solution.py:818
  17.2 3.8 %collective-permute-start.3 = (f32[24,128]{1,0:T(8,128)S(1)}, f32[24,128]{1,0:T(8,128)S(1)}, u32[]{:S(2)}, u32[]{:S(2)}) collective-permute-start(f32[24,128]{1,0:T(8,128)S(1)} %corners.1), channel_id=1, source_target_pairs={{0,1},{1,0},{2,3},{3,2},{4,5},{5,4},{6,7},{7,6},{8,9},{9,8},{10,11... | collective-permute-start | bytes 36872 | tf_op jit(solution)/shard_map/ppermute | solution.py:799

commit v8 on v7

--- a/solution.py
+++ b/solution.py
@@ -710,6 +710,7 @@
     for f in range(2):
         for k in range(layers):
             vel[0, f, k] = (sums[f, k] + stress[f]) * inverse[k]
+    cuts = [0, layers - layers // 4, layers]
     for sweep in range(1, PICARD):
         last = sweep == PICARD - 1
         old = sweep - 1
@@ -725,11 +726,13 @@
                     vel[sweep, f, k] = value * inside
             if last:
                 result[2, k] = ice[2, k] + HEATING_RATE * heat[:rows, :LANES]
-                copy = pltpu.make_async_copy(
-                    result.at[:, k], ice_out.at[:, k], sems.at[len(writes)]
-                )
-                copy.start()
-                writes.append(copy)
+                if k + 1 in cuts:
+                    part = pl.ds(cuts[cuts.index(k + 1) - 1], k + 1 - cuts[cuts.index(k + 1) - 1])
+                    copy = pltpu.make_async_copy(
+                        result.at[:, part], ice_out.at[:, part], sems.at[len(writes)]
+                    )
+                    copy.start()
+                    writes.append(copy)
     for copy in writes:
         copy.wait()
 

time: 24.6 us -> 24.7 us (level)
  no operation moved by 1% of the time
where the time goes in v8:
time: 24.7 us; the launch traced here: 24.4 us
  starting transfers between devices  12.1 us (49%)
  Pallas kernels  9.46 us (38%)
  waiting for transfers between devices  2.12 us (9%)
  between operations  0.7 us (3%)
    all_to_all x1, starting transfers between devices, local(): lax.all_to_all(blocks, 'wide', split_axis=0, concat_axis=0, tiled=True, a...  7.87 us
    ppermute x2, starting transfers between devices, narrow(): return [lax.ppermute(value, 'narrow', [(0, 1), (1, 0)])]  3.6 us
    pallas_call x1, Pallas kernels, local(): call(functools.partial(ocean_kernel, n_wide, n_narrow, cap, block, n_part...  2.64 us
    pallas_call x1, Pallas kernels, local(): call(edges_kernel, 'edges', 4.0, (kept((1 + n_tiles) * rows + levels, LAN...  2.23 us
    ppermute x2, waiting for transfers between devices, narrow(): return [lax.ppermute(value, 'narrow', [(0, 1), (1, 0)])]  2.11 us
    pallas_call x1, Pallas kernels, local(): call(functools.partial(final_kernel, n_wide, n_narrow, cap, block), 'fina...  1.8 us
    pallas_call x1, Pallas kernels, local(): call(functools.partial(first_kernel, n_wide, n_narrow, cap, block, n_part...  1.63 us
    pallas_call x1, Pallas kernels, local(): call(functools.partial(blocks_kernel, n_wide, n_narrow, cap, block, n_par...  1.06 us
  transfers between devices with their start and end apart: 5, of which 2 were waited for; matrix products, arithmetic and copies ran while one was open for 0% of the time, Pallas kernels for 22%

profile of v8, /device:TPU:0, one launch (start us, length us, event | category | flops | bytes accessed | tf_op | source)
XLA Modules:
  0.0 24.4 jit_solution(5447178523265763434)
XLA Ops:
  0.6 2.2 %edges.1 = (f32[128,128]{1,0:T(8,128)S(1)}, f32[392,128]{1,0:T(8,128)S(1)}, f32[392,128]{1,0:T(8,128)S(1)}, f32[6,16,128]{2,1,0:T(8,128)S(1)}, f32[3,10,16,128]{...) custom-call(f32[10,16,128]{2,1,0:T(8,128)} %bitcast.6, f32[10,16,128]{2,1,0:T(8,128)} %bitcast.7, f32[10,16,128]{2,1,0:T(8,128)} %bitcast.8, ...), custom_call_target="tpu_custom_call" | custom-call | flops 4000000000 | bytes 12000000 | tf_op jit(solution)/shard_map/edges/pallas_call | solution.py:783
  2.9 3.0 %collective-permute-start = (f32[128,128]{1,0:T(8,128)S(1)}, f32[128,128]{1,0:T(8,128)S(1)}, u32[]{:S(2)}, u32[]{:S(2)}) collective-permute-start(f32[128,128]{1,0:T(8,128)S(1)} %get-tuple-element.23), channel_id=1, source_target_pairs={{0,1},{1,0},{2,3},{3,2},{4,5},{5,4},{6,7},{7,6},{8,9},{9,8},{10,11... | collective-permute-start | bytes 196616 | tf_op jit(solution)/shard_map/ppermute | solution.py:802
  5.9 0.0 collective-permute-start.1
  5.9 0.7 %collective-permute-start.2 = (f32[392,128]{1,0:T(8,128)S(1)}, f32[392,128]{1,0:T(8,128)S(1)}, u32[]{:S(2)}, u32[]{:S(2)}) collective-permute-start(f32[392,128]{1,0:T(8,128)S(1)} %get-tuple-element.27), channel_id=1, source_target_pairs={{2,4},{6,8},{10,12},{14,16},{18,20},{22,24},{26,28},{4,2},{8,6},{1... | collective-permute-start | bytes 602120 | tf_op jit(solution)/shard_map/ppermute | solution.py:814
  6.6 1.6 %collective-permute-done.refs_0_ = f32[128,128]{1,0:T(8,128)S(1)} collective-permute-done((f32[128,128]{1,0:T(8,128)S(1)}, f32[128,128]{1,0:T(8,128)S(1)}, u32[]{:S(2)}, u32[]{:S(2)}) %collective-permute-start) | collective-permute-done | bytes 65568 | tf_op jit(solution)/shard_map/ppermute | solution.py:802
  8.1 1.1 %blocks.1 = f32[16,24,128]{2,1,0:T(8,128)} custom-call(f32[128,128]{1,0:T(8,128)S(1)} %collective-permute-done.refs_0_, f32[6,16,128]{2,1,0:T(8,128)S(1)} %get-tuple-element.24.refs_1_.refs_4_.refs_5_), custom_call_target="tpu_custom_call" | custom-call | flops 4000000000 | bytes 12000000 | tf_op jit(solution)/shard_map/blocks/pallas_call | solution.py:817
  9.2 7.9 %all-to-all-start = ((f32[16,24,128]{2,1,0:T(8,128)}), f32[16,24,128]{2,1,0:T(8,128)S(1)}, u32[]{:S(2)}, u32[]{:S(2)}) async-start(f32[16,24,128]{2,1,0:T(8,128)} %blocks.1), calls=%async_computation | async-start | bytes 393216 | tf_op jit(solution)/shard_map/all_to_all | solution.py:821
  17.1 0.0 collective-permute-done.1.refs_2_.pair.refs_3_
  17.1 0.0 collective-permute-done.2.refs_3_.cross.refs_4_
  17.1 0.1 corners.1
  17.2 0.6 %collective-permute-start.3 = (f32[24,128]{1,0:T(8,128)S(1)}, f32[24,128]{1,0:T(8,128)S(1)}, u32[]{:S(2)}, u32[]{:S(2)}) collective-permute-start(f32[24,128]{1,0:T(8,128)S(1)} %corners.1), channel_id=1, source_target_pairs={{0,1},{1,0},{2,3},{3,2},{4,5},{5,4},{6,7},{7,6},{8,9},{9,8},{10,11... | collective-permute-start | bytes 36872 | tf_op jit(solution)/shard_map/ppermute | solution.py:802
  17.8 2.6 %ocean.1 = (f32[3,16,80,128]{3,2,1,0:T(8,128)}, f32[16,8,128]{2,1,0:T(8,128)S(1)}, f32[88,128]{1,0:T(8,128)S(1)}) custom-call(f32[128,128]{1,0:T(8,128)S(1)} %collective-permute-done.refs_0_, f32[3,16,80,128]{3,2,1,0:T(8,128)S(1)} %get-tuple-element.25.refs_1_, f32[392,128]{1,0:T(8,128)S(1)} %collective-permute-done.1.refs_2_.pair.refs_3_, ...), custom_call_target="tpu_custom_call" | custom-call | flops 4000000000 | bytes 12000000 | tf_op jit(solution)/shard_map/ocean/pallas_call | solution.py:831
  20.4 0.5 %collective-permute-done.3.refs_1_ = f32[24,128]{1,0:T(8,128)S(1)} collective-permute-done((f32[24,128]{1,0:T(8,128)S(1)}, f32[24,128]{1,0:T(8,128)S(1)}, u32[]{:S(2)}, u32[]{:S(2)}) %collective-permute-start.3) | collective-permute-done | bytes 12320 | tf_op jit(solution)/shard_map/ppermute | solution.py:802
  21.0 1.6 %first.1 = (f32[2,10,24,256]{3,2,1,0:T(8,128)S(1)}, f32[10,24,256]{2,1,0:T(8,128)S(1)}, f32[10,24,256]{2,1,0:T(8,128)S(1)}, f32[3,24,256]{2,1,0:T(8,128)S(1)}, f...) custom-call(f32[128,128]{1,0:T(8,128)S(1)} %collective-permute-done.refs_0_, ...), custom_call_target="tpu_custom_call" | custom-call | flops 4000000000 | bytes 12000000 | tf_op jit(solution)/shard_map/first/pallas_call | solution.py:843
  22.6 0.0 all-to-all-done.refs_0_
  22.6 1.8 %final.1 = (f32[3,10,16,128]{3,2,1,0:T(8,128)}, f32[3,16,80,128]{3,2,1,0:T(8,128)}, f32[16,128]{1,0:T(8,128)}, f32[16,128]{1,0:T(8,128)}) custom-call(f32[16,24,128]{2,1,0:T(8,128)S(1)} %all-to-all-done.refs_0_, f32[88,128]{1,0:T(8,128)S(1)} %get-tuple-element.28.refs_1_, f32[72,128]{1,0:T(8,128)S(1)} %get-tuple-element.30.refs_2_, ...), custom_call_target="tpu_custom_call", output_to_operand_aliasing={{1}: (11, {})} | custom-call | flops 3000000000 | bytes 9000000 | tf_op jit(solution)/shard_map/final/pallas_call | solution.py:852
Async XLA Ops:
  2.9 5.3 %collective-permute-start = (f32[128,128]{1,0:T(8,128)S(1)}, f32[128,128]{1,0:T(8,128)S(1)}, u32[]{:S(2)}, u32[]{:S(2)}) collective-permute-start(f32[128,128]{1,0:T(8,128)S(1)} %get-tuple-element.23), channel_id=1, source_target_pairs={{0,1},{1,0},{2,3},{3,2},{4,5},{5,4},{6,7},{7,6},{8,9},{9,8},{10,11... | collective-permute-start | bytes 196616 | tf_op jit(solution)/shard_map/ppermute | solution.py:802
  5.9 11.2 %collective-permute-start.1 = (f32[392,128]{1,0:T(8,128)S(1)}, f32[392,128]{1,0:T(8,128)S(1)}, u32[]{:S(2)}, u32[]{:S(2)}) collective-permute-start(f32[392,128]{1,0:T(8,128)S(1)} %get-tuple-element.26), channel_id=1, source_target_pairs={{0,2},{4,6},{8,10},{12,14},{16,18},{20,22},{24,26},{28,30},{2,0},{... | collective-permute-start | bytes 602120 | tf_op jit(solution)/shard_map/ppermute | solution.py:814
  5.9 11.2 %collective-permute-start.2 = (f32[392,128]{1,0:T(8,128)S(1)}, f32[392,128]{1,0:T(8,128)S(1)}, u32[]{:S(2)}, u32[]{:S(2)}) collective-permute-start(f32[392,128]{1,0:T(8,128)S(1)} %get-tuple-element.27), channel_id=1, source_target_pairs={{2,4},{6,8},{10,12},{14,16},{18,20},{22,24},{26,28},{4,2},{8,6},{1... | collective-permute-start | bytes 602120 | tf_op jit(solution)/shard_map/ppermute | solution.py:814
  9.2 13.4 %all-to-all-start = ((f32[16,24,128]{2,1,0:T(8,128)}), f32[16,24,128]{2,1,0:T(8,128)S(1)}, u32[]{:S(2)}, u32[]{:S(2)}) async-start(f32[16,24,128]{2,1,0:T(8,128)} %blocks.1), calls=%async_computation | async-start | bytes 393216 | tf_op jit(solution)/shard_map/all_to_all | solution.py:821
  17.2 3.8 %collective-permute-start.3 = (f32[24,128]{1,0:T(8,128)S(1)}, f32[24,128]{1,0:T(8,128)S(1)}, u32[]{:S(2)}, u32[]{:S(2)}) collective-permute-start(f32[24,128]{1,0:T(8,128)S(1)} %corners.1), channel_id=1, source_target_pairs={{0,1},{1,0},{2,3},{3,2},{4,5},{5,4},{6,7},{7,6},{8,9},{9,8},{10,11... | collective-permute-start | bytes 36872 | tf_op jit(solution)/shard_map/ppermute | solution.py:802
